TPU v7x, 32 devices: a whole 2x2x4 slice. The times are simulated.
32 devices in a mesh: seq: 8 (over y, x, core), chan: 4 (over z).
Axes of the slice: x: 2, y: 2, z: 4, core: 2. Of those that a mesh axis runs over, the one named last changes fastest.
Arguments:
- tokens: bfloat16 [8192, 1024], P(('seq', 'chan')), may hold values from -6 to 6
- doc_ids: int32 [8192], P('seq'), may hold values from 0 to 2, as said below
- cotangent: bfloat16 [8192, 1024], P(('seq', 'chan')), may hold values from -6 to 6
- norm_gain: float32 [1024], replicated, may hold values from 0.1 to 1.9
- gate_proj: bfloat16 [1024, 1536], P(None, 'chan'), may hold values from -0.1875 to 0.1875
- input_proj: bfloat16 [1024, 1536], P(None, 'chan'), may hold values from -0.1875 to 0.1875
- conv_weight: float32 [4, 1536], P(None, 'chan'), may hold values from -3 to 3
- conv_bias: float32 [1536], P('chan'), may hold values from -3 to 3
- recall_weight: float32 [16, 96, 96], P('chan'), may hold values from -0.625 to 0.625
- recall_bias: float32 [16, 96], P('chan'), may hold values from -4 to 4
- admit_weight: float32 [16, 96, 96], P('chan'), may hold values from -0.625 to 0.625
- admit_bias: float32 [16, 96], P('chan'), may hold values from -4 to 4
- decay_param: float32 [1536], P('chan'), may hold values from 2 to 9
- out_proj: bfloat16 [1536, 1024], P('chan'), may hold values from -0.625 to 0.625
- mlp_gain: float32 [1024], replicated, may hold values from 0.1 to 1.9
- mlp_gate: bfloat16 [1024, 3072], P(('seq', 'chan')), may hold values from -0.1875 to 0.1875
- mlp_up: bfloat16 [1024, 3072], P(('seq', 'chan')), may hold values from -0.1875 to 0.1875
- mlp_down: bfloat16 [1024, 3072], P(('seq', 'chan')), may hold values from -0.21875 to 0.21875
Outputs:
- block_out: bfloat16 [8192, 1024], P(('seq', 'chan'))
- grad_tokens: float32 [8192, 1024], P(('seq', 'chan'))
- grad_norm_gain: float32 [1024], replicated
- grad_gate_proj: float32 [1024, 1536], P(None, 'chan')
- grad_input_proj: float32 [1024, 1536], P(None, 'chan')
- grad_conv_weight: float32 [4, 1536], P(None, 'chan')
- grad_conv_bias: float32 [1536], P('chan')
- grad_recall_weight: float32 [16, 96, 96], P('chan')
- grad_recall_bias: float32 [16, 96], P('chan')
- grad_admit_weight: float32 [16, 96, 96], P('chan')
- grad_admit_bias: float32 [16, 96], P('chan')
- grad_decay_param: float32 [1536], P('chan')
- grad_out_proj: float32 [1536, 1024], P('chan')
- grad_mlp_gain: float32 [1024], replicated
- grad_mlp_gate: float32 [1024, 3072], P(('seq', 'chan'))
- grad_mlp_up: float32 [1024, 3072], P(('seq', 'chan'))
- grad_mlp_down: float32 [1024, 3072], P(('seq', 'chan'))
- gate_mean: float32 [1536], P('chan')
Inputs may be any that keep to these rules, and one draw needn't show every extreme that they name: `doc_ids`: each token's document number within its sequence: 0 at a sequence's first token, never falling inside a sequence.
All inputs are finite; a program needn't handle non-finite values.
Results may differ from a plain program's by a relative error of at most 0.012.
Values may be sent and summed in bfloat16 or wider, within the bound.
No kernel may reach another device: no remote copies, remote signals or barrier semaphores. Data moves between devices by JAX's collectives and lax.ppermute only.
A program may use at most 320 MiB of HBM per device.

v0:
```python
import jax
import jax.numpy as jnp
from jax import lax
from jax.sharding import PartitionSpec as P

LENGTH = 1024


EPS = 1e-06
STRENGTH = 8.0
HIGHEST = lax.Precision.HIGHEST


def normalize(values, gain):
    scale = lax.rsqrt(jnp.mean(values * values, axis=-1, keepdims=True) + EPS)
    return values * scale * gain


def combine(early, late):
    return (early[0] * late[0], late[0] * early[1] + late[1])


def mixer(
    gated_in,
    inputs,
    doc_ids,
    conv_weight,
    conv_bias,
    recall_weight,
    recall_bias,
    admit_weight,
    admit_bias,
    decay_param,
):
    count, width = inputs.shape
    heads, block = recall_bias.shape
    places = jnp.arange(count) % LENGTH
    prior = jnp.concatenate([doc_ids[:1], doc_ids[:-1]])
    keeper = ((places > 0) & (doc_ids == prior)).astype(jnp.float32)
    conv = conv_bias + conv_weight[0] * inputs
    for shift in range(1, conv_weight.shape[0]):
        moved = jnp.concatenate([jnp.zeros((shift, width), jnp.float32), inputs[: count - shift]])
        moved_doc = jnp.concatenate([jnp.full((shift,), -1, jnp.int32), doc_ids[: count - shift]])
        valid = ((places >= shift) & (doc_ids == moved_doc)).astype(jnp.float32)
        conv = conv + conv_weight[shift] * moved * valid[:, None]
    grouped = conv.reshape(count, heads, block)
    recall = jax.nn.sigmoid(
        jnp.einsum("rhc,hcd->rhd", grouped, recall_weight, precision=HIGHEST).reshape(count, width)
        + recall_bias.reshape(width)
    )
    admit = jax.nn.sigmoid(
        jnp.einsum("rhc,hcd->rhd", grouped, admit_weight, precision=HIGHEST).reshape(count, width)
        + admit_bias.reshape(width)
    )
    log_decay = -STRENGTH * recall * jax.nn.softplus(-decay_param)
    decay = jnp.exp(log_decay)
    inject = jnp.sqrt(-jnp.expm1(2.0 * log_decay)) * admit * conv
    carried, state = lax.associative_scan(combine, (decay * keeper[:, None], inject), axis=0)
    return (jax.nn.gelu(gated_in) * state, jnp.sum(decay, axis=0))


def activation(gate, upward):
    return jax.nn.gelu(gate) * upward


def contract(left, right, left_dim, right_dim):
    return lax.dot_general(
        left, right, (((left_dim,), (right_dim,)), ((), ())), preferred_element_type=jnp.float32
    )


def on_device(
    tokens,
    doc_ids,
    cotangent,
    norm_gain,
    gate_proj,
    input_proj,
    conv_weight,
    conv_bias,
    recall_weight,
    recall_bias,
    admit_weight,
    admit_bias,
    decay_param,
    out_proj,
    mlp_gain,
    mlp_gate,
    mlp_up,
    mlp_down,
):
    local_rows = tokens.shape[0]
    width = gate_proj.shape[1]
    model = tokens.shape[1]
    hidden_width = mlp_gate.shape[1]
    seq_count = lax.axis_size("seq")
    chan_count = lax.axis_size("chan")
    row_piece = model // (seq_count * chan_count)
    mix_params = (
        conv_weight,
        conv_bias,
        recall_weight,
        recall_bias,
        admit_weight,
        admit_bias,
        decay_param,
    )

    def local_mix(gated_in, inputs, *weights):
        return mixer(gated_in, inputs, doc_ids, *weights)

    def regroup(values):
        return (
            values.reshape(values.shape[0], seq_count, chan_count, row_piece)
            .transpose(0, 2, 1, 3)
            .reshape(values.shape[0], model)
        )

    resid = tokens.astype(jnp.float32)
    normed, norm_pull = jax.vjp(normalize, resid, norm_gain)
    normed_low = normed.astype(jnp.bfloat16)
    gathered = lax.all_gather(normed_low, "chan", axis=0, tiled=True)
    gated_in = jnp.dot(gathered, gate_proj, preferred_element_type=jnp.float32).astype(jnp.bfloat16)
    inputs = jnp.dot(gathered, input_proj, preferred_element_type=jnp.float32).astype(jnp.bfloat16)
    mixed, mix_pull, decay_sum = jax.vjp(
        local_mix,
        gated_in.astype(jnp.float32),
        inputs.astype(jnp.float32),
        *mix_params,
        has_aux=True
    )
    branch_in = mixed.astype(jnp.bfloat16)
    branch = lax.psum_scatter(
        jnp.dot(
            lax.slice_in_dim(branch_in, 0, local_rows * lax.axis_size("chan"), axis=0),
            out_proj,
            preferred_element_type=jnp.float32,
        ),
        "chan",
        scatter_dimension=0,
        tiled=True,
    )
    middle = resid + branch
    second, second_pull = jax.vjp(normalize, middle, mlp_gain)
    second_low = second.astype(jnp.bfloat16)
    gate_all, up_all, down_all = (
        lax.all_gather(mlp_gate, ("seq", "chan"), axis=0, tiled=True),
        lax.all_gather(mlp_up, ("seq", "chan"), axis=0, tiled=True),
        lax.all_gather(mlp_down, ("seq", "chan"), axis=0, tiled=True),
    )
    gate = jnp.dot(second_low, gate_all, preferred_element_type=jnp.float32)
    upward = jnp.dot(second_low, up_all, preferred_element_type=jnp.float32)
    activated, act_pull = jax.vjp(activation, gate, upward)
    hidden = activated.astype(jnp.bfloat16)
    result = contract(hidden, down_all, 1, 1)
    block_out = (middle + result).astype(jnp.bfloat16)
    hidden_grad = jnp.dot(cotangent, down_all, preferred_element_type=jnp.float32)
    gate_grad, up_grad = act_pull(hidden_grad)
    gate_low = gate_grad.astype(jnp.bfloat16)
    up_low = up_grad.astype(jnp.bfloat16)
    second_grad = contract(gate_low, gate_all, 1, 1) + contract(up_low, up_all, 1, 1)
    middle_grad, gain_two = second_pull(second_grad)
    middle_grad = middle_grad + cotangent.astype(jnp.float32)
    second_regrouped = regroup(second_low)
    cot_regrouped = regroup(cotangent)
    group_grads = lax.psum_scatter(
        jnp.concatenate(
            [
                contract(second_regrouped, gate_low, 0, 0),
                contract(second_regrouped, up_low, 0, 0),
                contract(cot_regrouped, hidden, 0, 0),
            ],
            axis=1,
        ),
        "chan",
        scatter_dimension=0,
        tiled=True,
    )
    mlp_grads = lax.psum_scatter(group_grads, "seq", scatter_dimension=0, tiled=True)
    branch_grad = middle_grad.astype(jnp.bfloat16)
    group_rows = gathered.shape[0]
    piece = lax.all_gather(branch_grad, "chan", axis=0, tiled=True)
    start = jnp.int32(0)
    into_mix = jnp.zeros((group_rows, width), jnp.float32)
    out_grad = jnp.zeros((width, model), jnp.float32)
    into_mix = lax.dynamic_update_slice_in_dim(into_mix, contract(piece, out_proj, 1, 1), start, 0)
    used = lax.dynamic_slice_in_dim(branch_in, start, piece.shape[0], 0)
    into_mix, grad_out = (into_mix, out_grad + contract(used, piece, 0, 0))
    rounded = lax.optimization_barrier(into_mix.astype(jnp.bfloat16)).astype(jnp.float32)
    mix_grads = mix_pull(rounded)
    gate_back = mix_grads[0].astype(jnp.bfloat16)
    input_back = mix_grads[1].astype(jnp.bfloat16)
    gate_part = lax.slice_in_dim(gate_back, 0, local_rows * lax.axis_size("chan"), axis=0)
    input_part = lax.slice_in_dim(input_back, 0, local_rows * lax.axis_size("chan"), axis=0)
    normed_grad = lax.psum_scatter(
        contract(gate_part, gate_proj, 1, 1) + contract(input_part, input_proj, 1, 1),
        "chan",
        scatter_dimension=0,
        tiled=True,
    )
    grad_gate = contract(gathered, gate_back, 0, 0)
    grad_input = contract(gathered, input_back, 0, 0)
    token_part, gain_one = norm_pull(normed_grad)
    grad_tokens = middle_grad + token_part
    gain_one, gain_two = lax.psum((gain_one, gain_two), ("seq", "chan"))
    summed = lax.psum(
        (
            grad_gate,
            grad_input,
            grad_out,
            mix_grads[2],
            mix_grads[3],
            mix_grads[4],
            mix_grads[5],
            mix_grads[6],
            mix_grads[7],
            mix_grads[8],
            decay_sum,
        ),
        "seq",
    )
    total_rows = local_rows * chan_count * seq_count
    return (
        block_out,
        grad_tokens,
        gain_one,
        summed[0],
        summed[1],
        summed[3],
        summed[4],
        summed[5],
        summed[6],
        summed[7],
        summed[8],
        summed[9],
        summed[2],
        gain_two,
        mlp_grads[:, :hidden_width],
        mlp_grads[:, hidden_width : 2 * hidden_width],
        mlp_grads[:, 2 * hidden_width :],
        summed[10] / total_rows,
    )


def solution(mesh):
    in_specs = (
        P(("seq", "chan"), None),
        P("seq"),
        P(("seq", "chan"), None),
        P(),
        P(None, "chan"),
        P(None, "chan"),
        P(None, "chan"),
        P("chan"),
        P("chan", None, None),
        P("chan", None),
        P("chan", None, None),
        P("chan", None),
        P("chan"),
        P("chan", None),
        P(),
        P(("seq", "chan"), None),
        P(("seq", "chan"), None),
        P(("seq", "chan"), None),
    )
    out_specs = (
        P(("seq", "chan"), None),
        P(("seq", "chan"), None),
        P(),
        P(None, "chan"),
        P(None, "chan"),
        P(None, "chan"),
        P("chan"),
        P("chan", None, None),
        P("chan", None),
        P("chan", None, None),
        P("chan", None),
        P("chan"),
        P("chan", None),
        P(),
        P(("seq", "chan"), None),
        P(("seq", "chan"), None),
        P(("seq", "chan"), None),
        P("chan"),
    )
    return jax.shard_map(
        on_device, mesh=mesh, in_specs=in_specs, out_specs=out_specs, check_vma=False
    )
```

profile of v0, /device:TPU:17, one launch (start us, length us, event | category | flops | bytes accessed | tf_op | source)
XLA Modules:
  0.0 1413.2 jit_solution(16074112187881835892)
XLA Ops:
  13.3 44.1 %all-gather.6.cloned.1.call-done = bf16[1024,1024]{1,0:T(8,128)(2,1)} async-done(((bf16[256,1024]{1,0:T(8,128)(2,1)}), bf16[1024,1024]{1,0:T(8,128)(2,1)}) %all-gather.6.cloned.1.call-update) | async-done | bytes 2097168 | tf_op jit(solution)/shard_map/all_gather | solution.py:122
  80.9 5.8 exponential_multiply_fusion
  174.9 77.8 %reduce-scatter.5.cloned.1.call-done = f32[256,1024]{1,0:T(8,128)} async-done(((f32[1024,1024]{1,0:T(8,128)}), f32[256,1024]{1,0:T(8,128)}) %reduce-scatter.5.cloned.1.call-update) | async-done | bytes 1048592 | tf_op jit(solution)/shard_map/reduce_scatter | solution.py:133
  259.3 42.6 %all-gather.10.cloned.1.call-done = bf16[1024,3072]{1,0:T(8,128)(2,1)} async-done(((bf16[32,3072]{1,0:T(8,128)(2,1)}), bf16[1024,3072]{1,0:T(8,128)(2,1)}) %all-gather.10.cloned.1.call-update) | async-done | bytes 6291472 | tf_op jit(solution)/shard_map/all_gather | solution.py:148
  301.8 6.5 fusion.123
  308.3 64.6 %all-gather.8.cloned.1.call-done = bf16[1024,3072]{1,0:T(8,128)(2,1)} async-done(((bf16[32,3072]{1,0:T(8,128)(2,1)}), bf16[1024,3072]{1,0:T(8,128)(2,1)}) %all-gather.8.cloned.1.call-update) | async-done | bytes 6291472 | tf_op jit(solution)/shard_map/all_gather | solution.py:147
  372.8 6.4 fusion.122
  379.3 64.6 %all-gather.12.cloned.1.call-done = bf16[1024,3072]{1,0:T(8,128)(2,1)} async-done(((bf16[32,3072]{1,0:T(8,128)(2,1)}), bf16[1024,3072]{1,0:T(8,128)(2,1)}) %all-gather.12.cloned.1.call-update) | async-done | bytes 6291472 | tf_op jit(solution)/shard_map/all_gather | solution.py:149
  443.9 9.9 multiply_convert_fusion
  455.7 5.5 multiply_reduce_fusion.5
  463.3 11.9 reduce-scatter.9.cloned.1.call-start
  475.3 8.1 fusion.132
  483.4 6.3 fusion.131
  489.7 6.3 convolution_bitcast_fusion
  496.0 25.8 %pad_maximum_fusion = f32[1024,9216]{1,0:T(8,128)} fusion(f32[1024,3072]{1,0:T(8,128)} %convolution_bitcast_fusion, f32[1024,3072]{1,0:T(8,128)} %fusion.132, f32[1024,3072]{1,0:T(8,128)} %fusion.131), kind=kLoop, calls=%fused_computation | loop fusion | flops 18874368 | bytes 75497472 | tf_op jit(solution)/shard_map/concatenate | solution.py:167
  659.9 5.2 pad.483
  665.2 7.2 multiply_reduce_fusion
  705.1 436.2 %reduce-scatter.9.cloned.1.call-done = f32[256,9216]{1,0:T(8,128)} async-done(((f32[1024,9216]{1,0:T(8,128)}), f32[256,9216]{1,0:T(8,128)}) %reduce-scatter.9.cloned.1.call-update) | async-done | bytes 9437200 | tf_op jit(solution)/shard_map/reduce_scatter | solution.py:166
  1157.5 5.5 fusion.27
  1163.3 21.7 %all-reduce.108 = (f32[4,384]{1,0:T(4,128)}, f32[384]{0:T(512)}, f32[4,96]{1,0:T(4,128)}, f32[4,96]{1,0:T(4,128)}, f32[384]{0:T(512)}, /*index=5*/f32[384]{0:T(512)S(1)}) all-reduce(f32[4,384]{1,0:T(4,128)S(1)} %pad_add_fusion.8, f32[384]{0:T(512)S(1)} %get-tuple-element.20, ...), channel_id=1, replica_groups=mesh['seq'=8,'chan'=4] {'seq'}, use_global_device_ids=true, to_apply=%region_14.15 | all-reduce | flops 3456 | bytes 27648 | tf_op jit(solution)/shard_map/psum | solution.py:206
  1185.5 35.2 %reduce-scatter.7.cloned.1.call-done = f32[256,1024]{1,0:T(8,128)} async-done(((f32[1024,1024]{1,0:T(8,128)}), f32[256,1024]{1,0:T(8,128)}) %reduce-scatter.7.cloned.1.call-update) | async-done | bytes 1048592 | tf_op jit(solution)/shard_map/reduce_scatter | solution.py:195
  1222.3 39.9 %all-reduce.107 = (f32[1024]{0:T(1024)}, f32[1024]{0:T(1024)}) all-reduce(f32[1024]{0:T(1024)S(1)} %get-tuple-element.22, f32[1024]{0:T(1024)S(1)} %copy-done.190), channel_id=1, replica_groups=mesh['seq'=8,'chan'=4] {'seq','chan'}, use_global_device_ids=true, to_apply=%region_7.8 | all-reduce | flops 2048 | bytes 16384 | tf_op jit(solution)/shard_map/psum | solution.py:205
  1265.0 36.6 %reduce-scatter.11.cloned.1.call-done = f32[32,9216]{1,0:T(8,128)} async-done(((f32[256,9216]{1,0:T(8,128)}), f32[32,9216]{1,0:T(8,128)}) %reduce-scatter.11.cloned.1.call-update) | async-done | bytes 1179664 | tf_op jit(solution)/shard_map/reduce_scatter | solution.py:179
  1303.8 95.2 %all-reduce.112.cloned.1.call-done = (f32[1024,384]{1,0:T(8,128)}, f32[1024,384]{1,0:T(8,128)}, f32[4,96,96]{2,1,0:T(8,128)}, f32[4,96,96]{2,1,0:T(8,128)}, f32[384,1024]{1,0:T(8,128)}) async-done(((f32[1024,384]{1,0:T(8,128)}, f32[1024,384]{1,0:T(8,128)}, f32[4,96,96]{2,1,0:T(8,128)}, f32[4,96,96]{2,1,0:T(8,128)}, f32[384,1024]{1,0:T(8,128)}), (f32[1024,384]{1,0:T(8,128)}, f32[1024,384]{1,0:T(8,128)}, ...) | async-done | bytes 5013520 | tf_op jit(solution)/shard_map/psum | solution.py:206
  (732 shorter events, 325.8 us)
Async XLA Ops:
  8.0 160.7 %copy-start = (bf16[384,1024]{1,0:T(8,128)(2,1)S(1)}, bf16[384,1024]{1,0:T(8,128)(2,1)}, u32[]{:S(2)}) copy-start(bf16[384,1024]{1,0:T(8,128)(2,1)} %param.31) | copy-start | bytes 2359300
  8.1 49.3 %all-gather.6.cloned.1.call-start = ((), (), s32[]{:S(2)}) async-start(), calls=%async_computation.4 | async-start | bytes 2621440 | tf_op jit(solution)/shard_map/all_gather | solution.py:122
  11.6 241.2 %reduce-scatter.5.cloned.1.call-start = ((), (), s32[]{:S(2)}) async-start(), calls=%async_computation.5 | async-start | bytes 5242880 | tf_op jit(solution)/shard_map/reduce_scatter | solution.py:133
  12.2 68.6 %copy-start.141 = (f32[384]{0:T(512)}, f32[384]{0:T(512)S(1)}, u32[]{:S(2)}) copy-start(f32[384]{0:T(512)S(1)} %add.468) | copy-start | bytes 4612
  12.3 68.5 %copy-start.143 = (f32[384]{0:T(512)}, f32[384]{0:T(512)S(1)}, u32[]{:S(2)}) copy-start(f32[384]{0:T(512)S(1)} %add.463) | copy-start | bytes 4612
  13.3 67.6 %copy-start.157 = (f32[1024]{0:T(1024)}, f32[1024]{0:T(1024)S(1)}, u32[]{:S(2)}) copy-start(f32[1024]{0:T(1024)S(1)} %get-tuple-element.149) | copy-start | bytes 12292
  172.1 129.7 %all-gather.10.cloned.1.call-start = ((), (), s32[]{:S(2)}) async-start(), calls=%async_computation.7 | async-start | bytes 6488064 | tf_op jit(solution)/shard_map/all_gather | solution.py:148
  172.7 200.2 %all-gather.8.cloned.1.call-start = ((), (), s32[]{:S(2)}) async-start(), calls=%async_computation.6 | async-start | bytes 6488064 | tf_op jit(solution)/shard_map/all_gather | solution.py:147
  173.3 270.6 %all-gather.12.cloned.1.call-start = ((), (), s32[]{:S(2)}) async-start(), calls=%async_computation.8 | async-start | bytes 6488064 | tf_op jit(solution)/shard_map/all_gather | solution.py:149
  173.8 348.1 %all-gather.14.cloned.1.call-start = ((), (), s32[]{:S(2)}) async-start(), calls=%async_computation.9 | async-start | bytes 2621440 | tf_op jit(solution)/shard_map/all_gather | solution.py:182
  174.9 79.4 %copy-start.155 = (f32[1024]{0:T(1024)S(1)}, f32[1024]{0:T(1024)}, u32[]{:S(2)}) copy-start(f32[1024]{0:T(1024)} %param.32) | copy-start | bytes 12292
  254.4 206.9 %copy-start.179 = (f32[256]{0:T(256)}, f32[256]{0:T(256)S(1)}, u32[]{:S(2)}) copy-start(f32[256]{0:T(256)S(1)} %fusion.70) | copy-start | bytes 3076
  463.3 677.9 %reduce-scatter.9.cloned.1.call-start = ((), (), s32[]{:S(2)}) async-start(), calls=%async_computation.11 | async-start | bytes 47185920 | tf_op jit(solution)/shard_map/reduce_scatter | solution.py:166
  521.9 698.8 %reduce-scatter.7.cloned.1.call-start = ((), (), s32[]{:S(2)}) async-start(), calls=%async_computation.10 | async-start | bytes 5242880 | tf_op jit(solution)/shard_map/reduce_scatter | solution.py:195
  705.0 596.5 %reduce-scatter.11.cloned.1.call-start = ((), (), s32[]{:S(2)}) async-start(), calls=%async_computation.12 | async-start | bytes 10616832 | tf_op jit(solution)/shard_map/reduce_scatter | solution.py:179
  1141.3 257.7 %all-reduce.112.cloned.1.call-start = ((), (), s32[]{:S(2)}) async-start(), calls=%async_computation.13 | async-start | bytes 10223616 | tf_op jit(solution)/shard_map/psum | solution.py:206
  1157.4 63.2 %copy-start.154 = (f32[1024]{0:T(1024)S(1)}, f32[1024]{0:T(1024)}, u32[]{:S(2)}) copy-start(f32[1024]{0:T(1024)} %param.21) | copy-start | bytes 12292
  1157.5 63.2 %copy-start.178 = (f32[256]{0:T(256)S(1)}, f32[256]{0:T(256)}, u32[]{:S(2)}) copy-start(f32[256]{0:T(256)} %copy-done.177) | copy-start | bytes 3076
  1163.0 99.2 %copy-start.184 = (f32[256]{0:T(256)S(1)}, f32[256]{0:T(256)}, u32[]{:S(2)}) copy-start(f32[256]{0:T(256)} %copy-done.183) | copy-start | bytes 3076
  1163.0 99.2 %copy-start.32 = (bf16[256,1024]{1,0:T(8,128)(2,1)S(1)}, bf16[256,1024]{1,0:T(8,128)(2,1)}, u32[]{:S(2)}) copy-start(bf16[256,1024]{1,0:T(8,128)(2,1)} %param.20) | copy-start | bytes 1572868
  1163.0 99.2 %copy-start.34 = (f32[256,1024]{1,0:T(8,128)S(1)}, f32[256,1024]{1,0:T(8,128)}, u32[]{:S(2)}) copy-start(f32[256,1024]{1,0:T(8,128)} %copy-done.33) | copy-start | bytes 3145732
  1163.0 99.2 %copy-start.156 = (f32[1024]{0:T(1024)S(1)}, f32[1024]{0:T(1024)}, u32[]{:S(2)}) copy-start(f32[1024]{0:T(1024)} %param.32) | copy-start | bytes 12292
  1163.0 99.2 %copy-start.180 = (f32[256]{0:T(256)S(1)}, f32[256]{0:T(256)}, u32[]{:S(2)}) copy-start(f32[256]{0:T(256)} %copy-done.179) | copy-start | bytes 3076
  1163.0 99.2 %copy-start.182 = (f32[256]{0:T(256)S(1)}, f32[256]{0:T(256)}, u32[]{:S(2)}) copy-start(f32[256]{0:T(256)} %copy-done.181) | copy-start | bytes 3076
  (191 other events, 1304.9 us)
Sparse Core Ops, SparseCore 0:
  11.7 45.6 all-gather.5
  172.2 80.5 reduce-scatter.4
  463.4 43.2 all-gather.13
  522.0 619.1 reduce-scatter.8
  1143.4 77.2 reduce-scatter.6
  1224.4 77.0 reduce-scatter.10
  1307.1 91.8 all-reduce.111
Sparse Core Ops, SparseCore 1:
  175.9 125.9 all-gather.9
  305.0 67.8 all-gather.7
  376.0 67.8 all-gather.11
where the time goes:
time: 1430 us; the launch traced here: 1410 us
  waiting for transfers between devices  898 us (63%)
  local copies, waits for them, and re-layouts  213 us (15%)
  other arithmetic  110 us (8%)
  matrix products  99.8 us (7%)
  blocking collectives  61.6 us (4%)
  between operations  18.5 us (1%)
    reduce_scatter x1, waiting for transfers between devices, on_device(): lax.psum_scatter(jnp.concatenate([contract(second_regrouped, gate_low, 0,...  436 us
    pad x79, local copies, waits for them, and re-layouts, mixer(): lax.associative_scan(combine, (decay * keeper[:, None], inject), axis=0)  97.3 us
    psum x1, waiting for transfers between devices, on_device(): lax.psum((grad_gate, grad_input, grad_out, mix_grads[2], mix_grads[3], mi...  95.2 us
    reduce_scatter x1, waiting for transfers between devices, on_device(): lax.psum_scatter(jnp.dot(lax.slice_in_dim(branch_in, 0, local_rows * lax....  77.8 us
    slice x78, local copies, waits for them, and re-layouts, mixer(): lax.associative_scan(combine, (decay * keeper[:, None], inject), axis=0)  68.4 us
    all_gather x1, waiting for transfers between devices, on_device(): lax.all_gather(mlp_down, ('seq', 'chan'), axis=0, tiled=True)  64.6 us
    all_gather x1, waiting for transfers between devices, on_device(): lax.all_gather(mlp_gate, ('seq', 'chan'), axis=0, tiled=True)  64.6 us
    dot_general x12, matrix products, contract(): lax.dot_general(left, right, (((left_dim,), (right_dim,)), ((), ())), pre...  48.6 us
  transfers between devices with their start and end apart: 10, of which 9 were waited for; matrix products, arithmetic and copies ran while one was open for 19% of the time, Pallas kernels for 0%

commit v1 on v0

v1 whole, which is shorter than its diff:
```python
import functools

import jax
import jax.numpy as jnp
from jax import lax
from jax.experimental import pallas as pl
from jax.experimental.pallas import tpu as pltpu
from jax.sharding import PartitionSpec as P

LENGTH = 1024
EPS = 1e-06
STRENGTH = 8.0
HALO = 16
GELU_A = 0.7978845608028654
GELU_B = 0.044715
BF16 = jnp.bfloat16
F32 = jnp.float32
VMEM_BYTES = 60 * 1024 * 1024


def mm(left, right, left_dim, right_dim):
    return lax.dot_general(
        left, right, (((left_dim,), (right_dim,)), ((), ())), preferred_element_type=F32
    )


def gelu_parts(value):
    square = value * value
    th = jnp.tanh(GELU_A * value * (1.0 + GELU_B * square))
    half = 0.5 * (1.0 + th)
    slope = half + 0.5 * value * (1.0 - th * th) * (GELU_A * (1.0 + 3.0 * GELU_B * square))
    return value * half, slope


def gelu(value):
    th = jnp.tanh(GELU_A * value * (1.0 + GELU_B * value * value))
    return 0.5 * value * (1.0 + th)


def one_minus_exp(v):
    series = v * (
        1.0
        - v
        * (1 / 2)
        * (
            1.0
            - v
            * (1 / 3)
            * (1.0 - v * (1 / 4) * (1.0 - v * (1 / 5) * (1.0 - v * (1 / 6) * (1.0 - v * (1 / 7)))))
        )
    )
    return jnp.where(v < 0.4, series, 1.0 - jnp.exp(-v))


def rows_index(shape):
    return lax.broadcasted_iota(jnp.int32, shape, 0)


def scan_down(a, b):
    count = a.shape[0]
    index = rows_index(a.shape)
    step = 1
    while step < count:
        if step < 8:
            inside = index >= step
            a_prev = jnp.where(inside, pltpu.roll(a, step, 0), 1.0)
            b_prev = jnp.where(inside, pltpu.roll(b, step, 0), 0.0)
        else:
            a_prev = jnp.concatenate([jnp.ones_like(a[:step]), a[: count - step]], axis=0)
            b_prev = jnp.concatenate([jnp.zeros_like(b[:step]), b[: count - step]], axis=0)
        b = b + a * b_prev
        a = a * a_prev
        step *= 2
    return a, b


def scan_up(a, b):
    count = a.shape[0]
    index = rows_index(a.shape)
    step = 1
    while step < count:
        if step < 8:
            inside = index < count - step
            a_next = jnp.where(inside, pltpu.roll(a, count - step, 0), 1.0)
            b_next = jnp.where(inside, pltpu.roll(b, count - step, 0), 0.0)
        else:
            a_next = jnp.concatenate([a[step:], jnp.ones_like(a[:step])], axis=0)
            b_next = jnp.concatenate([b[step:], jnp.zeros_like(b[:step])], axis=0)
        b = b + a * b_next
        a = a * a_next
        step *= 2
    return a, b


def block_diagonal(flat, head, dtype):
    width = flat.shape[1]
    tall = jnp.concatenate([flat] * (width // head), axis=0)
    shape = (width, width)
    row = lax.broadcasted_iota(jnp.int32, shape, 0) // head
    col = lax.broadcasted_iota(jnp.int32, shape, 1) // head
    return jnp.where(row == col, tall, 0.0).astype(dtype)


def fold_diagonal(square, head):
    width = square.shape[0]
    row = lax.broadcasted_iota(jnp.int32, square.shape, 0) // head
    col = lax.broadcasted_iota(jnp.int32, square.shape, 1) // head
    kept = jnp.where(row == col, square, 0.0)
    total = kept[:head]
    for start in range(head, width, head):
        total = total + kept[start : start + head]
    return total


def vmem():
    return pl.BlockSpec(memory_space=pltpu.VMEM)


def smem():
    return pl.BlockSpec(memory_space=pltpu.SMEM)


def params(**more):
    return pltpu.CompilerParams(vmem_limit_bytes=VMEM_BYTES, **more)


def mix_local_kernel(own, head, pieces, me_ref, nx_ref, mask_ref, gates_ref, vec_ref, *rest):
    weight_refs, rest = rest[:pieces], rest[pieces:]
    weights, inputs_out, gated_out, kept_out, scan_out, edge_out = rest[-6:]
    if own:
        weights[0] = weight_refs[0][...]
    else:
        block = weight_refs[0].shape[1]
        for rel in range(pieces):
            start = pl.multiple_of((me_ref[0] ^ rel) * block, block)
            for part in range(3):
                weights[0, part, pl.ds(start, block), :] = weight_refs[rel][part]
    count = mask_ref.shape[0]
    gated = mm(nx_ref[HALO:], weights[0, 0], 1, 0).astype(BF16)
    gated_out[0] = gated
    inputs = mm(nx_ref[...], weights[0, 1], 1, 0).astype(BF16)
    inputs_out[0] = inputs
    wide = inputs.astype(F32)
    vec = vec_ref[...]
    conv = vec[4:5] + vec[0:1] * wide[HALO:]
    for shift in range(1, 4):
        moved = pltpu.roll(wide, shift, 0)[HALO:]
        conv = conv + vec[shift : shift + 1] * (moved * mask_ref[:, shift : shift + 1])
    low = conv.astype(BF16)
    width = conv.shape[1]
    recall_weight = block_diagonal(gates_ref[:, :width], head, BF16)
    admit_weight = block_diagonal(gates_ref[:, width:], head, BF16)
    recall = jax.nn.sigmoid(mm(low, recall_weight, 1, 0) + vec[5:6])
    admit = jax.nn.sigmoid(mm(low, admit_weight, 1, 0) + vec[6:7])
    rate = STRENGTH * recall * vec[7:8]
    decay = jnp.exp(-rate)
    inject = jnp.sqrt(one_minus_exp(2.0 * rate)) * admit * conv
    product, state = scan_down(decay * mask_ref[:, 1:2], inject)
    kept_out[0, 0] = conv
    kept_out[0, 1] = recall
    kept_out[0, 2] = admit
    scan_out[0, 0] = product
    scan_out[0, 1] = state
    edge_out[0, 0:1] = product[count - 1 :]
    edge_out[0, 1:2] = state[count - 1 :]
    edge_out[0, 2:3] = jnp.sum(decay, axis=0, keepdims=True)


def mix_local(shard, shards, head, me, nx, mask, gates, vec, weights, stacks):
    count = mask.shape[0]
    width = vec.shape[1]
    model = nx.shape[1]
    own = shard == 0
    pieces = len(weights)
    shapes = [
        ((shards, 3, model, width), BF16),
        ((shards, count + HALO, width), BF16),
        ((shards, count, width), BF16),
        ((shards, 3, count, width), F32),
        ((shards, 2, count, width), F32),
        ((shards, 8, width), F32),
    ]

    def at(shape):
        tail = (0,) * (len(shape) - 1)
        return pl.BlockSpec((1,) + shape[1:], lambda i: (shard,) + tail)

    first = [me, nx, mask, gates, vec, *weights]
    in_specs = [smem()] + [vmem()] * (len(first) - 1)
    aliases = {}
    if stacks is not None:
        aliases = {len(first) + i: i for i in range(len(stacks))}
        in_specs += [pl.BlockSpec(memory_space=pl.ANY)] * len(stacks)
        first += list(stacks)
    flops = 2 * (2 * count + HALO) * model * width + 4 * count * width * width
    return pl.pallas_call(
        functools.partial(mix_local_kernel, own, head, pieces),
        grid=(1,),
        out_shape=[jax.ShapeDtypeStruct(shape, dtype) for shape, dtype in shapes],
        in_specs=in_specs,
        out_specs=[at(shape) for shape, _ in shapes],
        input_output_aliases=aliases,
        compiler_params=params(),
        cost_estimate=pl.CostEstimate(
            flops=flops, bytes_accessed=8 * 1024 * 1024, transcendentals=6 * count * width
        ),
        name="mix_local",
    )(*first)


def carried(edges):
    total = edges[-1][0, 1:2]
    for edge in edges[-2::-1]:
        total = edge[0, 1:2] + edge[0, 0:1] * total
    return total


def branch_kernel(
    depth, scan_ref, gated_ref, weight_ref, resid_ref, gain_ref, *rest
):
    edges = rest[:depth]
    carry_out, branch_in_out, middle_out, second_out, acc = rest[depth:]
    step = pl.program_id(0)

    @pl.when(step == 0)
    def _():
        acc[...] = resid_ref[...].astype(F32)

    carry = carried(edges)
    carry_out[0] = jnp.broadcast_to(carry, carry_out.shape[1:])
    state = scan_ref[0, 1] + scan_ref[0, 0] * carry
    mixed = (gelu(gated_ref[0].astype(F32)) * state).astype(BF16)
    branch_in_out[0] = mixed
    acc[...] += mm(mixed, weight_ref[0, 0], 1, 1)

    @pl.when(step == pl.num_programs(0) - 1)
    def _():
        middle = acc[...]
        middle_out[...] = middle
        scale = lax.rsqrt(jnp.mean(middle * middle, axis=1, keepdims=True) + EPS)
        second_out[...] = (middle * scale * gain_ref[...]).astype(BF16)


def branch(scan, gated, weights, tokens, gain, edges):
    shards, _, count, width = scan.shape
    model = tokens.shape[1]

    def edge_spec(shift):
        return pl.BlockSpec((1, 8, width), lambda s: ((s + shards - shift % shards) % shards, 0, 0))

    return pl.pallas_call(
        functools.partial(branch_kernel, len(edges)),
        grid=(shards,),
        out_shape=[
            jax.ShapeDtypeStruct((shards, 8, width), F32),
            jax.ShapeDtypeStruct((shards, count, width), BF16),
            jax.ShapeDtypeStruct((count, model), F32),
            jax.ShapeDtypeStruct((count, model), BF16),
        ],
        in_specs=[
            pl.BlockSpec((1, 2, count, width), lambda s: (s, 0, 0, 0)),
            pl.BlockSpec((1, count, width), lambda s: (s, 0, 0)),
            pl.BlockSpec((1, 1, model, width), lambda s: (s, 2, 0, 0)),
            pl.BlockSpec((count, model), lambda s: (0, 0)),
            pl.BlockSpec((1, model), lambda s: (0, 0)),
        ]
        + [edge_spec(i + 1) for i in range(len(edges))],
        out_specs=[
            pl.BlockSpec((1, 8, width), lambda s: (s, 0, 0)),
            pl.BlockSpec((1, count, width), lambda s: (s, 0, 0)),
            pl.BlockSpec((count, model), lambda s: (0, 0)),
            pl.BlockSpec((count, model), lambda s: (0, 0)),
        ],
        scratch_shapes=[pltpu.VMEM((count, model), F32)],
        compiler_params=params(),
        name="mix_branch",
    )(scan, gated, weights, tokens, gain, *edges)


def mlp_kernel(
    sec_a, sec_b, cot_a, cot_b, weight_ref, gate_grad_out, up_grad_out, hidden_out, grad_a, grad_b
):
    second = jnp.concatenate([sec_a[...], sec_b[...]], axis=0)
    cot = jnp.concatenate([cot_a[...], cot_b[...]], axis=0)
    gate = mm(second, weight_ref[0], 1, 0)
    upward = mm(second, weight_ref[1], 1, 0)
    hidden_grad = mm(cot, weight_ref[2], 1, 0)
    act, slope = gelu_parts(gate)
    hidden_out[...] = (act * upward).astype(BF16)
    gate_grad = (hidden_grad * upward * slope).astype(BF16)
    up_grad = (hidden_grad * act).astype(BF16)
    gate_grad_out[...] = gate_grad
    up_grad_out[...] = up_grad
    back = mm(gate_grad, weight_ref[0], 1, 1) + mm(up_grad, weight_ref[1], 1, 1)
    count = sec_a.shape[0]
    grad_a[...] = back[:count].astype(BF16)
    grad_b[...] = back[count:].astype(BF16)


def mlp_block(sec_a, sec_b, cot_a, cot_b, weights):
    count, model = sec_a.shape
    width = weights.shape[2]
    wide = jax.ShapeDtypeStruct((2 * count, width), BF16)
    tall = jax.ShapeDtypeStruct((count, model), BF16)
    return pl.pallas_call(
        mlp_kernel,
        out_shape=[wide, wide, wide, tall, tall],
        in_specs=[vmem()] * 5,
        out_specs=[vmem()] * 5,
        compiler_params=params(),
        cost_estimate=pl.CostEstimate(
            flops=20 * count * model * width,
            bytes_accessed=8 * 1024 * 1024,
            transcendentals=2 * count * width,
        ),
        name="mlp_block",
    )(sec_a, sec_b, cot_a, cot_b, weights)


def mlp_grads_kernel(blocks, model, weight_ref, *rest):
    seconds, rest = rest[: 2 * blocks], rest[2 * blocks :]
    cots, rest = rest[: 2 * blocks], rest[2 * blocks :]
    gate_grads, rest = rest[:blocks], rest[blocks:]
    up_grads, rest = rest[:blocks], rest[blocks:]
    hiddens, rest = rest[:blocks], rest[blocks:]
    grads_out, rest = rest[0], rest[1:]
    results, acc = rest[: 2 * blocks], rest[2 * blocks]
    count = seconds[0].shape[0]
    for block in range(blocks):
        second = jnp.concatenate([seconds[2 * block][...], seconds[2 * block + 1][...]], axis=0)
        cot = jnp.concatenate([cots[2 * block][...], cots[2 * block + 1][...]], axis=0)
        hidden = hiddens[block][...]
        terms = (
            mm(second, gate_grads[block][...], 0, 0),
            mm(second, up_grads[block][...], 0, 0),
            mm(cot, hidden, 0, 0),
        )
        for part, term in enumerate(terms):
            if block == 0:
                acc[part] = term
            else:
                acc[part] += term
        result = mm(hidden, weight_ref[0], 1, 1)
        results[2 * block][...] = result[:count].astype(BF16)
        results[2 * block + 1][...] = result[count:].astype(BF16)
    shards, group, _, piece, _ = grads_out.shape
    for shard in range(shards):
        for owner in range(group):
            start = (owner * shards + shard) * piece
            for part in range(3):
                grads_out[shard, owner, part] = acc[part, start : start + piece].astype(BF16)


def mlp_grads(weights, seconds, cots, gate_grads, up_grads, hiddens, shards):
    group = len(seconds)
    count, model = seconds[0].shape
    width = weights.shape[2]
    piece = model // (group * shards)
    return pl.pallas_call(
        functools.partial(mlp_grads_kernel, group // 2, model),
        grid=(1,),
        out_shape=[jax.ShapeDtypeStruct((shards, group, 3, piece, width), BF16)]
        + [jax.ShapeDtypeStruct((count, model), BF16)] * group,
        in_specs=[pl.BlockSpec((1, model, width), lambda i: (2, 0, 0))]
        + [vmem()] * (2 * group + 3 * (group // 2)),
        out_specs=[vmem()] * (1 + group),
        scratch_shapes=[pltpu.VMEM((3, model, width), F32)],
        compiler_params=params(),
        cost_estimate=pl.CostEstimate(
            flops=8 * count * group * model * width,
            bytes_accessed=20 * 1024 * 1024,
            transcendentals=0,
        ),
        name="mlp_grads",
    )(weights, *seconds, *cots, *gate_grads, *up_grads, *hiddens)


def split_rows(me, values, own_out, other_out, lead):
    half, _, _, block, _ = own_out.shape
    for j in range(half):
        for out, rel in ((own_out, 2 * j), (other_out, 2 * j + 1)):
            start = pl.multiple_of((me ^ rel) * block, block)
            out[j, 0, lead] = values[pl.ds(start, block), :]


def adjoint_kernel(
    me_ref,
    grad_ref,
    normed_ref,
    weight_ref,
    gated_ref,
    scan_ref,
    kept_ref,
    carry_ref,
    branch_in_ref,
    mask_ref,
    rate_ref,
    gate_back_out,
    adjoint_out,
    edge_out,
    own_out,
    other_out,
    whole,
):
    grad = grad_ref[...]
    into = mm(grad, weight_ref[0, 0], 1, 0).astype(BF16).astype(F32)
    act, slope = gelu_parts(gated_ref[0].astype(F32))
    state = scan_ref[0, 1] + scan_ref[0, 0] * carry_ref[0, 0:1]
    gate_back = (into * state * slope).astype(BF16)
    gate_back_out[0] = gate_back
    decay = jnp.exp(-STRENGTH * kept_ref[0, 0] * rate_ref[0]) * mask_ref[:, 1:2]
    count = decay.shape[0]
    shifted = jnp.where(
        rows_index(decay.shape) < count - 1, pltpu.roll(decay, count - 1, 0), 1.0
    )
    product, value = scan_up(shifted, into * act)
    adjoint_out[0, 0] = product
    adjoint_out[0, 1] = value
    edge_out[0] = jnp.broadcast_to(decay[0:1] * value[0:1], edge_out.shape[1:])
    whole[...] = mm(normed_ref[...], gate_back, 0, 0).astype(BF16)
    split_rows(me_ref[0], whole, own_out, other_out, 0)
    whole[...] = mm(grad, branch_in_ref[0], 0, 0).astype(BF16)
    split_rows(me_ref[0], whole, own_out, other_out, 1)


def adjoint(me, grad, normed, weights, gated, scan, kept, carry, branch_in, mask, rate, group):
    shards, _, count, width = scan.shape
    model = grad.shape[1]
    block = model // group

    def flat(*shape):
        return pl.BlockSpec(shape, lambda s: (0,) * len(shape))

    def at(*shape):
        return pl.BlockSpec((1,) + shape, lambda s: (s,) + (0,) * len(shape))

    split = jax.ShapeDtypeStruct((group // 2, shards, 2, block, width), BF16)
    split_spec = pl.BlockSpec((group // 2, 1, 2, block, width), lambda s: (0, s, 0, 0, 0))
    return pl.pallas_call(
        adjoint_kernel,
        grid=(shards,),
        out_shape=[
            jax.ShapeDtypeStruct((shards, count, width), BF16),
            jax.ShapeDtypeStruct((shards, 2, count, width), F32),
            jax.ShapeDtypeStruct((shards, 8, width), F32),
            split,
            split,
        ],
        in_specs=[
            smem(),
            flat(count, model),
            flat(count, model),
            pl.BlockSpec((1, 1, model, width), lambda s: (s, 2, 0, 0)),
            at(count, width),
            at(2, count, width),
            pl.BlockSpec((1, 1, count, width), lambda s: (s, 1, 0, 0)),
            at(8, width),
            at(count, width),
            flat(*mask.shape),
            at(1, width),
        ],
        out_specs=[at(count, width), at(2, count, width), at(8, width), split_spec, split_spec],
        scratch_shapes=[pltpu.VMEM((model, width), BF16)],
        compiler_params=params(),
        cost_estimate=pl.CostEstimate(
            flops=6 * count * model * width * shards,
            bytes_accessed=24 * 1024 * 1024,
            transcendentals=4 * count * width * shards,
        ),
        name="mix_adjoint",
    )(me, grad, normed, weights, gated, scan, kept, carry, branch_in, mask, rate)


def mix_back_kernel(
    head,
    depth,
    me_ref,
    nx_ref,
    gate_weight_ref,
    input_weight_ref,
    inputs_ref,
    gate_back_ref,
    kept_ref,
    scan_ref,
    adjoint_ref,
    carry_ref,
    mask_ref,
    gates_ref,
    vec_ref,
    edge_ref,
    *rest,
):
    backs, decays = rest[:depth], rest[depth : 2 * depth - 1]
    own_out, other_out, normed_grad_out, whole, acc = rest[2 * depth - 1 :]
    step = pl.program_id(0)
    count = mask_ref.shape[0]
    width = vec_ref.shape[2]
    vec = vec_ref[0]
    incoming = backs[-1][0, 0:1]
    for back, edge in zip(backs[-2::-1], decays[::-1], strict=True):
        incoming = back[0, 0:1] + edge[0, 0:1] * incoming
    adj = adjoint_ref[0, 1] + adjoint_ref[0, 0] * incoming
    carry = carry_ref[0, 0:1]
    state = scan_ref[0, 1] + scan_ref[0, 0] * carry
    before = jnp.where(rows_index(state.shape) == 0, carry, pltpu.roll(state, 1, 0))
    conv, recall, admit = kept_ref[0, 0], kept_ref[0, 1], kept_ref[0, 2]
    speed = STRENGTH * vec[7:8]
    rate = recall * speed
    decay = jnp.exp(-rate)
    size = jnp.sqrt(one_minus_exp(2.0 * rate))
    sized = adj * size
    pulled = adj * admit
    log_grad = decay * (adj * before * mask_ref[:, 1:2] - pulled * conv * decay / size)
    recall_grad = -speed * log_grad * recall * (1.0 - recall)
    admit_grad = sized * conv * admit * (1.0 - admit)
    conv_grad = sized * admit
    recall_low = recall_grad.astype(BF16)
    admit_low = admit_grad.astype(BF16)
    recall_weight = block_diagonal(gates_ref[0, :, :width], head, BF16)
    admit_weight = block_diagonal(gates_ref[0, :, width:], head, BF16)
    conv_grad = conv_grad + mm(recall_low, recall_weight, 1, 1) + mm(admit_low, admit_weight, 1, 1)
    wide = inputs_ref[0].astype(F32)
    blank = jnp.zeros((HALO, width), F32)
    reach = jnp.concatenate([blank, vec[0:1] * conv_grad], axis=0)
    tap_grads = [jnp.sum(conv_grad * wide[HALO:], axis=0, keepdims=True)]
    for shift in range(1, 4):
        masked = conv_grad * mask_ref[:, shift : shift + 1]
        moved = pltpu.roll(wide, shift, 0)[HALO:]
        tap_grads.append(jnp.sum(masked * moved, axis=0, keepdims=True))
        back = jnp.concatenate([blank, vec[shift : shift + 1] * masked], axis=0)
        reach = reach + pltpu.roll(back, count + HALO - shift, 0)
    input_back = reach.astype(BF16)
    conv_low = conv.astype(BF16)
    model = nx_ref.shape[1]
    whole[:model] = mm(nx_ref[...], input_back, 0, 0).astype(BF16)
    whole[model : model + head] = fold_diagonal(mm(conv_low, recall_low, 0, 0), head).astype(BF16)
    whole[model + head : model + 2 * head] = fold_diagonal(
        mm(conv_low, admit_low, 0, 0), head
    ).astype(BF16)
    rows = tap_grads + [
        jnp.sum(conv_grad, axis=0, keepdims=True),
        jnp.sum(recall_grad, axis=0, keepdims=True),
        jnp.sum(admit_grad, axis=0, keepdims=True),
        jnp.sum(recall * log_grad, axis=0, keepdims=True),
        edge_ref[0, 2:3],
    ]
    rows.append(jnp.zeros((whole.shape[0] - model - 2 * head - len(rows), width), F32))
    whole[model + 2 * head :] = jnp.concatenate(rows, axis=0).astype(BF16)
    half, _, block, _ = own_out.shape
    main = model // (2 * half)
    extra = block - main
    for j in range(half):
        for out, rel in ((own_out, 2 * j), (other_out, 2 * j + 1)):
            owner = me_ref[0] ^ rel
            start = pl.multiple_of(owner * main, main)
            out[j, 0, :main] = whole[pl.ds(start, main), :]
            start = pl.multiple_of(model + owner * extra, extra)
            out[j, 0, main:] = whole[pl.ds(start, extra), :]
    through_gate = mm(gate_back_ref[0], gate_weight_ref[0, 0], 1, 1)
    through_input = mm(input_back, input_weight_ref[0, 0], 1, 1)

    @pl.when(step == 0)
    def _():
        acc[...] = through_input

    @pl.when(step > 0)
    def _():
        acc[...] += through_input

    acc[HALO:] += through_gate

    @pl.when(step == pl.num_programs(0) - 1)
    def _():
        normed_grad_out[...] = acc[...]


def mix_back(
    me, nx, weights, inputs, gate_back, kept, scan, adj, carry, mask, gates, vec, edge, backs, ahead, group
):
    shards, _, count, width = scan.shape
    model = nx.shape[1]
    head = gates.shape[1]
    depth = len(backs)
    tall = model + 256
    block = tall // group

    def flat(*shape):
        return pl.BlockSpec(shape, lambda s: (0,) * len(shape))

    def at(*shape):
        return pl.BlockSpec((1,) + shape, lambda s: (s,) + (0,) * len(shape))

    def ahead_spec(shift):
        return pl.BlockSpec((1, 8, width), lambda s: ((s + shift) % shards, 0, 0))

    split = jax.ShapeDtypeStruct((group // 2, shards, block, width), BF16)
    split_spec = pl.BlockSpec((group // 2, 1, block, width), lambda s: (0, s, 0, 0))
    return pl.pallas_call(
        functools.partial(mix_back_kernel, head, depth),
        grid=(shards,),
        out_shape=[split, split, jax.ShapeDtypeStruct((count + HALO, model), F32)],
        in_specs=[
            smem(),
            flat(count + HALO, model),
            pl.BlockSpec((1, 1, model, width), lambda s: (s, 0, 0, 0)),
            pl.BlockSpec((1, 1, model, width), lambda s: (s, 1, 0, 0)),
            at(count + HALO, width),
            at(count, width),
            at(3, count, width),
            at(2, count, width),
            at(2, count, width),
            at(8, width),
            flat(*mask.shape),
            at(head, 2 * width),
            at(8, width),
            at(8, width),
        ]
        + [ahead_spec(i + 1) for i in range(depth)]
        + [ahead_spec(i + 1) for i in range(depth - 1)],
        out_specs=[split_spec, split_spec, flat(count + HALO, model)],
        scratch_shapes=[
            pltpu.VMEM((tall, width), BF16),
            pltpu.VMEM((count + HALO, model), F32),
        ],
        compiler_params=params(),
        cost_estimate=pl.CostEstimate(
            flops=6 * count * model * width * shards,
            bytes_accessed=24 * 1024 * 1024,
            transcendentals=4 * count * width * shards,
        ),
        name="mix_back",
    )(
        me, nx, weights, weights, inputs, gate_back, kept, scan, adj, carry, mask, gates, vec, edge,
        *backs, *ahead
    )


def on_device(
    tokens,
    doc_ids,
    cotangent,
    norm_gain,
    gate_proj,
    input_proj,
    conv_weight,
    conv_bias,
    recall_weight,
    recall_bias,
    admit_weight,
    admit_bias,
    decay_param,
    out_proj,
    mlp_gain,
    mlp_gate,
    mlp_up,
    mlp_down,
):
    count, model = tokens.shape
    width = gate_proj.shape[1]
    heads, head, _ = recall_weight.shape
    hidden_width = mlp_gate.shape[1]
    piece = mlp_gate.shape[0]
    group = lax.axis_size("seq")
    shards = lax.axis_size("chan")
    block = model // group
    rank = lax.axis_index("seq")
    place = lax.axis_index("chan")
    me = rank.reshape(1).astype(jnp.int32)

    def flip(values, rel):
        return lax.ppermute(values, "seq", [(i, i ^ rel) for i in range(group)])

    def along(values, shift):
        return lax.ppermute(values, "chan", [(i, (i + shift) % shards) for i in range(shards)])

    def spread(values):
        held = [None] * group
        for rel in range(0, group, 2):
            held[rel] = values if rel == 0 else flip(values, rel)
        for rel in range(0, group, 2):
            held[rel + 1] = flip(held[rel], 1)
        return held

    def gather_sum(values):
        total = None
        for rel in range(0, group, 2):
            other = flip(values[rel + 1], 1)
            both = values[rel].astype(F32) + other.astype(F32)
            if rel:
                both = flip(both.astype(BF16), rel).astype(F32)
            total = both if total is None else total + both
        return total

    stacked = jnp.stack([gate_proj, input_proj, out_proj.T])
    mine = lax.dynamic_slice_in_dim(stacked, rank * block, block, 1)
    order = [0] + [s for i in range(1, shards // 2 + 1) for s in dict.fromkeys((i, shards - i))]
    at_shard = {}
    for shard in order[1:]:
        if shard == 1:
            at_shard[1] = along(mine, 1)
        elif shard <= shards // 2:
            at_shard[shard] = along(at_shard[shard - 1], 1)
        elif shard == shards - 1:
            at_shard[shard] = along(mine, -1)
        else:
            at_shard[shard] = along(at_shard[shard + 1], -1)
    weight_pieces = {0: [stacked]}
    for shard in order[1:]:
        weight_pieces[shard] = spread(at_shard[shard])

    speed = jax.nn.softplus(-decay_param)
    vec = jnp.concatenate(
        [
            conv_weight,
            conv_bias[None],
            recall_bias.reshape(1, width),
            admit_bias.reshape(1, width),
            speed[None],
        ]
    )
    gates = jnp.concatenate(
        [
            recall_weight.transpose(1, 0, 2).reshape(head, width),
            admit_weight.transpose(1, 0, 2).reshape(head, width),
        ],
        axis=1,
    ).astype(BF16)
    vecs = [vec] + [along(vec, s) for s in range(1, shards)]
    gates_all = [gates] + [along(gates, s) for s in range(1, shards)]

    offset = place * count
    spots = (offset + jnp.arange(count)) % LENGTH
    padded = jnp.concatenate([jnp.full((HALO,), -1, jnp.int32), doc_ids])
    here = lax.dynamic_slice_in_dim(padded, offset + HALO, count)
    columns = [jnp.ones((count,), F32)]
    for shift in range(1, 4):
        moved = lax.dynamic_slice_in_dim(padded, offset + HALO - shift, count)
        columns.append(((spots >= shift) & (here == moved)).astype(F32))
    columns += [jnp.zeros((count,), F32)] * 4
    mask = jnp.stack(columns, axis=1)

    resid = tokens.astype(F32)
    scale_one = lax.rsqrt(jnp.mean(resid * resid, axis=1, keepdims=True) + EPS)
    normed = (resid * scale_one * norm_gain).astype(BF16)
    nx = jnp.concatenate([along(normed[count - HALO :], 1), normed])

    slices = jnp.stack([mlp_gate, mlp_up, mlp_down])
    own_width = hidden_width // group
    slices = slices.reshape(3, piece, group, own_width).transpose(2, 0, 1, 3)
    slices = lax.all_to_all(slices, "seq", 0, 0, tiled=True)
    slices = lax.all_gather(slices, "chan", axis=0)
    mlp_weights = slices.transpose(2, 1, 0, 3, 4).reshape(3, model, own_width)

    cots = spread(cotangent)

    stacks = None
    for shard in order:
        stacks = mix_local(
            shard,
            shards,
            head,
            me,
            nx,
            mask,
            gates_all[shard],
            vecs[shard],
            weight_pieces[shard],
            stacks,
        )
    weights, inputs, gated, kept, scan, edge = stacks
    depth = LENGTH // count - 1
    behind = [along(edge, i + 1) for i in range(depth)]
    carry, branch_in, middle, second = branch(
        scan, gated, weights, tokens, mlp_gain.reshape(1, model), behind
    )
    ahead = [along(edge, -(i + 1)) for i in range(depth - 1)]

    seconds = spread(second)
    gate_grads, up_grads, hiddens, backs = [], [], [], []
    for rel in range(0, group, 2):
        gate_grad, up_grad, hidden, back_a, back_b = mlp_block(
            seconds[rel], seconds[rel + 1], cots[rel], cots[rel + 1], mlp_weights
        )
        gate_grads.append(gate_grad)
        up_grads.append(up_grad)
        hiddens.append(hidden)
        backs += [back_a, back_b]
    second_grad = gather_sum(backs)
    grads, *results = mlp_grads(
        mlp_weights, seconds, cots, gate_grads, up_grads, hiddens, shards
    )
    block_out = (middle + gather_sum(results)).astype(BF16)
    grads = lax.psum_scatter(grads, "chan", scatter_dimension=0)
    grads = lax.all_to_all(grads, "seq", 0, 0, tiled=True)
    grads = grads.transpose(1, 2, 0, 3).reshape(3, piece, hidden_width).astype(F32)

    def norm_back(grad, values, gain):
        scale = lax.rsqrt(jnp.mean(values * values, axis=1, keepdims=True) + EPS)
        scaled = grad * gain
        inner = jnp.mean(scaled * values, axis=1, keepdims=True)
        return (
            scale * scaled - values * (scale * scale * scale * inner),
            jnp.sum(grad * values * scale, axis=0),
        )

    back, gain_two = norm_back(second_grad, middle, mlp_gain)
    middle_grad = cotangent.astype(F32) + back
    branch_grad = middle_grad.astype(BF16)

    rate = jnp.stack([v[7:8] for v in vecs])
    gate_back, adj, edge_back, own_one, other_one = adjoint(
        me, branch_grad, normed, weights, gated, scan, kept, carry, branch_in, mask, rate, group
    )
    edges_back = [along(edge_back, -(i + 1)) for i in range(depth)]
    own_two, other_two, normed_grad = mix_back(
        me,
        nx,
        weights,
        inputs,
        gate_back,
        kept,
        scan,
        adj,
        carry,
        mask,
        jnp.stack(gates_all),
        jnp.stack(vecs),
        edge,
        edges_back,
        ahead,
        group,
    )

    def reduce(own, other):
        chip = own.astype(F32) + flip(other, 1).astype(F32)
        total = chip[0]
        for j in range(1, group // 2):
            total = total + flip(chip[j].astype(BF16), 2 * j).astype(F32)
        result = total[0]
        for s in range(1, shards):
            result = result + along(total[s].astype(BF16), -s).astype(F32)
        return result.astype(BF16)

    def assemble(values):
        held = jnp.stack(spread(values))
        index = jnp.arange(group) ^ rank
        return held[index]

    one = assemble(reduce(own_one, other_one))
    two = assemble(reduce(own_two, other_two))
    grad_gate = one[:, 0].reshape(model, width).astype(F32)
    grad_out = one[:, 1].reshape(model, width).T.astype(F32)
    grad_input = two[:, :block].reshape(model, width).astype(F32)
    small = two[:, block:].reshape(256, width).astype(F32)
    grad_recall = small[:head].reshape(head, heads, head).transpose(1, 0, 2)
    grad_admit = small[head : 2 * head].reshape(head, heads, head).transpose(1, 0, 2)
    lines = small[2 * head :]

    halo_grad = along(normed_grad[:HALO].astype(BF16), -1).astype(F32)
    inside = (place + 1) * count % LENGTH != 0
    normed_grad = normed_grad[HALO:]
    tail = normed_grad[count - HALO :] + jnp.where(inside, halo_grad, 0.0)
    normed_grad = jnp.concatenate([normed_grad[: count - HALO], tail])
    token_part, gain_one = norm_back(normed_grad, resid, norm_gain)
    grad_tokens = middle_grad + token_part
    gains = jnp.stack([gain_one, gain_two])
    rel = 1
    while rel < group:
        gains = gains + flip(gains, rel)
        rel *= 2
    rel = 1
    while rel < shards:
        gains = gains + lax.ppermute(gains, "chan", [(i, i ^ rel) for i in range(shards)])
        rel *= 2
    total_rows = count * group * shards
    return (
        block_out,
        grad_tokens,
        gains[0],
        grad_gate,
        grad_input,
        lines[:4],
        lines[4],
        grad_recall,
        lines[5].reshape(heads, head),
        grad_admit,
        lines[6].reshape(heads, head),
        lines[7] * STRENGTH * jax.nn.sigmoid(-decay_param),
        grad_out,
        gains[1],
        grads[0],
        grads[1],
        grads[2],
        lines[8] / total_rows,
    )


def solution(mesh):
    in_specs = (
        P(("seq", "chan"), None),
        P("seq"),
        P(("seq", "chan"), None),
        P(),
        P(None, "chan"),
        P(None, "chan"),
        P(None, "chan"),
        P("chan"),
        P("chan", None, None),
        P("chan", None),
        P("chan", None, None),
        P("chan", None),
        P("chan"),
        P("chan", None),
        P(),
        P(("seq", "chan"), None),
        P(("seq", "chan"), None),
        P(("seq", "chan"), None),
    )
    out_specs = (
        P(("seq", "chan"), None),
        P(("seq", "chan"), None),
        P(),
        P(None, "chan"),
        P(None, "chan"),
        P(None, "chan"),
        P("chan"),
        P("chan", None, None),
        P("chan", None),
        P("chan", None, None),
        P("chan", None),
        P("chan"),
        P("chan", None),
        P(),
        P(("seq", "chan"), None),
        P(("seq", "chan"), None),
        P(("seq", "chan"), None),
        P("chan"),
    )
    return jax.shard_map(
        on_device, mesh=mesh, in_specs=in_specs, out_specs=out_specs, check_vma=False
    )
```

time: 1430 us -> 462 us (0.32)
  waiting for transfers between devices: 898 us -> 137 us
  local copies, waits for them, and re-layouts: 213 us -> 25.3 us
  starting transfers between devices: 12.4 us -> 148 us
  Pallas kernels: 0 us -> 100 us
  matrix products: 99.8 us -> 0 us
  other arithmetic: 110 us -> 29.9 us
  blocking collectives: 61.6 us -> 0 us
    reduce_scatter x4 -> x1, waiting for transfers between devices: 586 us -> 0.01 us  [on_device(): grads = lax.psum_scatter(grads, 'chan', scatter_dimension=0)]
    all_gather x5 -> x1, waiting for transfers between devices: 216 us -> 0.01 us  [on_device(): slices = lax.all_gather(slices, 'chan', axis=0)]
    ppermute x0 -> x99, starting transfers between devices: none -> 139 us  [the longest x74 91.2 us: flip(): return lax.ppermute(values, 'seq', [(i, i ^ rel) for i in range(group)])]
    ppermute x0 -> x99, waiting for transfers between devices: none -> 135 us  [the longest x74 96.8 us: flip(): return lax.ppermute(values, 'seq', [(i, i ^ rel) for i in range(group)])]
    pallas_call x0 -> x12, Pallas kernels: none -> 100 us  [the longest x4 24.7 us: mlp_block(): pl.pallas_call(mlp_kernel, out_shape=[wide, wide, wide, tall, tall], in_s...]
    dot_general x24 -> x0, matrix products: 99.8 us -> none  [the longest x12 48.6 us: contract(): lax.dot_general(left, right, (((left_dim,), (right_dim,)), ((), ())), pre...]
    pad x79 -> x0, local copies, waits for them, and re-layouts: 97.3 us -> none  [mixer(): lax.associative_scan(combine, (decay * keeper[:, None], inject), axis=0)]
    psum x1 -> x0, waiting for transfers between devices: 95.2 us -> none  [on_device(): lax.psum((grad_gate, grad_input, grad_out, mix_grads[2], mix_grads[3], mi...]
  transfers between devices with their start and end apart: 10 -> 103, of which waited for: 9 -> 32; matrix products, arithmetic and copies ran while one was open for 19% -> 9% of each run, Pallas kernels for 0% -> 15%
where the time goes in v1:
time: 462 us; the launch traced here: 456 us
  starting transfers between devices  148 us (32%)
  waiting for transfers between devices  137 us (30%)
  Pallas kernels  100 us (22%)
  other arithmetic  29.9 us (6%)
  local copies, waits for them, and re-layouts  25.3 us (5%)
  between operations  15.6 us (3%)
    ppermute x74, waiting for transfers between devices, flip(): return lax.ppermute(values, 'seq', [(i, i ^ rel) for i in range(group)])  96.8 us
    ppermute x74, starting transfers between devices, flip(): return lax.ppermute(values, 'seq', [(i, i ^ rel) for i in range(group)])  91.2 us
    ppermute x23, waiting for transfers between devices, along(): lax.ppermute(values, 'chan', [(i, (i + shift) % shards) for i in range(sh...  36.7 us
    ppermute x23, starting transfers between devices, along(): lax.ppermute(values, 'chan', [(i, (i + shift) % shards) for i in range(sh...  30.6 us
    pallas_call x4, Pallas kernels, mlp_block(): pl.pallas_call(mlp_kernel, out_shape=[wide, wide, wide, tall, tall], in_s...  24.7 us
    pallas_call x4, Pallas kernels, mix_local(): pl.pallas_call(functools.partial(mix_local_kernel, own, head, pieces), gr...  23.2 us
    pallas_call x1, Pallas kernels, mix_back(): pl.pallas_call(functools.partial(mix_back_kernel, head, depth), grid=(sha...  17.7 us
    ppermute x2, starting transfers between devices, on_device(): lax.ppermute(gains, 'chan', [(i, i ^ rel) for i in range(shards)])  16.9 us
  transfers between devices with their start and end apart: 103, of which 32 were waited for; matrix products, arithmetic and copies ran while one was open for 9% of the time, Pallas kernels for 15%

profile of v1, /device:TPU:17, one launch (start us, length us, event | category | flops | bytes accessed | tf_op | source)
XLA Modules:
  0.0 456.0 jit_solution(14555534745325708677)
XLA Ops:
  38.8 6.0 %collective-permute-start.24 = (bf16[3,128,384]{2,1,0:T(8,128)(2,1)S(1)}, bf16[3,128,384]{2,1,0:T(8,128)(2,1)S(1)}, u32[]{:S(2)}, u32[]{:S(2)}) collective-permute-start(bf16[3,128,384]{2,1,0:T(8,128)(2,1)S(1)} %collective-permute-done.3.rest_0_), channel_id=1, source_target_pairs={{0,4},{4,0},{8,12},{12,8},{16,20},{20,16},{24,28},{28,24},{1,5},{5... | collective-permute-start | bytes 884744 | tf_op jit(solution)/shard_map/ppermute | solution.py:671
  54.7 7.1 %collective-permute-start.28 = (bf16[3,128,384]{2,1,0:T(8,128)(2,1)S(1)}, bf16[3,128,384]{2,1,0:T(8,128)(2,1)S(1)}, u32[]{:S(2)}, u32[]{:S(2)}) collective-permute-start(bf16[3,128,384]{2,1,0:T(8,128)(2,1)S(1)} %collective-permute-done.27.rest_4_), channel_id=1, source_target_pairs={{0,4},{4,0},{8,12},{12,8},{16,20},{20,16},{24,28},{28,24},{1,5},{5... | collective-permute-start | bytes 884744 | tf_op jit(solution)/shard_map/ppermute | solution.py:671
  62.3 11.8 %collective-permute-done.4.rest_0_ = bf16[3,128,384]{2,1,0:T(8,128)(2,1)S(1)} collective-permute-done((bf16[3,128,384]{2,1,0:T(8,128)(2,1)S(1)}, bf16[3,128,384]{2,1,0:T(8,128)(2,1)S(1)}, u32[]{:S(2)}, u32[]{:S(2)}) %collective-permute-start.4) | collective-permute-done | bytes 294944 | tf_op jit(solution)/shard_map/ppermute | solution.py:674
  93.6 6.3 %mix_local.4 = (bf16[4,3,1024,384]{3,2,1,0:T(8,128)(2,1)}, bf16[4,272,384]{2,1,0:T(8,128)(2,1)}, bf16[4,256,384]{2,1,0:T(8,128)(2,1)}, f32[4,3,256,384]{3,2,1,0:...) custom-call(s32[1]{0:T(128)} %bitcast.me_ref, bf16[272,1024]{1,0:T(8,128)(2,1)} %pad_maximum_fusion.3.nx_ref, ...), custom_call_target="tpu_custom_call" | custom-call | flops 566231040 | bytes 8388608 | tf_op jit(solution)/shard_map/mix_local/pallas_call | solution.py:196
  105.7 5.7 %mix_local.6 = (bf16[4,3,1024,384]{3,2,1,0:T(8,128)(2,1)}, bf16[4,272,384]{2,1,0:T(8,128)(2,1)}, bf16[4,256,384]{2,1,0:T(8,128)(2,1)}, f32[4,3,256,384]{3,2,1,0:...) custom-call(s32[1]{0:T(128)} %bitcast.me_ref, ...), custom_call_target="tpu_custom_call", output_to_operand_aliasing={{0}: (13, {}), {1}: (14, {}), {2}: (15, {}), {3}: (16, {}),... | custom-call | flops 566231040 | bytes 8388608 | tf_op jit(solution)/shard_map/mix_local/pallas_call | solution.py:196
  126.5 6.7 %mix_branch.1 = (f32[4,8,384]{2,1,0:T(8,128)}, bf16[4,256,384]{2,1,0:T(8,128)(2,1)}, f32[256,1024]{1,0:T(8,128)}, bf16[256,1024]{1,0:T(8,128)(2,1)}) custom-call(f32[4,2,256,384]{3,2,1,0:T(8,128)} %get-tuple-element.101.scan_ref, bf16[4,256,384]{2,1,0:T(8,128)(2,1)} %get-tuple-element.102.gated_ref, ...), custom_call_target="tpu_custom_call" | custom-call | tf_op jit(solution)/shard_map/mix_branch/pallas_call | solution.py:251
  138.5 9.0 %collective-permute-done.35.sec_a.rest_2_ = bf16[256,1024]{1,0:T(8,128)(2,1)} collective-permute-done((bf16[256,1024]{1,0:T(8,128)(2,1)}, bf16[256,1024]{1,0:T(8,128)(2,1)}, u32[]{:S(2)}, u32[]{:S(2)}) %collective-permute-start.35) | collective-permute-done | bytes 524320 | tf_op jit(solution)/shard_map/ppermute | solution.py:671
  151.7 10.1 %collective-permute-start.38 = (bf16[256,1024]{1,0:T(8,128)(2,1)}, bf16[256,1024]{1,0:T(8,128)(2,1)}, u32[]{:S(2)}, u32[]{:S(2)}) collective-permute-start(bf16[256,1024]{1,0:T(8,128)(2,1)} %collective-permute-done.37.sec_a.rest_4_), channel_id=1, source_target_pairs={{0,4},{4,0},{8,12},{12,8},{16,20},{20,16},{24,28},{28,24},{1,5},{5... | collective-permute-start | bytes 1572872 | tf_op jit(solution)/shard_map/ppermute | solution.py:671
  166.9 6.2 %mlp_block.5 = (bf16[512,384]{1,0:T(8,128)(2,1)}, bf16[512,384]{1,0:T(8,128)(2,1)}, bf16[512,384]{1,0:T(8,128)(2,1)}, bf16[256,1024]{1,0:T(8,128)(2,1)}, bf16[256,1024]{1,0:T(8,128)(2,1)}) custom-call(bf16[256,1024]{1,0:T(8,128)(2,1)} %collective-permute-done.35.sec_a.rest_2_, bf16[256,1024]{1,0:T(8,128)(2,1)} %copy-done.70, bf16[256,1024]{1,0:T(8,128)(2,1)} %copy-done.68, ...), custom_call_target="tpu_custom_call" | custom-call | flops 2013265920 | bytes 8388608 | tf_op jit(solution)/shard_map/mlp_block/pallas_call | solution.py:305
  173.5 6.2 %mlp_block.6 = (bf16[512,384]{1,0:T(8,128)(2,1)}, bf16[512,384]{1,0:T(8,128)(2,1)}, bf16[512,384]{1,0:T(8,128)(2,1)}, bf16[256,1024]{1,0:T(8,128)(2,1)}, bf16[256,1024]{1,0:T(8,128)(2,1)}) custom-call(bf16[256,1024]{1,0:T(8,128)(2,1)} %collective-permute-done.37.sec_a.rest_4_, bf16[256,1024]{1,0:T(8,128)(2,1)} %collective-permute-done.38.sec_b.rest_5_, ...), custom_call_target="tpu_custom_call" | custom-call | flops 2013265920 | bytes 8388608 | tf_op jit(solution)/shard_map/mlp_block/pallas_call | solution.py:305
  179.8 6.2 %mlp_block.4 = (bf16[512,384]{1,0:T(8,128)(2,1)}, bf16[512,384]{1,0:T(8,128)(2,1)}, bf16[512,384]{1,0:T(8,128)(2,1)}, bf16[256,1024]{1,0:T(8,128)(2,1)}, bf16[256,1024]{1,0:T(8,128)(2,1)}) custom-call(bf16[256,1024]{1,0:T(8,128)(2,1)} %get-tuple-element.106.sec_a.rest_0_, bf16[256,1024]{1,0:T(8,128)(2,1)} %collective-permute-done.34.sec_b.rest_1_, ...), custom_call_target="tpu_custom_call" | custom-call | flops 2013265920 | bytes 8388608 | tf_op jit(solution)/shard_map/mlp_block/pallas_call | solution.py:305
  187.2 6.2 %mlp_block.7 = (bf16[512,384]{1,0:T(8,128)(2,1)}, bf16[512,384]{1,0:T(8,128)(2,1)}, bf16[512,384]{1,0:T(8,128)(2,1)}, bf16[256,1024]{1,0:T(8,128)(2,1)}, bf16[256,1024]{1,0:T(8,128)(2,1)}) custom-call(bf16[256,1024]{1,0:T(8,128)(2,1)} %collective-permute-done.39.sec_a.rest_6_, bf16[256,1024]{1,0:T(8,128)(2,1)} %collective-permute-done.40.sec_b.rest_7_, ...), custom_call_target="tpu_custom_call" | custom-call | flops 2013265920 | bytes 8388608 | tf_op jit(solution)/shard_map/mlp_block/pallas_call | solution.py:305
  198.3 8.5 %collective-permute-done.57 = bf16[256,1024]{1,0:T(8,128)(2,1)S(1)} collective-permute-done((bf16[256,1024]{1,0:T(8,128)(2,1)S(1)}, bf16[256,1024]{1,0:T(8,128)(2,1)S(1)}, u32[]{:S(2)}, u32[]{:S(2)}) %collective-permute-start.57) | collective-permute-done | bytes 524320 | tf_op jit(solution)/shard_map/ppermute | solution.py:671
  206.8 12.6 %collective-permute-done.59 = bf16[256,1024]{1,0:T(8,128)(2,1)S(1)} collective-permute-done((bf16[256,1024]{1,0:T(8,128)(2,1)S(1)}, bf16[256,1024]{1,0:T(8,128)(2,1)S(1)}, u32[]{:S(2)}, u32[]{:S(2)}) %collective-permute-start.59) | collective-permute-done | bytes 524320 | tf_op jit(solution)/shard_map/ppermute | solution.py:671
  221.5 12.5 %mix_adjoint.1 = (bf16[4,256,384]{2,1,0:T(8,128)(2,1)}, f32[4,2,256,384]{3,2,1,0:T(8,128)}, f32[4,8,384]{2,1,0:T(8,128)}, bf16[4,4,2,128,384]{4,3,2,1,0:T(8,128)(2,1)}, bf16[4,4,2,128,384]{4,3,2,1,0:T(8,128)(2,1)}) custom-call(s32[1]{0:T(128)} %bitcast.me_ref, bf16[256,1024]{1,0:T(8,128)(2,1)} %fusion.31.grad_ref, bf16[256,1024]{1,0:T(8,128)(2,1)} %copy-done.4, ...), custom_call_target="tpu_custom_call" | custom-call | flops 2415919104 | bytes 25165824 | tf_op jit(solution)/shard_map/mix_adjoint/pallas_call | solution.py:439
  240.4 17.7 %mix_back.1 = (bf16[4,4,160,384]{3,2,1,0:T(8,128)(2,1)}, bf16[4,4,160,384]{3,2,1,0:T(8,128)(2,1)}, f32[272,1024]{1,0:T(8,128)}) custom-call(s32[1]{0:T(128)} %bitcast.me_ref, bf16[272,1024]{1,0:T(8,128)(2,1)} %pad_maximum_fusion.3.nx_ref, bf16[4,3,1024,384]{3,2,1,0:T(8,128)(2,1)} %get-tuple-element.103.weight_ref.gate_weight_ref.input_weight_ref, ...), custom_call_target="tpu_custom_call" | custom-call | flops 2415919104 | bytes 25165824 | tf_op jit(solution)/shard_map/mix_back/pallas_call | solution.py:598
  260.7 15.4 %mlp_grads.1 = (bf16[4,8,3,32,384]{4,3,2,1,0:T(8,128)(2,1)}, bf16[256,1024]{1,0:T(8,128)(2,1)}, bf16[256,1024]{1,0:T(8,128)(2,1)}, bf16[256,1024]{1,0:T(8,128)(2...) custom-call(bf16[3,1024,384]{2,1,0:T(8,128)(2,1)} %bitcast.180, ...), custom_call_target="tpu_custom_call" | custom-call | flops 6442450944 | bytes 20971520 | tf_op jit(solution)/shard_map/mlp_grads/pallas_call | solution.py:359
  292.0 9.0 %collective-permute-done.68 = f32[2,1024]{1,0:T(2,128)S(1)} collective-permute-done((f32[2,1024]{1,0:T(2,128)S(1)}, f32[2,1024]{1,0:T(2,128)S(1)}, u32[]{:S(2)}, u32[]{:S(2)}) %collective-permute-start.68) | collective-permute-done | bytes 8224 | tf_op jit(solution)/shard_map/ppermute | solution.py:671
  301.0 14.4 %collective-permute-start.69 = (f32[2,1024]{1,0:T(2,128)S(1)}, f32[2,1024]{1,0:T(2,128)S(1)}, u32[]{:S(2)}, u32[]{:S(2)}) collective-permute-start(f32[2,1024]{1,0:T(2,128)S(1)} %add.247), channel_id=1, source_target_pairs={{0,1},{1,0},{2,3},{3,2},{4,5},{5,4},{6,7},{7,6},{8,9},{9,8},{10,11... | collective-permute-start | bytes 24584 | tf_op jit(solution)/shard_map/ppermute | solution.py:873
  331.1 6.8 %collective-permute-done.54 = bf16[256,1024]{1,0:T(8,128)(2,1)S(1)} collective-permute-done((bf16[256,1024]{1,0:T(8,128)(2,1)S(1)}, bf16[256,1024]{1,0:T(8,128)(2,1)S(1)}, u32[]{:S(2)}, u32[]{:S(2)}) %collective-permute-start.54) | collective-permute-done | bytes 524320 | tf_op jit(solution)/shard_map/ppermute | solution.py:671
  363.5 7.2 %convert_add_fusion = (f32[4,4,2,128,384]{4,3,2,1,0:T(8,128)}, bf16[4,4,2,128,384]{4,3,2,1,0:T(8,128)(2,1)S(1)}) fusion(bf16[4,4,2,128,384]{4,3,2,1,0:T(8,128)(2,1)} %collective-permute-done.71, bf16[4,4,2,128,384]{4,3,2,1,0:T(8,128)(2,1)} %get-tuple-element.143), kind=kLoop, calls=%fused_computation.2 | loop fusion | flops 6291456 | bytes 15728640 | tf_op jit(solution)/shard_map/add | solution.py:835
  384.3 7.1 %collective-permute-done.72 = bf16[4,2,128,384]{3,2,1,0:T(8,128)(2,1)S(1)} collective-permute-done((bf16[4,2,128,384]{3,2,1,0:T(8,128)(2,1)}, bf16[4,2,128,384]{3,2,1,0:T(8,128)(2,1)S(1)}, u32[]{:S(2)}, u32[]{:S(2)}) %collective-permute-start.72) | collective-permute-done | bytes 786464 | tf_op jit(solution)/shard_map/ppermute | solution.py:671
  391.4 16.7 %collective-permute-done.74 = bf16[4,2,128,384]{3,2,1,0:T(8,128)(2,1)} collective-permute-done((bf16[4,2,128,384]{3,2,1,0:T(8,128)(2,1)}, bf16[4,2,128,384]{3,2,1,0:T(8,128)(2,1)}, u32[]{:S(2)}, u32[]{:S(2)}) %collective-permute-start.74) | collective-permute-done | bytes 786464 | tf_op jit(solution)/shard_map/ppermute | solution.py:671
  415.1 10.1 %collective-permute-done.76 = bf16[2,128,384]{2,1,0:T(8,128)(2,1)S(1)} collective-permute-done((bf16[2,128,384]{2,1,0:T(8,128)(2,1)S(1)}, bf16[2,128,384]{2,1,0:T(8,128)(2,1)S(1)}, u32[]{:S(2)}, u32[]{:S(2)}) %collective-permute-start.76) | collective-permute-done | bytes 196640 | tf_op jit(solution)/shard_map/ppermute | solution.py:674
  (456 shorter events, 215.0 us)
Async XLA Ops:
  10.6 34.2 %collective-permute-start.14 = (bf16[3,128,384]{2,1,0:T(8,128)(2,1)S(1)}, bf16[3,128,384]{2,1,0:T(8,128)(2,1)S(1)}, u32[]{:S(2)}, u32[]{:S(2)}) collective-permute-start(bf16[3,128,384]{2,1,0:T(8,128)(2,1)S(1)} %constant_dynamic-slice_fusion), channel_id=1, source_target_pairs={{0,3},{1,0},{2,1},{3,2},{4,7},{5,4},{6,5},{7,6},{8,11},{9,8},{10,9... | collective-permute-start | bytes 884744 | tf_op jit(solution)/shard_map/ppermute | solution.py:674
  17.1 145.4 %all-gather.3.cloned.1.call-start = ((), (), s32[]{:S(2)}) async-start(), calls=%async_computation.4 | async-start | bytes 2949120 | tf_op jit(solution)/shard_map/all_gather | solution.py:751
  25.0 354.9 %reduce-scatter.2.cloned.1.call-start = ((), (), s32[]{:S(2)}) async-start(), calls=%async_computation.3 | async-start | bytes 2949120 | tf_op jit(solution)/shard_map/reduce_scatter | solution.py:793
  48.4 25.7 %collective-permute-start.4 = (bf16[3,128,384]{2,1,0:T(8,128)(2,1)S(1)}, bf16[3,128,384]{2,1,0:T(8,128)(2,1)S(1)}, u32[]{:S(2)}, u32[]{:S(2)}) collective-permute-start(bf16[3,128,384]{2,1,0:T(8,128)(2,1)S(1)} %collective-permute-done.3.rest_0_), channel_id=1, source_target_pairs={{0,1},{1,2},{2,3},{3,0},{4,5},{5,6},{6,7},{7,4},{8,9},{9,10},{10,1... | collective-permute-start | bytes 884744 | tf_op jit(solution)/shard_map/ppermute | solution.py:674
  54.7 21.6 %collective-permute-start.28 = (bf16[3,128,384]{2,1,0:T(8,128)(2,1)S(1)}, bf16[3,128,384]{2,1,0:T(8,128)(2,1)S(1)}, u32[]{:S(2)}, u32[]{:S(2)}) collective-permute-start(bf16[3,128,384]{2,1,0:T(8,128)(2,1)S(1)} %collective-permute-done.27.rest_4_), channel_id=1, source_target_pairs={{0,4},{4,0},{8,12},{12,8},{16,20},{20,16},{24,28},{28,24},{1,5},{5... | collective-permute-start | bytes 884744 | tf_op jit(solution)/shard_map/ppermute | solution.py:671
  79.4 32.8 %collective-permute-start.5 = (bf16[3,128,384]{2,1,0:T(8,128)(2,1)S(1)}, bf16[3,128,384]{2,1,0:T(8,128)(2,1)}, u32[]{:S(2)}, u32[]{:S(2)}) collective-permute-start(bf16[3,128,384]{2,1,0:T(8,128)(2,1)S(1)} %collective-permute-done.4.rest_0_), channel_id=1, source_target_pairs={{0,4},{4,0},{8,12},{12,8},{16,20},{20,16},{24,28},{28,24},{1,5},{5... | collective-permute-start | bytes 884744 | tf_op jit(solution)/shard_map/ppermute | solution.py:671
  84.4 28.5 %collective-permute-start.11 = (bf16[3,128,384]{2,1,0:T(8,128)(2,1)}, bf16[3,128,384]{2,1,0:T(8,128)(2,1)}, u32[]{:S(2)}, u32[]{:S(2)}) collective-permute-start(bf16[3,128,384]{2,1,0:T(8,128)(2,1)} %collective-permute-done.10.rest_6_), channel_id=1, source_target_pairs={{0,4},{4,0},{8,12},{12,8},{16,20},{20,16},{24,28},{28,24},{1,5},{5... | collective-permute-start | bytes 884744 | tf_op jit(solution)/shard_map/ppermute | solution.py:671
  91.0 22.0 %collective-permute-start.7 = (bf16[3,128,384]{2,1,0:T(8,128)(2,1)}, bf16[3,128,384]{2,1,0:T(8,128)(2,1)}, u32[]{:S(2)}, u32[]{:S(2)}) collective-permute-start(bf16[3,128,384]{2,1,0:T(8,128)(2,1)} %collective-permute-done.6.rest_2_), channel_id=1, source_target_pairs={{0,4},{4,0},{8,12},{12,8},{16,20},{20,16},{24,28},{28,24},{1,5},{5... | collective-permute-start | bytes 884744 | tf_op jit(solution)/shard_map/ppermute | solution.py:671
  111.4 23.6 %collective-permute-start.42 = (bf16[256,1024]{1,0:T(8,128)(2,1)S(1)}, bf16[256,1024]{1,0:T(8,128)(2,1)S(1)}, u32[]{:S(2)}, u32[]{:S(2)}) collective-permute-start(bf16[256,1024]{1,0:T(8,128)(2,1)S(1)} %copy-done.7), channel_id=1, source_target_pairs={{0,8},{4,12},{8,0},{12,4},{16,24},{20,28},{24,16},{28,20},{1,9},{5... | collective-permute-start | bytes 1572872 | tf_op jit(solution)/shard_map/ppermute | solution.py:671
  112.2 25.1 %collective-permute-start.44 = (bf16[256,1024]{1,0:T(8,128)(2,1)S(1)}, bf16[256,1024]{1,0:T(8,128)(2,1)S(1)}, u32[]{:S(2)}, u32[]{:S(2)}) collective-permute-start(bf16[256,1024]{1,0:T(8,128)(2,1)S(1)} %copy-done.7), channel_id=1, source_target_pairs={{0,16},{4,20},{8,24},{12,28},{16,0},{20,4},{24,8},{28,12},{1,17},{... | collective-permute-start | bytes 1572872 | tf_op jit(solution)/shard_map/ppermute | solution.py:671
  135.0 26.8 %collective-permute-start.43 = (bf16[256,1024]{1,0:T(8,128)(2,1)S(1)}, bf16[256,1024]{1,0:T(8,128)(2,1)}, u32[]{:S(2)}, u32[]{:S(2)}) collective-permute-start(bf16[256,1024]{1,0:T(8,128)(2,1)S(1)} %collective-permute-done.42.cot_a.rest_10_), channel_id=1, source_target_pairs={{0,4},{4,0},{8,12},{12,8},{16,20},{20,16},{24,28},{28,24},{1,5},{5... | collective-permute-start | bytes 1572872 | tf_op jit(solution)/shard_map/ppermute | solution.py:671
  137.3 24.6 %collective-permute-start.45 = (bf16[256,1024]{1,0:T(8,128)(2,1)S(1)}, bf16[256,1024]{1,0:T(8,128)(2,1)}, u32[]{:S(2)}, u32[]{:S(2)}) collective-permute-start(bf16[256,1024]{1,0:T(8,128)(2,1)S(1)} %collective-permute-done.44.cot_a.rest_12_), channel_id=1, source_target_pairs={{0,4},{4,0},{8,12},{12,8},{16,20},{20,16},{24,28},{28,24},{1,5},{5... | collective-permute-start | bytes 1572872 | tf_op jit(solution)/shard_map/ppermute | solution.py:671
  137.6 28.3 %collective-permute-start.39 = (bf16[256,1024]{1,0:T(8,128)(2,1)}, bf16[256,1024]{1,0:T(8,128)(2,1)}, u32[]{:S(2)}, u32[]{:S(2)}) collective-permute-start(bf16[256,1024]{1,0:T(8,128)(2,1)} %get-tuple-element.106.sec_a.rest_0_), channel_id=1, source_target_pairs={{0,24},{4,28},{8,16},{12,20},{16,8},{20,12},{24,0},{28,4},{1,25},{... | collective-permute-start | bytes 1572872 | tf_op jit(solution)/shard_map/ppermute | solution.py:671
  194.6 24.8 %collective-permute-start.59 = (bf16[256,1024]{1,0:T(8,128)(2,1)S(1)}, bf16[256,1024]{1,0:T(8,128)(2,1)S(1)}, u32[]{:S(2)}, u32[]{:S(2)}) collective-permute-start(bf16[256,1024]{1,0:T(8,128)(2,1)S(1)} %add_convert_fusion.1), channel_id=1, source_target_pairs={{0,16},{4,20},{8,24},{12,28},{16,0},{20,4},{24,8},{28,12},{1,17},{... | collective-permute-start | bytes 1572872 | tf_op jit(solution)/shard_map/ppermute | solution.py:671
  195.7 23.7 %collective-permute-start.61 = (bf16[256,1024]{1,0:T(8,128)(2,1)S(1)}, bf16[256,1024]{1,0:T(8,128)(2,1)S(1)}, u32[]{:S(2)}, u32[]{:S(2)}) collective-permute-start(bf16[256,1024]{1,0:T(8,128)(2,1)S(1)} %add_convert_fusion), channel_id=1, source_target_pairs={{0,24},{4,28},{8,16},{12,20},{16,8},{20,12},{24,0},{28,4},{1,25},{... | collective-permute-start | bytes 1572872 | tf_op jit(solution)/shard_map/ppermute | solution.py:671
  258.1 27.4 %collective-permute-start.85 = (bf16[4,4,160,384]{3,2,1,0:T(8,128)(2,1)}, bf16[4,4,160,384]{3,2,1,0:T(8,128)(2,1)}, u32[]{:S(2)}, u32[]{:S(2)}) collective-permute-start(bf16[4,4,160,384]{3,2,1,0:T(8,128)(2,1)} %get-tuple-element.146), channel_id=1, source_target_pairs={{0,4},{4,0},{8,12},{12,8},{16,20},{20,16},{24,28},{28,24},{1,5},{5... | collective-permute-start | bytes 5898248 | tf_op jit(solution)/shard_map/ppermute | solution.py:671
  276.9 46.1 %collective-permute-start.48 = (bf16[256,1024]{1,0:T(8,128)(2,1)}, bf16[256,1024]{1,0:T(8,128)(2,1)}, u32[]{:S(2)}, u32[]{:S(2)}) collective-permute-start(bf16[256,1024]{1,0:T(8,128)(2,1)} %get-tuple-element.120), channel_id=1, source_target_pairs={{0,4},{4,0},{8,12},{12,8},{16,20},{20,16},{24,28},{28,24},{1,5},{5... | collective-permute-start | bytes 1572872 | tf_op jit(solution)/shard_map/ppermute | solution.py:671
  287.9 29.3 %collective-permute-start.86 = (bf16[4,160,384]{2,1,0:T(8,128)(2,1)S(1)}, bf16[4,160,384]{2,1,0:T(8,128)(2,1)S(1)}, u32[]{:S(2)}, u32[]{:S(2)}) collective-permute-start(bf16[4,160,384]{2,1,0:T(8,128)(2,1)S(1)} %get-tuple-element.173), channel_id=1, source_target_pairs={{0,8},{4,12},{8,0},{12,4},{16,24},{20,28},{24,16},{28,20},{1,9},{5... | collective-permute-start | bytes 1474568 | tf_op jit(solution)/shard_map/ppermute | solution.py:671
  288.6 28.8 %collective-permute-start.87 = (bf16[4,160,384]{2,1,0:T(8,128)(2,1)S(1)}, bf16[4,160,384]{2,1,0:T(8,128)(2,1)S(1)}, u32[]{:S(2)}, u32[]{:S(2)}) collective-permute-start(bf16[4,160,384]{2,1,0:T(8,128)(2,1)S(1)} %get-tuple-element.175), channel_id=1, source_target_pairs={{0,16},{4,20},{8,24},{12,28},{16,0},{20,4},{24,8},{28,12},{1,17},{... | collective-permute-start | bytes 1474568 | tf_op jit(solution)/shard_map/ppermute | solution.py:671
  288.7 31.3 %collective-permute-start.88 = (bf16[4,160,384]{2,1,0:T(8,128)(2,1)S(1)}, bf16[4,160,384]{2,1,0:T(8,128)(2,1)S(1)}, u32[]{:S(2)}, u32[]{:S(2)}) collective-permute-start(bf16[4,160,384]{2,1,0:T(8,128)(2,1)S(1)} %get-tuple-element.174), channel_id=1, source_target_pairs={{0,24},{4,28},{8,16},{12,20},{16,8},{20,12},{24,0},{28,4},{1,25},{... | collective-permute-start | bytes 1474568 | tf_op jit(solution)/shard_map/ppermute | solution.py:671
  320.0 43.5 %collective-permute-start.71 = (bf16[4,4,2,128,384]{4,3,2,1,0:T(8,128)(2,1)}, bf16[4,4,2,128,384]{4,3,2,1,0:T(8,128)(2,1)}, u32[]{:S(2)}, u32[]{:S(2)}) collective-permute-start(bf16[4,4,2,128,384]{4,3,2,1,0:T(8,128)(2,1)} %get-tuple-element.144), channel_id=1, source_target_pairs={{0,4},{4,0},{8,12},{12,8},{16,20},{20,16},{24,28},{28,24},{1,5},{5... | collective-permute-start | bytes 9437192 | tf_op jit(solution)/shard_map/ppermute | solution.py:671
  322.9 21.6 %collective-permute-start.70 = (f32[2,1024]{1,0:T(2,128)S(1)}, f32[2,1024]{1,0:T(2,128)S(1)}, u32[]{:S(2)}, u32[]{:S(2)}) collective-permute-start(f32[2,1024]{1,0:T(2,128)S(1)} %add.248), channel_id=1, source_target_pairs={{0,2},{1,3},{2,0},{3,1},{4,6},{5,7},{6,4},{7,5},{8,10},{9,11},{10,... | collective-permute-start | bytes 24584 | tf_op jit(solution)/shard_map/ppermute | solution.py:873
  373.0 35.1 %collective-permute-start.74 = (bf16[4,2,128,384]{3,2,1,0:T(8,128)(2,1)}, bf16[4,2,128,384]{3,2,1,0:T(8,128)(2,1)}, u32[]{:S(2)}, u32[]{:S(2)}) collective-permute-start(bf16[4,2,128,384]{3,2,1,0:T(8,128)(2,1)} %get-tuple-element.171), channel_id=1, source_target_pairs={{0,24},{4,28},{8,16},{12,20},{16,8},{20,12},{24,0},{28,4},{1,25},{... | collective-permute-start | bytes 2359304 | tf_op jit(solution)/shard_map/ppermute | solution.py:671
  379.8 53.7 %all-to-all-start.1 = ((bf16[8,3,32,384]{3,2,1,0:T(8,128)(2,1)}), bf16[8,3,32,384]{3,2,1,0:T(8,128)(2,1)S(1)}, u32[]{:S(2)}, u32[]{:S(2)}) async-start(bf16[8,3,32,384]{3,2,1,0:T(8,128)(2,1)} %bitcast.192), calls=%async_computation.2 | async-start | bytes 1179648 | tf_op jit(solution)/shard_map/all_to_all | solution.py:794
  (152 other events, 2274.4 us)
Sparse Core Ops, SparseCore 0:
  25.1 59.4 all-gather.2
  277.4 47.1 reduce-scatter.1

commit v2 on v1

v2 whole, which is shorter than its diff:
```python
import functools

import jax
import jax.numpy as jnp
from jax import lax
from jax.experimental import pallas as pl
from jax.experimental.pallas import tpu as pltpu
from jax.sharding import PartitionSpec as P

LENGTH = 1024
EPS = 1e-06
STRENGTH = 8.0
HALO = 16
TABLE = 256
COST = 0.3
GELU_A = 0.7978845608028654
GELU_B = 0.044715
BF16 = jnp.bfloat16
F32 = jnp.float32
MIB = 1024 * 1024


def mm(left, right, left_dim, right_dim):
    return lax.dot_general(
        left, right, (((left_dim,), (right_dim,)), ((), ())), preferred_element_type=F32
    )


def gelu_parts(value):
    square = value * value
    th = jnp.tanh(GELU_A * value * (1.0 + GELU_B * square))
    half = 0.5 * (1.0 + th)
    slope = half + 0.5 * value * (1.0 - th * th) * (GELU_A * (1.0 + 3.0 * GELU_B * square))
    return value * half, slope


def gelu(value):
    th = jnp.tanh(GELU_A * value * (1.0 + GELU_B * value * value))
    return 0.5 * value * (1.0 + th)


def one_minus_exp(v):
    series = v * (
        1.0
        - v
        * (1 / 2)
        * (
            1.0
            - v
            * (1 / 3)
            * (1.0 - v * (1 / 4) * (1.0 - v * (1 / 5) * (1.0 - v * (1 / 6) * (1.0 - v * (1 / 7)))))
        )
    )
    return jnp.where(v < 0.4, series, 1.0 - jnp.exp(-v))


def rows_index(shape):
    return lax.broadcasted_iota(jnp.int32, shape, 0)


def scan_down(a, b):
    count = a.shape[0]
    index = rows_index(a.shape)
    step = 1
    while step < count:
        if step < 8:
            inside = index >= step
            a_prev = jnp.where(inside, pltpu.roll(a, step, 0), 1.0)
            b_prev = jnp.where(inside, pltpu.roll(b, step, 0), 0.0)
        else:
            a_prev = jnp.concatenate([jnp.ones_like(a[:step]), a[: count - step]], axis=0)
            b_prev = jnp.concatenate([jnp.zeros_like(b[:step]), b[: count - step]], axis=0)
        b = b + a * b_prev
        a = a * a_prev
        step *= 2
    return a, b


def scan_up(a, b):
    count = a.shape[0]
    index = rows_index(a.shape)
    step = 1
    while step < count:
        if step < 8:
            inside = index < count - step
            a_next = jnp.where(inside, pltpu.roll(a, count - step, 0), 1.0)
            b_next = jnp.where(inside, pltpu.roll(b, count - step, 0), 0.0)
        else:
            a_next = jnp.concatenate([a[step:], jnp.ones_like(a[:step])], axis=0)
            b_next = jnp.concatenate([b[step:], jnp.zeros_like(b[:step])], axis=0)
        b = b + a * b_next
        a = a * a_next
        step *= 2
    return a, b


def block_diagonal(flat, head, dtype):
    width = flat.shape[1]
    tall = jnp.concatenate([flat] * (width // head), axis=0)
    shape = (width, width)
    row = lax.broadcasted_iota(jnp.int32, shape, 0) // head
    col = lax.broadcasted_iota(jnp.int32, shape, 1) // head
    return jnp.where(row == col, tall, 0.0).astype(dtype)


def fold_diagonal(square, head):
    width = square.shape[0]
    row = lax.broadcasted_iota(jnp.int32, square.shape, 0) // head
    col = lax.broadcasted_iota(jnp.int32, square.shape, 1) // head
    kept = jnp.where(row == col, square, 0.0)
    total = kept[:head]
    for start in range(head, width, head):
        total = total + kept[start : start + head]
    return total


def vmem():
    return pl.BlockSpec(memory_space=pltpu.VMEM)


def smem():
    return pl.BlockSpec(memory_space=pltpu.SMEM)


def launch(
    kernel,
    inputs,
    in_specs,
    micros,
    after=(),
    carry=(),
    prefetch=0,
    grid=(),
    out_shape=(),
    out_specs=(),
    scratch_shapes=(),
    aliases=None,
    name=None,
    vmem_mib=60,
):
    count, extra, through = len(inputs), len(after), len(carry)
    made = len(out_shape)
    aliases = dict(aliases or {})
    for i in range(through):
        aliases[count + extra + i] = made + i

    def body(*refs):
        first = count + extra + through
        kernel(*refs[:count], *refs[first : first + made], *refs[first + made + through :])

    anywhere = pl.BlockSpec(memory_space=pl.ANY)
    return pl.pallas_call(
        body,
        out_shape=list(out_shape) + [jax.ShapeDtypeStruct(c.shape, c.dtype) for c in carry],
        grid_spec=pltpu.PrefetchScalarGridSpec(
            num_scalar_prefetch=prefetch,
            grid=grid,
            in_specs=list(in_specs) + [anywhere] * (extra + through),
            out_specs=list(out_specs) + [anywhere] * through,
            scratch_shapes=scratch_shapes,
        ),
        input_output_aliases=aliases,
        compiler_params=pltpu.CompilerParams(vmem_limit_bytes=vmem_mib * MIB),
        cost_estimate=pl.CostEstimate(
            flops=int(micros * 1.1e9 * COST), bytes_accessed=int(micros * 3.5e6 * COST), transcendentals=0
        ),
        name=name,
    )(*inputs, *after, *carry)


def split_features(core, source, own_out, other_out):
    half = own_out.shape[1]
    block = 128
    quads = half // block
    for quad in range(quads):
        for out, who in ((own_out, core), (other_out, 1 - core)):
            start = pl.multiple_of((quad * 2 + who) * block, block)
            out[:, quad * block : (quad + 1) * block] = source[:, pl.ds(start, block)]


def pack_kernel(*refs):
    *pieces, out = refs
    for i, ref in enumerate(pieces):
        out[i] = ref[0]


def pack(pieces, carry, after):
    return launch(
        pack_kernel,
        pieces,
        [vmem()] * len(pieces),
        0.1,
        after,
        carry,
        out_shape=[jax.ShapeDtypeStruct((len(pieces),) + pieces[0].shape[1:], pieces[0].dtype)],
        out_specs=[vmem()],
        name="pack",
        vmem_mib=8,
    )


def fence(carry, after=()):
    return launch(lambda *refs: None, [], [], 0.01, after, carry, name="fence", vmem_mib=1)


def prepare_kernel(
    slots_ref,
    gate_ref,
    input_ref,
    out_ref,
    recall_ref,
    recall_bias_ref,
    admit_ref,
    admit_bias_ref,
    taps_ref,
    bias_ref,
    decay_ref,
    weights,
    table_out,
    pieces_out,
    table,
):
    weights[0] = gate_ref[...]
    weights[1] = input_ref[...]
    weights[2] = out_ref[...].T
    heads, head, _ = recall_ref.shape
    for h in range(heads):
        cols = slice(h * head, (h + 1) * head)
        table[:head, cols] = recall_ref[h]
        table[head : 2 * head, cols] = admit_ref[h]
    side = jnp.concatenate
    lines = side(
        [
            taps_ref[...],
            bias_ref[...].reshape(1, -1),
            side([recall_bias_ref[h : h + 1] for h in range(heads)], axis=1),
            side([admit_bias_ref[h : h + 1] for h in range(heads)], axis=1),
            jax.nn.softplus(-decay_ref[...].reshape(1, -1)),
        ],
        axis=0,
    )
    high = lines.astype(BF16).astype(F32)
    rest = lines - high
    mid = rest.astype(BF16).astype(F32)
    table[2 * head : 2 * head + 8] = high
    table[2 * head + 8 : 2 * head + 16] = mid
    table[2 * head + 16 : 2 * head + 24] = rest - mid
    table[2 * head + 24 :] = jnp.zeros((table.shape[0] - 2 * head - 24, table.shape[1]), F32)
    table_out[...] = table[...].astype(BF16)
    count, rows, _ = pieces_out.shape
    block = pieces_block(weights.shape[1], rows)
    extra = rows - 3 * block
    for k in range(count):
        start = pl.multiple_of(slots_ref[k] * block, block)
        for part in range(3):
            pieces_out[k, part * block : (part + 1) * block] = weights[part, pl.ds(start, block), :]
        start = pl.multiple_of(slots_ref[k] * extra, extra)
        pieces_out[k, 3 * block :] = table_out[pl.ds(start, extra), :]

def norm_kernel(core_ref, ends_ref, tokens_ref, gain_ref, normed_out, *halves_out):
    for ref, rows in ((ends_ref, slice(0, HALO)), (tokens_ref, slice(HALO, None))):
        values = ref[...].astype(F32)
        scale = lax.rsqrt(jnp.mean(values * values, axis=1, keepdims=True) + EPS)
        normed_out[rows] = (values * scale * gain_ref[...]).astype(BF16)
    if halves_out:
        split_features(core_ref[0], normed_out, *halves_out)


def norm(core, ends, tokens, gain, group):
    count, model = tokens.shape
    halves = half_shapes(HALO + count, model, group)
    return launch(
        norm_kernel,
        [core, ends, tokens, gain.reshape(1, model)],
        [smem()] + [vmem()] * 3,
        0.1,
        out_shape=[jax.ShapeDtypeStruct((HALO + count, model), BF16)] + halves,
        out_specs=[vmem()] * (1 + len(halves)),
        name="norm",
        vmem_mib=16,
    )


def pieces_block(model, rows):
    return rows * model // (3 * model + TABLE)


def half_shapes(rows, model, group):
    return [jax.ShapeDtypeStruct((rows, model // 2), BF16)] * (2 if model // group == 128 else 0)


def prepare(slots, gate, inputs, out, recall, recall_bias, admit, admit_bias, taps, bias, decay, group):
    model, width = gate.shape
    rows = (3 * model + TABLE) // group
    return launch(
        prepare_kernel,
        [slots, gate, inputs, out, recall, recall_bias, admit, admit_bias, taps, bias, decay],
        [smem()] + [vmem()] * 10,
        0.1,
        out_shape=[
            jax.ShapeDtypeStruct((3, model, width), BF16),
            jax.ShapeDtypeStruct((TABLE, width), BF16),
            jax.ShapeDtypeStruct((slots.shape[0], rows, width), BF16),
        ],
        out_specs=[vmem()] * 3,
        scratch_shapes=[pltpu.VMEM((TABLE, width), F32)],
        name="prepare",
    )


def mix_local_kernel(own, head, counts, stacked, slots_ref, normed_ref, mask_ref, *rest):
    piece_refs, rest = rest[: len(counts)], rest[len(counts) :]
    weights, inputs_out, gated_out, kept_out, scan_out, edge_out, gates_out, vec_out = rest[
        stacked : stacked + 8
    ]
    (table,) = rest[stacked + 8 :]
    model = normed_ref.shape[1]
    if own:
        weights[0] = piece_refs[0][...]
        table[...] = piece_refs[1][...].astype(F32)
    else:
        number = 0
        for ref, many in zip(piece_refs, counts, strict=True):
            rows = ref.shape[1]
            block = pieces_block(model, rows)
            extra = rows - 3 * block
            for k in range(many):
                slot = slots_ref[number]
                number += 1
                start = pl.multiple_of(slot * block, block)
                for part in range(3):
                    weights[0, part, pl.ds(start, block), :] = ref[
                        k, part * block : (part + 1) * block
                    ]
                start = pl.multiple_of(slot * extra, extra)
                table[pl.ds(start, extra), :] = ref[k, 3 * block :].astype(F32)
    count = mask_ref.shape[0]
    vec = table[2 * head : 2 * head + 8] + (
        table[2 * head + 8 : 2 * head + 16] + table[2 * head + 16 : 2 * head + 24]
    )
    vec_out[0] = vec
    gates_out[0] = table[: 2 * head].astype(BF16)
    gated = mm(normed_ref[HALO:], weights[0, 0], 1, 0).astype(BF16)
    gated_out[0] = gated
    inputs = mm(normed_ref[...], weights[0, 1], 1, 0).astype(BF16)
    inputs_out[0] = inputs
    wide = inputs.astype(F32)
    conv = vec[4:5] + vec[0:1] * wide[HALO:]
    for shift in range(1, 4):
        moved = pltpu.roll(wide, shift, 0)[HALO:]
        conv = conv + vec[shift : shift + 1] * (moved * mask_ref[:, shift : shift + 1])
    low = conv.astype(BF16)
    recall_weight = block_diagonal(table[:head], head, BF16)
    admit_weight = block_diagonal(table[head : 2 * head], head, BF16)
    recall = jax.nn.sigmoid(mm(low, recall_weight, 1, 0) + vec[5:6])
    admit = jax.nn.sigmoid(mm(low, admit_weight, 1, 0) + vec[6:7])
    rate = STRENGTH * recall * vec[7:8]
    decay = jnp.exp(-rate)
    inject = jnp.sqrt(one_minus_exp(2.0 * rate)) * admit * conv
    product, state = scan_down(decay * mask_ref[:, 1:2], inject)
    kept_out[0, 0] = conv
    kept_out[0, 1] = recall
    kept_out[0, 2] = admit
    scan_out[0, 0] = product
    scan_out[0, 1] = state
    edge_out[0, 0:1] = product[count - 1 :]
    edge_out[0, 1:2] = state[count - 1 :]
    edge_out[0, 2:3] = jnp.sum(decay, axis=0, keepdims=True)


def mix_local(shard, shards, head, slots, normed, mask, pieces, stacks, after=(), carry=()):
    count = mask.shape[0]
    model = normed.shape[1]
    width = pieces[0].shape[-1]
    own = shard == 0
    counts = [p.shape[0] for p in pieces]
    shapes = [
        ((shards, 3, model, width), BF16),
        ((shards, count + HALO, width), BF16),
        ((shards, count, width), BF16),
        ((shards, 3, count, width), F32),
        ((shards, 2, count, width), F32),
        ((shards, 8, width), F32),
        ((shards, 2 * head, width), BF16),
        ((shards, 8, width), F32),
    ]

    def at(shape):
        tail = (0,) * (len(shape) - 1)
        return pl.BlockSpec((1,) + shape[1:], lambda i: (shard,) + tail)

    first = [slots, normed, mask, *pieces]
    in_specs = [smem()] + [vmem()] * (len(first) - 1)
    aliases = {}
    if stacks is not None:
        aliases = {len(first) + i: i for i in range(len(stacks))}
        in_specs += [pl.BlockSpec(memory_space=pl.ANY)] * len(stacks)
        first += list(stacks)
    outs = launch(
        functools.partial(mix_local_kernel, own, head, counts, len(aliases)),
        first,
        in_specs,
        5.7,
        after=after,
        carry=carry,
        grid=(1,),
        out_shape=[jax.ShapeDtypeStruct(shape, dtype) for shape, dtype in shapes],
        out_specs=[at(shape) for shape, _ in shapes],
        scratch_shapes=[pltpu.VMEM((TABLE, width), F32)],
        aliases=aliases,
        name="mix_local",
    )
    return outs[:8], outs[8:]


def carried(edges):
    total = edges[-1][0, 1:2]
    for edge in edges[-2::-1]:
        total = edge[0, 1:2] + edge[0, 0:1] * total
    return total


def branch_kernel(
    depth, scan_ref, gated_ref, weight_ref, resid_ref, gain_ref, *rest
):
    edges = rest[:depth]
    carry_out, branch_in_out, middle_out, second_out, again_out, acc = rest[depth:]
    step = pl.program_id(0)

    @pl.when(step == 0)
    def _():
        acc[...] = resid_ref[...].astype(F32)

    carry = carried(edges)
    carry_out[0] = jnp.broadcast_to(carry, carry_out.shape[1:])
    state = scan_ref[0, 1] + scan_ref[0, 0] * carry
    mixed = (gelu(gated_ref[0].astype(F32)) * state).astype(BF16)
    branch_in_out[0] = mixed
    acc[...] += mm(mixed, weight_ref[0, 0], 1, 1)

    @pl.when(step == pl.num_programs(0) - 1)
    def _():
        middle = acc[...]
        middle_out[...] = middle
        scale = lax.rsqrt(jnp.mean(middle * middle, axis=1, keepdims=True) + EPS)
        second = (middle * scale * gain_ref[...]).astype(BF16)
        second_out[...] = second
        again_out[...] = second


def branch(scan, gated, weights, tokens, gain, edges, after):
    shards, _, count, width = scan.shape
    model = tokens.shape[1]

    def edge_spec(shift):
        return pl.BlockSpec((1, 8, width), lambda s: ((s + shards - shift % shards) % shards, 0, 0))

    return launch(
        functools.partial(branch_kernel, len(edges)),
        [scan, gated, weights, tokens, gain, *edges],
        [
            pl.BlockSpec((1, 2, count, width), lambda s: (s, 0, 0, 0)),
            pl.BlockSpec((1, count, width), lambda s: (s, 0, 0)),
            pl.BlockSpec((1, 1, model, width), lambda s: (s, 2, 0, 0)),
            pl.BlockSpec((count, model), lambda s: (0, 0)),
            pl.BlockSpec((1, model), lambda s: (0, 0)),
        ]
        + [edge_spec(i + 1) for i in range(len(edges))],
        0.1,
        after,
        grid=(shards,),
        out_shape=[
            jax.ShapeDtypeStruct((shards, 8, width), F32),
            jax.ShapeDtypeStruct((shards, count, width), BF16),
            jax.ShapeDtypeStruct((count, model), F32),
            jax.ShapeDtypeStruct((count, model), BF16),
            jax.ShapeDtypeStruct((count, model), BF16),
        ],
        out_specs=[
            pl.BlockSpec((1, 8, width), lambda s: (s, 0, 0)),
            pl.BlockSpec((1, count, width), lambda s: (s, 0, 0)),
            pl.BlockSpec((count, model), lambda s: (0, 0)),
            pl.BlockSpec((count, model), lambda s: (0, 0)),
            pl.BlockSpec((count, model), lambda s: (0, 0)),
        ],
        scratch_shapes=[pltpu.VMEM((count, model), F32)],
        name="mix_branch",
    )


def arrange_kernel(core_ref, own_ref, other_ref, out_ref):
    shards, quads, _, piece, _ = own_ref.shape
    for ref, core in ((own_ref, core_ref[0]), (other_ref, 1 - core_ref[0])):
        for shard in range(shards):
            for quad in range(quads):
                start = pl.multiple_of(((quad * 2 + core) * shards + shard) * piece, piece)
                for part in range(3):
                    out_ref[part, pl.ds(start, piece), :] = ref[shard, quad, part]


def arrange(core, own, other, after):
    shards, quads, _, piece, width = own.shape
    if piece % 16:
        both = jnp.where(core[0] == 0, jnp.stack([own, other]), jnp.stack([other, own]))
        return both.transpose(3, 2, 0, 1, 4, 5).reshape(3, 2 * shards * quads * piece, width)
    return launch(
        arrange_kernel,
        [core, own, other],
        [smem(), vmem(), vmem()],
        0.1,
        after,
        out_shape=[jax.ShapeDtypeStruct((3, 2 * shards * quads * piece, width), BF16)],
        out_specs=[vmem()],
        name="mlp_arrange",
        vmem_mib=16,
    )[0]


def mlp_tiles(width):
    tile = 256 if width % 256 == 0 else width
    return [slice(start, start + tile) for start in range(0, width, tile)]


def mlp_kernel(
    second_ref,
    cot_ref,
    weight_ref,
    gate_grad_out,
    up_grad_out,
    hidden_out,
    back_out,
):
    second = second_ref[...]
    cot = cot_ref[...]
    total = None
    for cols in mlp_tiles(weight_ref.shape[2]):
        gate_weight, up_weight = weight_ref[0, :, cols], weight_ref[1, :, cols]
        gate = mm(second, gate_weight, 1, 0)
        upward = mm(second, up_weight, 1, 0)
        hidden_grad = mm(cot, weight_ref[2, :, cols], 1, 0)
        act, slope = gelu_parts(gate)
        hidden_out[:, cols] = (act * upward).astype(BF16)
        gate_grad = (hidden_grad * upward * slope).astype(BF16)
        up_grad = (hidden_grad * act).astype(BF16)
        gate_grad_out[:, cols] = gate_grad
        up_grad_out[:, cols] = up_grad
        back = mm(gate_grad, gate_weight, 1, 1) + mm(up_grad, up_weight, 1, 1)
        total = back if total is None else total + back
    back_out[...] = total.astype(BF16)


def mlp_block(second, cot, weights, after, carry):
    count, model = second.shape
    width = weights.shape[-1]
    wide = jax.ShapeDtypeStruct((count, width), BF16)
    return launch(
        mlp_kernel,
        [second, cot, weights],
        [vmem()] * 3,
        7.4,
        after,
        carry,
        out_shape=[wide, wide, wide, jax.ShapeDtypeStruct((count, model), BF16)],
        out_specs=[vmem()] * 4,
        name="mlp_block",
        vmem_mib=16,
    )


def mlp_grads_kernel(quads, quad_ref, core_ref, weight_ref, *rest):
    cots, rest = rest[:quads], rest[quads:]
    seconds, rest = rest[:quads], rest[quads:]
    gate_grads, rest = rest[:quads], rest[quads:]
    up_grads, rest = rest[:quads], rest[quads:]
    hiddens, rest = rest[:quads], rest[quads:]
    *grads_out, results_out, second, cot, left, whole_ref = rest
    count = seconds[0].shape[0]
    rows = [slice(rel * count, (rel + 1) * count) for rel in range(quads)]
    for rel in range(quads):
        second[rows[rel]] = seconds[rel][...]
        cot[rows[rel]] = cots[rel][...]
    total = None
    for cols in mlp_tiles(weight_ref.shape[2]):
        for part, (base, group) in enumerate(
            ((second, gate_grads), (second, up_grads), (cot, hiddens))
        ):
            for rel in range(quads):
                left[rows[rel]] = group[rel][:, cols]
            whole = mm(base[...], left[...], 0, 0).astype(BF16)
            if len(grads_out) == 1:
                grads_out[0][part, :, cols] = whole
                continue
            whole_ref[...] = whole
            shards, _, _, piece, _ = grads_out[0].shape
            for out, core in zip(grads_out, (core_ref[0], 1 - core_ref[0]), strict=True):
                for shard in range(shards):
                    for quad in range(quads):
                        start = pl.multiple_of(((quad * 2 + core) * shards + shard) * piece, piece)
                        out[shard, quad, part, :, cols] = whole_ref[pl.ds(start, piece), :]
        result = mm(left[...], weight_ref[2, :, cols], 1, 1)
        total = result if total is None else total + result
    for rel in range(quads):
        results_out[quad_ref[0] ^ rel] = total[rows[rel]].astype(BF16)


def mlp_grads(quad, core, weights, cots, seconds, gate_grads, up_grads, hiddens, shards):
    quads = len(seconds)
    count, model = seconds[0].shape
    width = weights.shape[2]
    tile = mlp_tiles(width)[0].stop
    piece = model // (quads * 2 * shards)
    shapes = [(shards, quads, 3, piece, width)] * 2 if piece % 16 == 0 else [(3, model, width)]
    *grads, results = launch(
        functools.partial(mlp_grads_kernel, quads),
        [quad, core, weights, *cots, *seconds, *gate_grads, *up_grads, *hiddens],
        [smem()] * 2 + [vmem()] * (1 + 5 * quads),
        15.0,
        out_shape=[jax.ShapeDtypeStruct(shape, BF16) for shape in shapes]
        + [jax.ShapeDtypeStruct((quads, count, model), BF16)],
        out_specs=[vmem()] * (1 + len(shapes)),
        scratch_shapes=[
            pltpu.VMEM((quads * count, model), BF16),
            pltpu.VMEM((quads * count, model), BF16),
            pltpu.VMEM((quads * count, tile), BF16),
            pltpu.VMEM((model, tile), BF16),
        ],
        name="mlp_grads",
        vmem_mib=32,
    )
    if piece % 16:
        both = grads[0].reshape(3, quads, 2, shards, piece, width).transpose(2, 3, 1, 0, 4, 5)
        grads = [lax.dynamic_index_in_dim(both, who, 0, False) for who in (core[0], 1 - core[0])]
    return *grads, results


def add_kernel(a_ref, b_ref, out_ref):
    out_ref[...] = (a_ref[...].astype(F32) + b_ref[...].astype(F32)).astype(BF16)


def add_pair(a, b, after=()):
    return launch(
        add_kernel,
        [a, b],
        [vmem()] * 2,
        0.1,
        after,
        out_shape=[jax.ShapeDtypeStruct(a.shape, BF16)],
        out_specs=[vmem()],
        name="add_pair",
        vmem_mib=16,
    )[0]


def middle_kernel(blocks, back_ref, *rest):
    (*backs, values_ref, cot_ref, gain_ref, core_ref), outs = rest[: blocks + 3], rest[blocks + 3 :]
    middle_grad_out, low_out, gain_out, *halves_out = outs
    grad = back_ref[...].astype(F32)
    for ref in backs:
        grad = grad + ref[...].astype(F32)
    values = values_ref[...]
    scale = lax.rsqrt(jnp.mean(values * values, axis=1, keepdims=True) + EPS)
    scaled = grad * gain_ref[...]
    inner = jnp.mean(scaled * values, axis=1, keepdims=True)
    total = cot_ref[...].astype(F32) + scale * scaled - values * (scale * scale * scale * inner)
    middle_grad_out[...] = total
    low_out[...] = total.astype(BF16)
    if halves_out:
        split_features(core_ref[0], low_out, *halves_out)
    gain_out[...] = jnp.sum(grad * values * scale, axis=0, keepdims=True)


def middle_back(backs, values, cot, gain, core, group, after, carry):
    count, model = values.shape
    halves = half_shapes(count, model, group)
    return launch(
        functools.partial(middle_kernel, len(backs)),
        [*backs, values, cot, gain.reshape(1, model), core],
        [vmem()] * (len(backs) + 3) + [smem()],
        0.1,
        after,
        carry,
        out_shape=[
            jax.ShapeDtypeStruct((count, model), F32),
            jax.ShapeDtypeStruct((count, model), BF16),
            jax.ShapeDtypeStruct((1, model), F32),
        ]
        + halves,
        out_specs=[vmem()] * (3 + len(halves)),
        name="middle_back",
        vmem_mib=16,
    )


def tokens_kernel(
    inside_ref, grad_ref, halo_ref, tokens_ref, gain_ref, middle_grad_ref, gain_two_ref, out, lines_out
):
    grad = grad_ref[HALO:]
    count = grad.shape[0]
    last = jnp.where(inside_ref[0] > 0, halo_ref[...].astype(F32), 0.0)
    grad = jnp.concatenate([grad[: count - HALO], grad[count - HALO :] + last], axis=0)
    values = tokens_ref[...].astype(F32)
    scale = lax.rsqrt(jnp.mean(values * values, axis=1, keepdims=True) + EPS)
    scaled = grad * gain_ref[...]
    inner = jnp.mean(scaled * values, axis=1, keepdims=True)
    out[...] = middle_grad_ref[...] + scale * scaled - values * (scale * scale * scale * inner)
    both = (jnp.sum(grad * values * scale, axis=0, keepdims=True), gain_two_ref[...])
    lines_out[...] = pack_gains(both, lines_out.shape[1])


def gain_chunk(model, width):
    chunk = 128
    while chunk * 2 <= width:
        chunk *= 2
    while chunk > width:
        chunk //= 2
    return chunk


def gain_lines(model, width):
    return 4 * (model // gain_chunk(model, width))


def pack_gains(both, width):
    chunk = gain_chunk(both[0].shape[1], width)
    lines = []
    for value in both:
        high = value.astype(BF16).astype(F32)
        for term in (high, value - high):
            lines += [term[:, i : i + chunk] for i in range(0, term.shape[1], chunk)]
    lines = jnp.concatenate(lines, axis=0)
    if chunk < width:
        blank = jnp.zeros((lines.shape[0], width - chunk), F32)
        lines = jnp.concatenate([lines, blank], axis=1)
    return lines.astype(BF16)


def unpack_gains(lines, model):
    chunk = gain_chunk(model, lines.shape[1])
    many = model // chunk
    lines = lines.astype(F32)
    both = []
    for i in range(2):
        value = lines[2 * i * many : (2 * i + 1) * many] + lines[
            (2 * i + 1) * many : (2 * i + 2) * many
        ]
        both.append(
            jnp.concatenate([value[j : j + 1, :chunk] for j in range(many)], axis=1)
        )
    return both


def tokens_back(inside, grad, halo, tokens, gain, middle_grad, gain_two, width):
    count, model = tokens.shape
    return launch(
        tokens_kernel,
        [inside, grad, halo, tokens, gain.reshape(1, model), middle_grad, gain_two],
        [smem()] + [vmem()] * 6,
        0.1,
        out_shape=[
            jax.ShapeDtypeStruct((count, model), F32),
            jax.ShapeDtypeStruct((gain_lines(model, width), width), BF16),
        ],
        out_specs=[vmem()] * 2,
        name="tokens_back",
        vmem_mib=16,
    )


def adjoint_kernel(
    grad_ref,
    weight_ref,
    gated_ref,
    scan_ref,
    kept_ref,
    carry_ref,
    mask_ref,
    vec_ref,
    gate_back_out,
    adjoint_out,
    edge_out,
):
    into = mm(grad_ref[...], weight_ref[0, 0], 1, 0).astype(BF16).astype(F32)
    act, slope = gelu_parts(gated_ref[0].astype(F32))
    state = scan_ref[0, 1] + scan_ref[0, 0] * carry_ref[0, 0:1]
    gate_back_out[0] = (into * state * slope).astype(BF16)
    decay = jnp.exp(-STRENGTH * kept_ref[0, 0] * vec_ref[0, 7:8]) * mask_ref[:, 1:2]
    count = decay.shape[0]
    shifted = jnp.where(
        rows_index(decay.shape) < count - 1, pltpu.roll(decay, count - 1, 0), 1.0
    )
    product, value = scan_up(shifted, into * act)
    adjoint_out[0, 0] = product
    adjoint_out[0, 1] = value
    edge_out[0] = jnp.broadcast_to(decay[0:1] * value[0:1], edge_out.shape[1:])


def adjoint(grad, weights, gated, scan, kept, carry, mask, vec, through):
    shards, _, count, width = scan.shape
    model = grad.shape[1]

    def flat(*shape):
        return pl.BlockSpec(shape, lambda s: (0,) * len(shape))

    def at(*shape):
        return pl.BlockSpec((1,) + shape, lambda s: (s,) + (0,) * len(shape))

    return launch(
        adjoint_kernel,
        [grad, weights, gated, scan, kept, carry, mask, vec],
        [
            flat(count, model),
            pl.BlockSpec((1, 1, model, width), lambda s: (s, 2, 0, 0)),
            at(count, width),
            at(2, count, width),
            pl.BlockSpec((1, 1, count, width), lambda s: (s, 1, 0, 0)),
            at(8, width),
            flat(*mask.shape),
            at(8, width),
        ],
        0.1,
        carry=through,
        grid=(shards,),
        out_shape=[
            jax.ShapeDtypeStruct((shards, count, width), BF16),
            jax.ShapeDtypeStruct((shards, 2, count, width), F32),
            jax.ShapeDtypeStruct((shards, 8, width), F32),
        ],
        out_specs=[at(count, width), at(2, count, width), at(8, width)],
        name="mix_adjoint",
    )


def outer_kernel(groups, core_ref, *rest):
    pairs, rest = rest[: 4 * groups], rest[4 * groups :]
    *smalls, out, left, right, small = rest
    count = pairs[0].shape[0]
    quads, shards = out.shape[:2]
    block = left.shape[1] // quads
    for group in range(groups):
        left_ref, left_other, right_ref, right_other = pairs[4 * group : 4 * group + 4]
        left[:count] = left_ref[...]
        left[count:] = left_other[...]
        for s in range(shards):
            right[:count] = right_ref[s]
            right[count:] = right_other[s]
            total = mm(left[...], right[...], 0, 0).astype(BF16)
            for quad in range(quads):
                out[quad, s, group * block : (group + 1) * block] = total[
                    quad * block : (quad + 1) * block
                ]
    if smalls:
        extra = out.shape[2] - groups * block
        for s in range(shards):
            small[...] = (smalls[0][s].astype(F32) + smalls[1][s].astype(F32)).astype(BF16)
            for quad in range(quads):
                start = pl.multiple_of((quad * 2 + core_ref[0]) * extra, extra)
                out[quad, s, groups * block :] = small[pl.ds(start, extra), :]


def outer(core, quads, pairs, smalls=(), after=(), carry=()):
    shards, count, width = pairs[2].shape
    model = pairs[0].shape[1]
    groups = len(pairs) // 4
    rows = groups * model // quads + (TABLE // (2 * quads) if smalls else 0)
    return launch(
        functools.partial(outer_kernel, groups),
        [core, *pairs, *smalls],
        [smem()] + [vmem()] * (len(pairs) + len(smalls)),
        0.1,
        after,
        carry,
        out_shape=[jax.ShapeDtypeStruct((quads, shards, rows, width), BF16)],
        out_specs=[vmem()],
        scratch_shapes=[
            pltpu.VMEM((2 * count, model), BF16),
            pltpu.VMEM((2 * count, width), BF16),
            pltpu.VMEM((TABLE, width), BF16),
        ],
        name="mix_outer",
        vmem_mib=16,
    )


def mix_back_kernel(
    head,
    depth,
    gate_weight_ref,
    input_weight_ref,
    inputs_ref,
    gate_back_ref,
    kept_ref,
    scan_ref,
    adjoint_ref,
    carry_ref,
    mask_ref,
    gates_ref,
    vec_ref,
    edge_ref,
    *rest,
):
    backs, decays = rest[:depth], rest[depth : 2 * depth - 1]
    input_back_out, small_out, normed_grad_out, acc = rest[2 * depth - 1 :]
    step = pl.program_id(0)
    count = mask_ref.shape[0]
    width = vec_ref.shape[2]
    vec = vec_ref[0]
    incoming = backs[-1][0, 0:1]
    for back, edge in zip(backs[-2::-1], decays[::-1], strict=True):
        incoming = back[0, 0:1] + edge[0, 0:1] * incoming
    adj = adjoint_ref[0, 1] + adjoint_ref[0, 0] * incoming
    carry = carry_ref[0, 0:1]
    state = scan_ref[0, 1] + scan_ref[0, 0] * carry
    before = jnp.where(rows_index(state.shape) == 0, carry, pltpu.roll(state, 1, 0))
    conv, recall, admit = kept_ref[0, 0], kept_ref[0, 1], kept_ref[0, 2]
    speed = STRENGTH * vec[7:8]
    rate = recall * speed
    decay = jnp.exp(-rate)
    size = jnp.sqrt(one_minus_exp(2.0 * rate))
    sized = adj * size
    pulled = adj * admit
    log_grad = decay * (adj * before * mask_ref[:, 1:2] - pulled * conv * decay / size)
    recall_grad = -speed * log_grad * recall * (1.0 - recall)
    admit_grad = sized * conv * admit * (1.0 - admit)
    conv_grad = sized * admit
    recall_low = recall_grad.astype(BF16)
    admit_low = admit_grad.astype(BF16)
    gates = gates_ref[0].astype(F32)
    recall_weight = block_diagonal(gates[:head], head, BF16)
    admit_weight = block_diagonal(gates[head:], head, BF16)
    conv_grad = conv_grad + mm(recall_low, recall_weight, 1, 1) + mm(admit_low, admit_weight, 1, 1)
    wide = inputs_ref[0].astype(F32)
    blank = jnp.zeros((HALO, width), F32)
    reach = jnp.concatenate([blank, vec[0:1] * conv_grad], axis=0)
    tap_grads = [jnp.sum(conv_grad * wide[HALO:], axis=0, keepdims=True)]
    for shift in range(1, 4):
        masked = conv_grad * mask_ref[:, shift : shift + 1]
        moved = pltpu.roll(wide, shift, 0)[HALO:]
        tap_grads.append(jnp.sum(masked * moved, axis=0, keepdims=True))
        back = jnp.concatenate([blank, vec[shift : shift + 1] * masked], axis=0)
        reach = reach + pltpu.roll(back, count + HALO - shift, 0)
    input_back = reach.astype(BF16)
    conv_low = conv.astype(BF16)
    input_back_out[0] = input_back
    small_out[0, :head] = fold_diagonal(mm(conv_low, recall_low, 0, 0), head).astype(BF16)
    small_out[0, head : 2 * head] = fold_diagonal(mm(conv_low, admit_low, 0, 0), head).astype(BF16)
    rows = tap_grads + [
        jnp.sum(conv_grad, axis=0, keepdims=True),
        jnp.sum(recall_grad, axis=0, keepdims=True),
        jnp.sum(admit_grad, axis=0, keepdims=True),
        jnp.sum(recall * log_grad, axis=0, keepdims=True),
        edge_ref[0, 2:3],
    ]
    rows.append(jnp.zeros((TABLE - 2 * head - len(rows), width), F32))
    small_out[0, 2 * head :] = jnp.concatenate(rows, axis=0).astype(BF16)
    through_gate = mm(gate_back_ref[0], gate_weight_ref[0, 0], 1, 1)
    through_input = mm(input_back, input_weight_ref[0, 0], 1, 1)

    @pl.when(step == 0)
    def _():
        acc[...] = through_input

    @pl.when(step > 0)
    def _():
        acc[...] += through_input

    acc[HALO:] += through_gate

    @pl.when(step == pl.num_programs(0) - 1)
    def _():
        normed_grad_out[...] = acc[...]


def mix_back(
    weights, inputs, gate_back, kept, scan, adj, carry, mask, gates, vec, edge, backs, ahead, after
):
    shards, _, count, width = scan.shape
    model = weights.shape[2]
    head = gates.shape[1] // 2
    depth = len(backs)

    def flat(*shape):
        return pl.BlockSpec(shape, lambda s: (0,) * len(shape))

    def at(*shape):
        return pl.BlockSpec((1,) + shape, lambda s: (s,) + (0,) * len(shape))

    def ahead_spec(shift):
        return pl.BlockSpec((1, 8, width), lambda s: ((s + shift) % shards, 0, 0))

    return launch(
        functools.partial(mix_back_kernel, head, depth),
        [
            weights, weights, inputs, gate_back, kept, scan, adj, carry, mask, gates, vec,
            edge, *backs, *ahead,
        ],
        [
            pl.BlockSpec((1, 1, model, width), lambda s: (s, 0, 0, 0)),
            pl.BlockSpec((1, 1, model, width), lambda s: (s, 1, 0, 0)),
            at(count + HALO, width),
            at(count, width),
            at(3, count, width),
            at(2, count, width),
            at(2, count, width),
            at(8, width),
            flat(*mask.shape),
            at(2 * head, width),
            at(8, width),
            at(8, width),
        ]
        + [ahead_spec(i + 1) for i in range(depth)]
        + [ahead_spec(i + 1) for i in range(depth - 1)],
        0.1,
        after,
        grid=(shards,),
        out_shape=[
            jax.ShapeDtypeStruct((shards, count + HALO, width), BF16),
            jax.ShapeDtypeStruct((shards, TABLE, width), BF16),
            jax.ShapeDtypeStruct((count + HALO, model), F32),
        ],
        out_specs=[at(count + HALO, width), at(TABLE, width), flat(count + HALO, model)],
        scratch_shapes=[pltpu.VMEM((count + HALO, model), F32)],
        name="mix_back",
    )


def home_kernel(groups, shards, place_ref, *rest):
    parts, (out, lines) = rest[: groups * shards], rest[groups * shards :]
    start = 0
    for group in range(groups):
        refs = parts[group * shards : (group + 1) * shards]
        size = refs[0].shape[0]
        if group == groups - 1:
            size -= lines.shape[1]
        total = refs[0][:size].astype(F32)
        for ref in refs[1:]:
            total = total + ref[:size].astype(F32)
        out[start : start + size] = total.astype(BF16)
        start += size
    for s in range(shards):
        lines[s] = refs[s][size:].astype(F32)
    model = lines.shape[1] // 4 * gain_chunk(0, lines.shape[2])
    total = None
    for owner in range(shards):
        which = lax.rem(owner - place_ref[0] + shards, shards)
        value = unpack_gains(lines[which], model)
        total = value if total is None else [a + b for a, b in zip(total, value, strict=True)]
    out[start:] = pack_gains(total, lines.shape[2])


def home_sum(place, groups, extra):
    shards = len(groups[0])
    rows = sum(group[0].shape[0] for group in groups)
    width = groups[0][0].shape[1]
    return launch(
        functools.partial(home_kernel, len(groups), shards),
        [place, *[part for group in groups for part in group]],
        [smem()] + [vmem()] * (len(groups) * shards),
        0.1,
        out_shape=[jax.ShapeDtypeStruct((rows, width), BF16)],
        out_specs=[vmem()],
        scratch_shapes=[pltpu.VMEM((shards, extra, width), F32)],
        name="home_sum",
        vmem_mib=16,
    )[0]


def assemble_kernel(
    rows_total,
    core_ref,
    own_ref,
    other_ref,
    decay_ref,
    gate_out,
    out_out,
    input_out,
    recall_out,
    admit_out,
    recall_bias_out,
    admit_bias_out,
    taps_out,
    bias_out,
    decay_out,
    mean_out,
    gain_one_out,
    gain_two_out,
    whole,
    small,
):
    quads, rows, _ = own_ref.shape
    model = gate_out.shape[0]
    block = model // (2 * quads)
    extra = TABLE // (2 * quads)
    for quad in range(quads):
        for ref, who in ((own_ref, core_ref[0]), (other_ref, 1 - core_ref[0])):
            start = pl.multiple_of((quad * 2 + who) * block, block)
            gate_out[pl.ds(start, block), :] = ref[quad, :block].astype(F32)
            whole[pl.ds(start, block), :] = ref[quad, block : 2 * block].astype(F32)
            input_out[pl.ds(start, block), :] = ref[quad, 2 * block : 3 * block].astype(F32)
            start = pl.multiple_of((quad * 2 + who) * extra, extra)
            small[pl.ds(start, extra), :] = ref[quad, 3 * block : 3 * block + extra].astype(F32)
    out_out[...] = whole[...].T
    heads, head, _ = recall_out.shape
    lines = small[2 * head : 2 * head + 16]
    for h in range(heads):
        cols = slice(h * head, (h + 1) * head)
        recall_out[h] = small[:head, cols]
        admit_out[h] = small[head : 2 * head, cols]
        recall_bias_out[h : h + 1] = lines[5:6, cols]
        admit_bias_out[h : h + 1] = lines[6:7, cols]
    taps_out[...] = lines[:4]
    bias_out[...] = lines[4]
    decay_out[...] = lines[7] * (STRENGTH * jax.nn.sigmoid(-decay_ref[...]))
    mean_out[...] = lines[8] * (1.0 / rows_total)
    gains = None
    for ref in (own_ref, other_ref):
        part = None
        for quad in range(quads):
            value = unpack_gains(ref[quad, 3 * block + extra :], model)
            part = value if part is None else [a + b for a, b in zip(part, value, strict=True)]
        gains = part if gains is None else [a + b for a, b in zip(gains, part, strict=True)]
    gain_one_out[...] = gains[0].reshape(model)
    gain_two_out[...] = gains[1].reshape(model)


def assemble(core, own, other, decay, model, heads, head, rows_total):
    width = own.shape[2]
    shapes = [
        (model, width),
        (width, model),
        (model, width),
        (heads, head, head),
        (heads, head, head),
        (heads, head),
        (heads, head),
        (4, width),
        (width,),
        (width,),
        (width,),
        (model,),
        (model,),
    ]
    return launch(
        functools.partial(assemble_kernel, rows_total),
        [core, own, other, decay],
        [smem(), vmem(), vmem(), vmem()],
        0.1,
        out_shape=[jax.ShapeDtypeStruct(shape, F32) for shape in shapes],
        out_specs=[vmem()] * len(shapes),
        scratch_shapes=[pltpu.VMEM((model, width), F32), pltpu.VMEM((TABLE, width), F32)],
        name="assemble",
        vmem_mib=16,
    )


def on_device(
    tokens,
    doc_ids,
    cotangent,
    norm_gain,
    gate_proj,
    input_proj,
    conv_weight,
    conv_bias,
    recall_weight,
    recall_bias,
    admit_weight,
    admit_bias,
    decay_param,
    out_proj,
    mlp_gain,
    mlp_gate,
    mlp_up,
    mlp_down,
):
    count, model = tokens.shape
    width = gate_proj.shape[1]
    heads, head, _ = recall_weight.shape
    hidden_width = mlp_gate.shape[1]
    piece = mlp_gate.shape[0]
    quads = lax.axis_size("quad")
    shards = lax.axis_size("chan")
    group = 2 * quads
    quad = lax.axis_index("quad").astype(jnp.int32)
    core = lax.axis_index("core").astype(jnp.int32)
    place = lax.axis_index("chan").astype(jnp.int32)
    quad_one, core_one = quad.reshape(1), core.reshape(1)

    def hop(values, rel):
        return lax.ppermute(values, "quad", [(i, i ^ rel) for i in range(quads)])

    def swap(values):
        return lax.ppermute(values, "core", [(0, 1), (1, 0)])

    def along(values, shift):
        return lax.ppermute(values, "chan", [(i, (i + shift) % shards) for i in range(shards)])

    def share(values):
        every = jnp.broadcast_to(values[None], (quads,) + values.shape)
        return lax.all_to_all(every, "quad", 0, 0, tiled=True)

    slots = (quad * 2 + core).reshape(1)
    arriving = jnp.stack([(quad ^ rel) * 2 for rel in range(quads)])
    arriving = jnp.concatenate([arriving + core, arriving + 1 - core])

    def halves(values, made):
        if made:
            return made
        rows = values.shape[0]
        split = values.reshape(rows, quads, 2, model // group)
        return [
            lax.dynamic_index_in_dim(split, who, 2, False).reshape(rows, model // 2)
            for who in (core, 1 - core)
        ]

    ends = along(tokens[count - HALO :], 1)
    own_weights, own_table, pieces = prepare(
        slots,
        gate_proj,
        input_proj,
        out_proj,
        recall_weight,
        recall_bias,
        admit_weight,
        admit_bias,
        conv_weight,
        conv_bias,
        decay_param,
        group,
    )
    arrived = along(pieces, 1)
    normed, *made = norm(core_one, ends, tokens, norm_gain, group)

    offset = place * count
    spots = (offset + jnp.arange(count)) % LENGTH
    padded = jnp.concatenate([jnp.full((HALO,), -1, jnp.int32), doc_ids])
    here = lax.dynamic_slice_in_dim(padded, offset + HALO, count)
    columns = [jnp.ones((count,), F32)]
    for shift in range(1, 4):
        moved = lax.dynamic_slice_in_dim(padded, offset + HALO - shift, count)
        columns.append(((spots >= shift) & (here == moved)).astype(F32))
    columns += [jnp.zeros((count,), F32)] * 4
    mask = jnp.stack(columns, axis=1)

    own_width = hidden_width // quads
    slices = jnp.stack([mlp_gate, mlp_up, mlp_down])
    slices = slices.reshape(3, piece, quads, own_width).transpose(2, 0, 1, 3)
    def local(shard, weight_pieces, stacks, after=()):
        return mix_local(
            shard, shards, head, arriving, normed, mask, weight_pieces, stacks, after
        )

    normed_own, normed_other = halves(normed, made)
    normed_other = swap(normed_other)
    stacks, _ = local(0, [own_weights, own_table], None)
    (slices,) = fence([slices], [pieces])
    slices = lax.all_to_all(slices, "quad", 0, 0, tiled=True)
    near = quads // 2 + 1
    cots = [cotangent] + [hop(cotangent, rel) for rel in range(1, near)]
    gathered, waits, edges, shard_pieces = None, [normed_other, *cots[1:]], [stacks[5]], []
    for s in range(1, shards + 1):
        onward = [arrived] if s < shards else [cotangent]
        if s == min(2, shards - 1):
            onward.append(slices)
        if s == 1:
            arrived, *onward = fence(onward, waits)
        else:
            packed, arrived, *onward = pack(held, onward, [edges[s - 2]])
            stacks, _ = local(s - 1, [packed, swap(packed)], stacks)
            edges.append(stacks[5])
        if onward:
            gathered = lax.all_gather(onward[0], "chan", axis=0)
        if s == shards:
            cots += [hop(arrived, rel) for rel in range(near, quads)]
            break
        held = [arrived] + [hop(arrived, rel) for rel in range(1, quads)]
        if s < shards - 1:
            arrived = along(arrived, 1)
    weights, inputs, gated, kept, scan, edge, gates, vec = stacks
    (edge,) = fence([edge], cots[near:])
    depth = LENGTH // count - 1
    behind = [along(edge, i + 1) for i in range(depth)]
    (gathered,) = fence([gathered], behind)
    carry, branch_in, middle, second, again = branch(
        scan, gated, weights, tokens, mlp_gain.reshape(1, model), behind, []
    )
    mlp_weights = arrange(core_one, gathered, swap(gathered), [second])
    ahead = [along(edge, -(i + 1)) for i in range(depth - 1)]
    branch_in_other = swap(branch_in)

    gate_grads, up_grads, hiddens, backs, seconds = [], [], [], [], []
    for rel in range(quads):
        if rel == 0:
            seconds.append(second)
        else:
            seconds.append(hop(second if rel < near else again, rel))
        gate_grad, up_grad, hidden, back, *carry_on = mlp_block(
            seconds[rel], cots[rel], mlp_weights,
            backs[-1:] if rel else [*ahead, branch_in_other], [] if rel else [again],
        )
        if rel == 0:
            (again,) = carry_on
        gate_grads.append(gate_grad)
        up_grads.append(up_grad)
        hiddens.append(hidden)
        backs.append(back)
    backs = [hop(back, rel) if rel else back for rel, back in enumerate(backs)]
    own_grads, other_grads, results = mlp_grads(
        quad_one, core_one, mlp_weights, cots, seconds, gate_grads, up_grads, hiddens, shards
    )
    results = lax.all_to_all(results, "quad", 0, 0, tiled=True)
    middle_grad, branch_grad, gain_two, *made, own_grads, other_grads = middle_back(
        backs, middle, cotangent, mlp_gain, core_one, group, [], [own_grads, other_grads]
    )

    def reduce(chip):
        return jnp.sum(lax.all_to_all(chip, "quad", 0, 0, tiled=True).astype(F32), axis=0)

    grad_own, grad_other = halves(branch_grad, made)
    block_out = (middle + jnp.sum(results.astype(F32), axis=0)).astype(BF16)
    gate_back, adj, edge_back, own_grads = adjoint(
        branch_grad, weights, gated, scan, kept, carry, mask, vec, [own_grads]
    )
    edges_back = [along(edge_back, -(i + 1)) for i in range(depth)]
    (chip_one,) = outer(
        core_one,
        quads,
        [
            normed_own[HALO:],
            normed_other[HALO:],
            gate_back,
            swap(gate_back),
            grad_own,
            swap(grad_other),
            branch_in,
            branch_in_other,
        ],
        after=[*edges_back, results],
    )
    grads = add_pair(own_grads, swap(other_grads))
    grads = lax.psum_scatter(grads, "chan", scatter_dimension=0)

    def home(totals):
        return [totals[0]] + [along(totals[s].astype(BF16), -s) for s in range(1, shards)]

    sum_one = reduce(chip_one)
    input_back, small, normed_grad = mix_back(
        weights, inputs, gate_back, kept, scan, adj, carry, mask, gates, vec, edge, edges_back, ahead,
        [chip_one],
    )

    halo_grad = along(normed_grad[:HALO].astype(BF16), -1)
    inside = ((place + 1) * count % LENGTH != 0).astype(jnp.int32).reshape(1)
    grad_tokens, lines = tokens_back(
        inside, normed_grad, halo_grad, tokens, norm_gain, middle_grad, gain_two, width
    )
    (chip_two,) = outer(
        core_one,
        quads,
        [normed_own, normed_other, input_back, swap(input_back)],
        [small, swap(small)],
        [sum_one, lines],
    )
    home_one = home(sum_one)
    extra = lines.shape[0]
    totals = reduce(chip_two)
    totals, grads = fence([totals, grads], home_one[1:])
    grads = lax.all_to_all(grads, "quad", 0, 0, tiled=True)
    grads = grads.transpose(1, 2, 0, 3).reshape(3, piece, hidden_width).astype(F32)
    totals = jnp.concatenate(
        [totals, jnp.broadcast_to(lines.astype(F32)[None], (shards, extra, width))], axis=1
    )
    everything = home_sum(place.reshape(1), [home_one, home(totals)], extra)
    (everything,) = fence([everything], [grads])
    own = share(everything)
    (
        grad_gate,
        grad_out,
        grad_input,
        grad_recall,
        grad_admit,
        grad_recall_bias,
        grad_admit_bias,
        grad_taps,
        grad_bias,
        grad_decay,
        gate_mean,
        gain_one,
        gain_two,
    ) = assemble(
        core_one, own, swap(own), decay_param, model, heads, head, count * group * shards
    )

    return (
        block_out,
        grad_tokens,
        gain_one,
        grad_gate,
        grad_input,
        grad_taps,
        grad_bias,
        grad_recall,
        grad_recall_bias,
        grad_admit,
        grad_admit_bias,
        grad_decay,
        grad_out,
        gain_two,
        grads[0],
        grads[1],
        grads[2],
        gate_mean,
    )


def solution(mesh):
    in_specs = (
        P(("quad", "core", "chan"), None),
        P(("quad", "core")),
        P(("quad", "core", "chan"), None),
        P(),
        P(None, "chan"),
        P(None, "chan"),
        P(None, "chan"),
        P("chan"),
        P("chan", None, None),
        P("chan", None),
        P("chan", None, None),
        P("chan", None),
        P("chan"),
        P("chan", None),
        P(),
        P(("quad", "core", "chan"), None),
        P(("quad", "core", "chan"), None),
        P(("quad", "core", "chan"), None),
    )
    out_specs = (
        P(("quad", "core", "chan"), None),
        P(("quad", "core", "chan"), None),
        P(),
        P(None, "chan"),
        P(None, "chan"),
        P(None, "chan"),
        P("chan"),
        P("chan", None, None),
        P("chan", None),
        P("chan", None, None),
        P("chan", None),
        P("chan"),
        P("chan", None),
        P(),
        P(("quad", "core", "chan"), None),
        P(("quad", "core", "chan"), None),
        P(("quad", "core", "chan"), None),
        P("chan"),
    )
    devices = mesh.devices
    quads, shards = devices.shape[0] // 2, devices.shape[1]
    split = jax.sharding.Mesh(devices.reshape(quads, 2, shards), ("quad", "core", "chan"))
    return jax.shard_map(
        on_device, mesh=split, in_specs=in_specs, out_specs=out_specs, check_vma=False
    )
```

time: 462 us -> 362 us (0.78)
  starting transfers between devices: 148 us -> 70.8 us
  waiting for transfers between devices: 137 us -> 103 us
  blocking collectives: 0 us -> 20.1 us
  other arithmetic: 29.9 us -> 10.5 us
  local copies, waits for them, and re-layouts: 25.3 us -> 32.6 us
    ppermute x76 -> x30, starting transfers between devices: 108 us -> 32.4 us  [the longest x18 17.4 us: hop(): return lax.ppermute(values, 'quad', [(i, i ^ rel) for i in range(quads)])]
    ppermute x76 -> x30, waiting for transfers between devices: 98.6 us -> 44.6 us  [the longest x18 41.9 us: hop(): return lax.ppermute(values, 'quad', [(i, i ^ rel) for i in range(quads)])]
    all_to_all x2 -> x5, waiting for transfers between devices: 1.38 us -> 33.4 us  [the longest x2 33.4 us: reduce(): lax.all_to_all(chip, 'quad', 0, 0, tiled=True).astype(F32)]
    all_to_all x0 -> x1, blocking collectives: none -> 20.1 us  [share(): return lax.all_to_all(every, 'quad', 0, 0, tiled=True)]
    unnamed x164 -> x136, local copies, waits for them, and re-layouts: 10.2 us -> 27.7 us
    ppermute x23 -> x17, starting transfers between devices: 30.6 us -> 16.1 us  [along(): lax.ppermute(values, 'chan', [(i, (i + shift) % shards) for i in range(sh...]
    all_to_all x2 -> x5, starting transfers between devices: 9.54 us -> 22.3 us  [the longest x2 9.36 us: reduce(): lax.all_to_all(chip, 'quad', 0, 0, tiled=True).astype(F32)]
    add x9 -> x1, other arithmetic: 12.4 us -> 0.08 us  [on_device(): arriving = jnp.concatenate([arriving + core, arriving + 1 - core])]
  transfers between devices with their start and end apart: 103 -> 54, of which waited for: 32 -> 21; matrix products, arithmetic and copies ran while one was open for 9% -> 5% of each run, Pallas kernels for 15% -> 27%
where the time goes in v2:
time: 362 us; the launch traced here: 355 us
  Pallas kernels  103 us (28%)
  waiting for transfers between devices  103 us (28%)
  starting transfers between devices  70.8 us (20%)
  local copies, waits for them, and re-layouts  32.6 us (9%)
  blocking collectives  20.1 us (6%)
  between operations  15.3 us (4%)
  other arithmetic  10.5 us (3%)
    pallas_call x31, Pallas kernels, launch(): pl.pallas_call(body, out_shape=list(out_shape) + [jax.ShapeDtypeStruct(c....  103 us
    ppermute x18, waiting for transfers between devices, hop(): return lax.ppermute(values, 'quad', [(i, i ^ rel) for i in range(quads)])  41.9 us
    all_to_all x2, waiting for transfers between devices, reduce(): lax.all_to_all(chip, 'quad', 0, 0, tiled=True).astype(F32)  33.4 us
    unnamed x136, local copies, waits for them, and re-layouts  27.7 us
    ppermute x17, waiting for transfers between devices, along(): lax.ppermute(values, 'chan', [(i, (i + shift) % shards) for i in range(sh...  25.1 us
    all_to_all x1, blocking collectives, share(): return lax.all_to_all(every, 'quad', 0, 0, tiled=True)  20.1 us
    ppermute x18, starting transfers between devices, hop(): return lax.ppermute(values, 'quad', [(i, i ^ rel) for i in range(quads)])  17.4 us
    ppermute x17, starting transfers between devices, along(): lax.ppermute(values, 'chan', [(i, (i + shift) % shards) for i in range(sh...  16.1 us
  transfers between devices with their start and end apart: 54, of which 21 were waited for; matrix products, arithmetic and copies ran while one was open for 5% of the time, Pallas kernels for 27%

profile of v2, /device:TPU:17, one launch (start us, length us, event | category | flops | bytes accessed | tf_op | source)
XLA Modules:
  0.0 355.5 jit_solution(11208930912058524744)
XLA Ops:
  17.0 4.3 %all-to-all-start = ((bf16[4,3,32,768]{3,2,1,0:T(8,128)(2,1)}), bf16[4,3,32,768]{3,2,1,0:T(8,128)(2,1)}, u32[]{:S(2)}, u32[]{:S(2)}) async-start(bf16[4,3,32,768]{3,2,1,0:T(8,128)(2,1)} %fence.7), calls=%async_computation | async-start | bytes 1179648 | tf_op jit(solution)/shard_map/all_to_all | solution.py:1256
  31.2 6.3 %mix_local.4 = (bf16[4,3,1024,384]{3,2,1,0:T(8,128)(2,1)}, bf16[4,272,384]{2,1,0:T(8,128)(2,1)}, bf16[4,256,384]{2,1,0:T(8,128)(2,1)}, f32[4,3,256,384]{3,2,1,0:...) custom-call(s32[8]{0:T(128)} %pad_add_fusion.1.refs_0_, ...), custom_call_target="tpu_custom_call" | custom-call | flops 1880999936 | bytes 5985000 | tf_op jit(solution)/shard_map/mix_local/pallas_call | solution.py:152
  38.3 5.1 %collective-permute-done.7.refs_3_ = bf16[1,416,384]{2,1,0:T(8,128)(2,1)} collective-permute-done((bf16[1,416,384]{2,1,0:T(8,128)(2,1)S(1)}, bf16[1,416,384]{2,1,0:T(8,128)(2,1)}, u32[]{:S(2)}, u32[]{:S(2)}) %collective-permute-start.7) | collective-permute-done | bytes 319520 | tf_op jit(solution)/shard_map/ppermute | solution.py:1189
  52.9 5.8 %mix_local.5 = (bf16[4,3,1024,384]{3,2,1,0:T(8,128)(2,1)}, bf16[4,272,384]{2,1,0:T(8,128)(2,1)}, bf16[4,256,384]{2,1,0:T(8,128)(2,1)}, f32[4,3,256,384]{3,2,1,0:...) custom-call(s32[8]{0:T(128)} %pad_add_fusion.1.refs_0_, ...), custom_call_target="tpu_custom_call", output_to_operand_aliasing={{0}: (5, {}), {1}: (6, {}), {2}: (7, {}), {3}: (8, {}), {4}... | custom-call | flops 1880999936 | bytes 5985000 | tf_op jit(solution)/shard_map/mix_local/pallas_call | solution.py:152
  58.7 6.0 %collective-permute-done.10.refs_2_ = bf16[1,416,384]{2,1,0:T(8,128)(2,1)S(1)} collective-permute-done((bf16[1,416,384]{2,1,0:T(8,128)(2,1)S(1)}, bf16[1,416,384]{2,1,0:T(8,128)(2,1)S(1)}, u32[]{:S(2)}, u32[]{:S(2)}) %collective-permute-start.10) | collective-permute-done | bytes 319520 | tf_op jit(solution)/shard_map/ppermute | solution.py:1189
  72.5 5.8 %mix_local.6 = (bf16[4,3,1024,384]{3,2,1,0:T(8,128)(2,1)}, bf16[4,272,384]{2,1,0:T(8,128)(2,1)}, bf16[4,256,384]{2,1,0:T(8,128)(2,1)}, f32[4,3,256,384]{3,2,1,0:...) custom-call(s32[8]{0:T(128)} %pad_add_fusion.1.refs_0_, ...), custom_call_target="tpu_custom_call", output_to_operand_aliasing={{0}: (5, {}), {1}: (6, {}), {2}: (7, {}), {3}: (8, {}), {4}... | custom-call | flops 1880999936 | bytes 5985000 | tf_op jit(solution)/shard_map/mix_local/pallas_call | solution.py:152
  78.2 7.3 %collective-permute-done.15.refs_2_ = bf16[1,416,384]{2,1,0:T(8,128)(2,1)S(1)} collective-permute-done((bf16[1,416,384]{2,1,0:T(8,128)(2,1)S(1)}, bf16[1,416,384]{2,1,0:T(8,128)(2,1)S(1)}, u32[]{:S(2)}, u32[]{:S(2)}) %collective-permute-start.15) | collective-permute-done | bytes 319520 | tf_op jit(solution)/shard_map/ppermute | solution.py:1189
  92.2 5.7 %mix_local.7 = (bf16[4,3,1024,384]{3,2,1,0:T(8,128)(2,1)}, bf16[4,272,384]{2,1,0:T(8,128)(2,1)}, bf16[4,256,384]{2,1,0:T(8,128)(2,1)}, f32[4,3,256,384]{3,2,1,0:...) custom-call(s32[8]{0:T(128)} %pad_add_fusion.1.refs_0_, ...), custom_call_target="tpu_custom_call", output_to_operand_aliasing={{0}: (5, {}), {1}: (6, {}), {2}: (7, {}), {3}: (8, {}), {4}... | custom-call | flops 1880999936 | bytes 5985000 | tf_op jit(solution)/shard_map/mix_local/pallas_call | solution.py:152
  97.9 5.0 %collective-permute-done.19.refs_0_.refs_1_.refs_6_ = bf16[256,1024]{1,0:T(8,128)(2,1)S(1)} collective-permute-done((bf16[256,1024]{1,0:T(8,128)(2,1)S(1)}, bf16[256,1024]{1,0:T(8,128)(2,1)S(1)}, u32[]{:S(2)}, u32[]{:S(2)}) %collective-permute-start.19) | collective-permute-done | bytes 524320 | tf_op jit(solution)/shard_map/ppermute | solution.py:1189
  116.7 7.1 %mix_branch.1 = (f32[4,8,384]{2,1,0:T(8,128)}, bf16[4,256,384]{2,1,0:T(8,128)(2,1)}, f32[256,1024]{1,0:T(8,128)}, bf16[256,1024]{1,0:T(8,128)(2,1)}, bf16[256,1024]{1,0:T(8,128)(2,1)}) custom-call(f32[4,2,256,384]{3,2,1,0:T(8,128)} %get-tuple-element.153.refs_0_.refs_3_.refs_5_, bf16[4,256,384]{2,1,0:T(8,128)(2,1)} %get-tuple-element.154.refs_1_.refs_2_, ...), custom_call_target="tpu_custom_call" | custom-call | flops 33000000 | bytes 105000 | tf_op jit(solution)/shard_map/mix_branch/pallas_call | solution.py:152
  132.8 4.4 %collective-permute-done.24.refs_0_.refs_8_ = bf16[256,1024]{1,0:T(8,128)(2,1)S(1)} collective-permute-done((bf16[256,1024]{1,0:T(8,128)(2,1)}, bf16[256,1024]{1,0:T(8,128)(2,1)S(1)}, u32[]{:S(2)}, u32[]{:S(2)}) %collective-permute-start.24) | collective-permute-done | bytes 524320 | tf_op jit(solution)/shard_map/ppermute | solution.py:1189
  152.6 8.8 %mlp_grads.1 = (bf16[4,4,3,32,768]{4,3,2,1,0:T(8,128)(2,1)S(1)}, bf16[4,4,3,32,768]{4,3,2,1,0:T(8,128)(2,1)}, bf16[4,256,1024]{2,1,0:T(8,128)(2,1)S(1)}) custom-call(s32[1]{0:T(128)} %bitcast.12.refs_0_, s32[1]{0:T(128)} %bitcast.4.refs_0_.refs_1_.refs_7_, bf16[3,1024,768]{2,1,0:T(8,128)(2,1)S(1)} %mlp_arrange.1.refs_2_, bf16[256,1024]{1,0:T(8,128)(2,1)S(1)} %copy-done.19, ...), custom_call_target="tpu_custom_call" | custom-call | flops 4950000128 | bytes 15750000 | tf_op jit(solution)/shard_map/mlp_grads/pallas_call | solution.py:152
  161.4 9.4 %collective-permute-done.30.refs_3_ = bf16[256,1024]{1,0:T(8,128)(2,1)S(1)} collective-permute-done((bf16[256,1024]{1,0:T(8,128)(2,1)S(1)}, bf16[256,1024]{1,0:T(8,128)(2,1)S(1)}, u32[]{:S(2)}, u32[]{:S(2)}) %collective-permute-start.30) | collective-permute-done | bytes 524320 | tf_op jit(solution)/shard_map/ppermute | solution.py:1189
  177.3 4.5 %all-to-all-start.1 = ((bf16[4,256,1024]{2,1,0:T(8,128)(2,1)}), bf16[4,256,1024]{2,1,0:T(8,128)(2,1)}, u32[]{:S(2)}, u32[]{:S(2)}) async-start(bf16[4,256,1024]{2,1,0:T(8,128)(2,1)} %copy-done.18), calls=%async_computation.1 | async-start | bytes 4194304 | tf_op jit(solution)/shard_map/all_to_all | solution.py:1310
  181.8 8.8 %mix_adjoint.1 = (bf16[4,256,384]{2,1,0:T(8,128)(2,1)}, f32[4,2,256,384]{3,2,1,0:T(8,128)}, f32[4,8,384]{2,1,0:T(8,128)}, bf16[4,4,3,32,768]{4,3,2,1,0:T(8,128)(2,1)}) custom-call(bf16[256,1024]{1,0:T(8,128)(2,1)} %copy-done.39, bf16[4,3,1024,384]{3,2,1,0:T(8,128)(2,1)} %get-tuple-element.155.refs_2_.refs_1_.refs_0_, ...), custom_call_target="tpu_custom_call", output_to_operand_aliasing={{3}: (8, {})} | custom-call | flops 33000000 | bytes 105000 | tf_op jit(solution)/shard_map/mix_adjoint/pallas_call | solution.py:152
  210.3 5.2 %mix_outer.2.refs_17_ = bf16[4,4,256,384]{3,2,1,0:T(8,128)(2,1)} custom-call(s32[1]{0:T(128)} %bitcast.4.refs_0_.refs_1_.refs_7_, bf16[256,512]{1,0:T(8,128)(2,1)S(1)} %slice.56.refs_1_, bf16[256,512]{1,0:T(8,128)(2,1)S(1)} %slice.70.refs_2_, bf16[4,256,384]{2,1,0:T(8,128)(2,1)S(1)} %copy-done.10, bf16[4,256,384]{2,1,0:T(8,128)(2,1)} %collective-permute-done.34.refs_4_, ...), custom_call_target="tpu_custom_call" | custom-call | flops 33000000 | bytes 105000 | tf_op jit(solution)/shard_map/mix_outer/pallas_call | solution.py:152
  216.7 4.9 %all-to-all-start.2 = ((bf16[4,4,256,384]{3,2,1,0:T(8,128)(2,1)}), bf16[4,4,256,384]{3,2,1,0:T(8,128)(2,1)}, u32[]{:S(2)}, u32[]{:S(2)}) async-start(bf16[4,4,256,384]{3,2,1,0:T(8,128)(2,1)} %mix_outer.2.refs_17_), calls=%async_computation.2 | async-start | bytes 6291456 | tf_op jit(solution)/shard_map/all_to_all | solution.py:1316
  221.7 13.7 %mix_back.1 = (bf16[4,272,384]{2,1,0:T(8,128)(2,1)}, bf16[4,256,384]{2,1,0:T(8,128)(2,1)}, f32[272,1024]{1,0:T(8,128)}) custom-call(bf16[4,3,1024,384]{3,2,1,0:T(8,128)(2,1)} %get-tuple-element.155.refs_2_.refs_1_.refs_0_, bf16[4,3,1024,384]{3,2,1,0:T(8,128)(2,1)} %get-tuple-element.155.refs_2_.refs_1_.refs_0_, ...), custom_call_target="tpu_custom_call" | custom-call | flops 33000000 | bytes 105000 | tf_op jit(solution)/shard_map/mix_back/pallas_call | solution.py:152
  244.3 13.3 %all-to-all-done.2 = bf16[4,4,256,384]{3,2,1,0:T(8,128)(2,1)} async-done(((bf16[4,4,256,384]{3,2,1,0:T(8,128)(2,1)}), bf16[4,4,256,384]{3,2,1,0:T(8,128)(2,1)}, u32[]{:S(2)}, u32[]{:S(2)}) %all-to-all-start.2) | async-done | bytes 3145760 | tf_op jit(solution)/shard_map/all_to_all | solution.py:1316
  260.3 4.7 %mix_outer.3 = bf16[4,4,160,384]{3,2,1,0:T(8,128)(2,1)} custom-call(s32[1]{0:T(128)} %bitcast.4.refs_0_.refs_1_.refs_7_, bf16[272,512]{1,0:T(8,128)(2,1)S(1)} %get-tuple-element.193.refs_1_, bf16[272,512]{1,0:T(8,128)(2,1)S(1)} %collective-permute-done.1.refs_0_.refs_2_, bf16[4,272,384]{2,1,0:T(8,128)(2,1)S(1)} %copy-done.26, ...), custom_call_target="tpu_custom_call" | custom-call | flops 33000000 | bytes 105000 | tf_op jit(solution)/shard_map/mix_outer/pallas_call | solution.py:152
  264.9 4.4 %all-to-all-start.3 = ((bf16[4,4,160,384]{3,2,1,0:T(8,128)(2,1)}), bf16[4,4,160,384]{3,2,1,0:T(8,128)(2,1)}, u32[]{:S(2)}, u32[]{:S(2)}) async-start(bf16[4,4,160,384]{3,2,1,0:T(8,128)(2,1)} %mix_outer.3), calls=%async_computation.3 | async-start | bytes 3932160 | tf_op jit(solution)/shard_map/all_to_all | solution.py:1316
  272.2 20.1 %all-to-all-done.3 = bf16[4,4,160,384]{3,2,1,0:T(8,128)(2,1)} async-done(((bf16[4,4,160,384]{3,2,1,0:T(8,128)(2,1)}), bf16[4,4,160,384]{3,2,1,0:T(8,128)(2,1)}, u32[]{:S(2)}, u32[]{:S(2)}) %all-to-all-start.3) | async-done | bytes 1966112 | tf_op jit(solution)/shard_map/all_to_all | solution.py:1316
  304.4 7.3 %collective-permute-done.44.refs_7_ = bf16[176,384]{1,0:T(8,128)(2,1)S(1)} collective-permute-done((bf16[176,384]{1,0:T(8,128)(2,1)S(1)}, bf16[176,384]{1,0:T(8,128)(2,1)S(1)}, u32[]{:S(2)}, u32[]{:S(2)}) %collective-permute-start.44) | collective-permute-done | bytes 135200 | tf_op jit(solution)/shard_map/ppermute | solution.py:1195
  317.0 20.1 %all_to_all.30.refs_1_ = bf16[4,432,384]{2,1,0:T(8,128)(2,1)S(1)} all-to-all(bf16[4,432,384]{2,1,0:T(8,128)(2,1)S(1)} %broadcast_in_dim.5), channel_id=1, replica_groups=mesh['quad'=4,'core'=2,'chan'=4] {'quad'}, dimensions={0} | all-to-all | bytes 2654208 | tf_op jit(solution)/shard_map/all_to_all | solution.py:1199
  (291 shorter events, 152.3 us)
Async XLA Ops:
  7.2 18.2 %collective-permute-start.2 = (bf16[256,1024]{1,0:T(8,128)(2,1)}, bf16[256,1024]{1,0:T(8,128)(2,1)S(1)}, u32[]{:S(2)}, u32[]{:S(2)}) collective-permute-start(bf16[256,1024]{1,0:T(8,128)(2,1)} %refs_5_.4), channel_id=1, source_target_pairs={{0,8},{8,0},{16,24},{24,16},{1,9},{9,1},{17,25},{25,17},{2,10},{10... | collective-permute-start | bytes 1572872 | tf_op jit(solution)/shard_map/ppermute | solution.py:1189
  8.5 16.9 %collective-permute-start.3 = (bf16[256,1024]{1,0:T(8,128)(2,1)}, bf16[256,1024]{1,0:T(8,128)(2,1)S(1)}, u32[]{:S(2)}, u32[]{:S(2)}) collective-permute-start(bf16[256,1024]{1,0:T(8,128)(2,1)} %refs_5_.4), channel_id=1, source_target_pairs={{0,16},{8,24},{16,0},{24,8},{1,17},{9,25},{17,1},{25,9},{2,18},{10... | collective-permute-start | bytes 1572872 | tf_op jit(solution)/shard_map/ppermute | solution.py:1189
  17.0 20.6 %all-to-all-start = ((bf16[4,3,32,768]{3,2,1,0:T(8,128)(2,1)}), bf16[4,3,32,768]{3,2,1,0:T(8,128)(2,1)}, u32[]{:S(2)}, u32[]{:S(2)}) async-start(bf16[4,3,32,768]{3,2,1,0:T(8,128)(2,1)} %fence.7), calls=%async_computation | async-start | bytes 1179648 | tf_op jit(solution)/shard_map/all_to_all | solution.py:1256
  21.3 87.1 %all-gather.3.cloned.1.call-start = ((), (), s32[]{:S(2)}) async-start(), calls=%async_computation.8 | async-start | bytes 2949120 | tf_op jit(solution)/shard_map/all_gather | solution.py:1271
  48.5 16.2 %collective-permute-start.10 = (bf16[1,416,384]{2,1,0:T(8,128)(2,1)S(1)}, bf16[1,416,384]{2,1,0:T(8,128)(2,1)S(1)}, u32[]{:S(2)}, u32[]{:S(2)}) collective-permute-start(bf16[1,416,384]{2,1,0:T(8,128)(2,1)S(1)} %get-tuple-element.125.refs_0_), channel_id=1, source_target_pairs={{0,16},{8,24},{16,0},{24,8},{1,17},{9,25},{17,1},{25,9},{2,18},{10... | collective-permute-start | bytes 958472 | tf_op jit(solution)/shard_map/ppermute | solution.py:1189
  48.9 15.8 %collective-permute-start.11 = (bf16[1,416,384]{2,1,0:T(8,128)(2,1)S(1)}, bf16[1,416,384]{2,1,0:T(8,128)(2,1)S(1)}, u32[]{:S(2)}, u32[]{:S(2)}) collective-permute-start(bf16[1,416,384]{2,1,0:T(8,128)(2,1)S(1)} %get-tuple-element.125.refs_0_), channel_id=1, source_target_pairs={{0,24},{8,16},{16,8},{24,0},{1,25},{9,17},{17,9},{25,1},{2,26},{10... | collective-permute-start | bytes 958472 | tf_op jit(solution)/shard_map/ppermute | solution.py:1189
  69.8 15.7 %collective-permute-start.15 = (bf16[1,416,384]{2,1,0:T(8,128)(2,1)S(1)}, bf16[1,416,384]{2,1,0:T(8,128)(2,1)S(1)}, u32[]{:S(2)}, u32[]{:S(2)}) collective-permute-start(bf16[1,416,384]{2,1,0:T(8,128)(2,1)S(1)} %get-tuple-element.135.refs_0_), channel_id=1, source_target_pairs={{0,16},{8,24},{16,0},{24,8},{1,17},{9,25},{17,1},{25,9},{2,18},{10... | collective-permute-start | bytes 958472 | tf_op jit(solution)/shard_map/ppermute | solution.py:1189
  124.1 16.3 %collective-permute-start.25 = (bf16[256,1024]{1,0:T(8,128)(2,1)}, bf16[256,1024]{1,0:T(8,128)(2,1)S(1)}, u32[]{:S(2)}, u32[]{:S(2)}) collective-permute-start(bf16[256,1024]{1,0:T(8,128)(2,1)} %get-tuple-element.160.refs_3_.refs_0_.refs_7_), channel_id=1, source_target_pairs={{0,16},{8,24},{16,0},{24,8},{1,17},{9,25},{17,1},{25,9},{2,18},{10... | collective-permute-start | bytes 1572872 | tf_op jit(solution)/shard_map/ppermute | solution.py:1189
  131.4 16.9 %collective-permute-start.27 = (bf16[256,1024]{1,0:T(8,128)(2,1)S(1)}, bf16[256,1024]{1,0:T(8,128)(2,1)S(1)}, u32[]{:S(2)}, u32[]{:S(2)}) collective-permute-start(bf16[256,1024]{1,0:T(8,128)(2,1)S(1)} %get-tuple-element.163), channel_id=1, source_target_pairs={{0,24},{8,16},{16,8},{24,0},{1,25},{9,17},{17,9},{25,1},{2,26},{10... | collective-permute-start | bytes 1572872 | tf_op jit(solution)/shard_map/ppermute | solution.py:1189
  140.2 21.2 %collective-permute-start.28 = (bf16[256,1024]{1,0:T(8,128)(2,1)S(1)}, bf16[256,1024]{1,0:T(8,128)(2,1)S(1)}, u32[]{:S(2)}, u32[]{:S(2)}) collective-permute-start(bf16[256,1024]{1,0:T(8,128)(2,1)S(1)} %get-tuple-element.167.refs_3_), channel_id=1, source_target_pairs={{0,8},{8,0},{16,24},{24,16},{1,9},{9,1},{17,25},{25,17},{2,10},{10... | collective-permute-start | bytes 1572872 | tf_op jit(solution)/shard_map/ppermute | solution.py:1189
  143.4 18.0 %collective-permute-start.29 = (bf16[256,1024]{1,0:T(8,128)(2,1)S(1)}, bf16[256,1024]{1,0:T(8,128)(2,1)S(1)}, u32[]{:S(2)}, u32[]{:S(2)}) collective-permute-start(bf16[256,1024]{1,0:T(8,128)(2,1)S(1)} %get-tuple-element.169.refs_3_), channel_id=1, source_target_pairs={{0,16},{8,24},{16,0},{24,8},{1,17},{9,25},{17,1},{25,9},{2,18},{10... | collective-permute-start | bytes 1572872 | tf_op jit(solution)/shard_map/ppermute | solution.py:1189
  151.2 19.5 %collective-permute-start.30 = (bf16[256,1024]{1,0:T(8,128)(2,1)S(1)}, bf16[256,1024]{1,0:T(8,128)(2,1)S(1)}, u32[]{:S(2)}, u32[]{:S(2)}) collective-permute-start(bf16[256,1024]{1,0:T(8,128)(2,1)S(1)} %get-tuple-element.181), channel_id=1, source_target_pairs={{0,24},{8,16},{16,8},{24,0},{1,25},{9,17},{17,9},{25,1},{2,26},{10... | collective-permute-start | bytes 1572872 | tf_op jit(solution)/shard_map/ppermute | solution.py:1189
  174.9 17.3 %collective-permute-start.42 = (bf16[4,4,3,32,768]{4,3,2,1,0:T(8,128)(2,1)}, bf16[4,4,3,32,768]{4,3,2,1,0:T(8,128)(2,1)}, u32[]{:S(2)}, u32[]{:S(2)}) collective-permute-start(bf16[4,4,3,32,768]{4,3,2,1,0:T(8,128)(2,1)} %get-tuple-element.204), channel_id=1, source_target_pairs={{0,4},{4,0},{1,5},{5,1},{2,6},{6,2},{3,7},{7,3},{8,12},{12,8},{9,1... | collective-permute-start | bytes 7077896 | tf_op jit(solution)/shard_map/ppermute | solution.py:1192
  177.3 30.2 %all-to-all-start.1 = ((bf16[4,256,1024]{2,1,0:T(8,128)(2,1)}), bf16[4,256,1024]{2,1,0:T(8,128)(2,1)}, u32[]{:S(2)}, u32[]{:S(2)}) async-start(bf16[4,256,1024]{2,1,0:T(8,128)(2,1)} %copy-done.18), calls=%async_computation.1 | async-start | bytes 4194304 | tf_op jit(solution)/shard_map/all_to_all | solution.py:1310
  181.8 112.5 %reduce-scatter.2.cloned.1.call-start = ((), (), s32[]{:S(2)}) async-start(), calls=%async_computation.7 | async-start | bytes 2949120 | tf_op jit(solution)/shard_map/reduce_scatter | solution.py:1340
  190.6 16.9 %collective-permute-start.34 = (bf16[4,256,384]{2,1,0:T(8,128)(2,1)}, bf16[4,256,384]{2,1,0:T(8,128)(2,1)}, u32[]{:S(2)}, u32[]{:S(2)}) collective-permute-start(bf16[4,256,384]{2,1,0:T(8,128)(2,1)} %get-tuple-element.189.refs_3_), channel_id=1, source_target_pairs={{0,4},{4,0},{1,5},{5,1},{2,6},{6,2},{3,7},{7,3},{8,12},{12,8},{9,1... | collective-permute-start | bytes 2359304 | tf_op jit(solution)/shard_map/ppermute | solution.py:1192
  216.7 41.0 %all-to-all-start.2 = ((bf16[4,4,256,384]{3,2,1,0:T(8,128)(2,1)}), bf16[4,4,256,384]{3,2,1,0:T(8,128)(2,1)}, u32[]{:S(2)}, u32[]{:S(2)}) async-start(bf16[4,4,256,384]{3,2,1,0:T(8,128)(2,1)} %mix_outer.2.refs_17_), calls=%async_computation.2 | async-start | bytes 6291456 | tf_op jit(solution)/shard_map/all_to_all | solution.py:1316
  235.3 24.9 %collective-permute-start.40 = (bf16[4,272,384]{2,1,0:T(8,128)(2,1)}, bf16[4,272,384]{2,1,0:T(8,128)(2,1)}, u32[]{:S(2)}, u32[]{:S(2)}) collective-permute-start(bf16[4,272,384]{2,1,0:T(8,128)(2,1)} %get-tuple-element.200.refs_3_), channel_id=1, source_target_pairs={{0,4},{4,0},{1,5},{5,1},{2,6},{6,2},{3,7},{7,3},{8,12},{12,8},{9,1... | collective-permute-start | bytes 2506760 | tf_op jit(solution)/shard_map/ppermute | solution.py:1192
  236.5 23.7 %collective-permute-start.41 = (bf16[4,256,384]{2,1,0:T(8,128)(2,1)}, bf16[4,256,384]{2,1,0:T(8,128)(2,1)}, u32[]{:S(2)}, u32[]{:S(2)}) collective-permute-start(bf16[4,256,384]{2,1,0:T(8,128)(2,1)} %get-tuple-element.201.refs_5_), channel_id=1, source_target_pairs={{0,4},{4,0},{1,5},{5,1},{2,6},{6,2},{3,7},{7,3},{8,12},{12,8},{9,1... | collective-permute-start | bytes 2359304 | tf_op jit(solution)/shard_map/ppermute | solution.py:1192
  264.9 27.4 %all-to-all-start.3 = ((bf16[4,4,160,384]{3,2,1,0:T(8,128)(2,1)}), bf16[4,4,160,384]{3,2,1,0:T(8,128)(2,1)}, u32[]{:S(2)}, u32[]{:S(2)}) async-start(bf16[4,4,160,384]{3,2,1,0:T(8,128)(2,1)} %mix_outer.3), calls=%async_computation.3 | async-start | bytes 3932160 | tf_op jit(solution)/shard_map/all_to_all | solution.py:1316
  270.2 24.0 %collective-permute-start.37 = (bf16[256,384]{1,0:T(8,128)(2,1)}, bf16[256,384]{1,0:T(8,128)(2,1)S(1)}, u32[]{:S(2)}, u32[]{:S(2)}) collective-permute-start(bf16[256,384]{1,0:T(8,128)(2,1)} %get-tuple-element.227), channel_id=1, source_target_pairs={{0,3},{1,0},{2,1},{3,2},{4,7},{5,4},{6,5},{7,6},{8,11},{9,8},{10,9... | collective-permute-start | bytes 589832 | tf_op jit(solution)/shard_map/ppermute | solution.py:1195
  270.2 24.0 %collective-permute-start.38 = (bf16[256,384]{1,0:T(8,128)(2,1)}, bf16[256,384]{1,0:T(8,128)(2,1)S(1)}, u32[]{:S(2)}, u32[]{:S(2)}) collective-permute-start(bf16[256,384]{1,0:T(8,128)(2,1)} %get-tuple-element.226), channel_id=1, source_target_pairs={{0,2},{1,3},{2,0},{3,1},{4,6},{5,7},{6,4},{7,5},{8,10},{9,11},{10,... | collective-permute-start | bytes 589832 | tf_op jit(solution)/shard_map/ppermute | solution.py:1195
  272.2 22.0 %collective-permute-start.39 = (bf16[256,384]{1,0:T(8,128)(2,1)S(1)}, bf16[256,384]{1,0:T(8,128)(2,1)S(1)}, u32[]{:S(2)}, u32[]{:S(2)}) collective-permute-start(bf16[256,384]{1,0:T(8,128)(2,1)S(1)} %get-tuple-element.225), channel_id=1, source_target_pairs={{0,1},{1,2},{2,3},{3,0},{4,5},{5,6},{6,7},{7,4},{8,9},{9,10},{10,1... | collective-permute-start | bytes 589832 | tf_op jit(solution)/shard_map/ppermute | solution.py:1195
  296.2 19.4 %all-to-all-start.4 = ((bf16[4,3,32,768]{3,2,1,0:T(8,128)(2,1)}), bf16[4,3,32,768]{3,2,1,0:T(8,128)(2,1)}, u32[]{:S(2)}, u32[]{:S(2)}) async-start(bf16[4,3,32,768]{3,2,1,0:T(8,128)(2,1)} %copy-done.17), calls=%async_computation.5 | async-start | bytes 1179648 | tf_op jit(solution)/shard_map/all_to_all | solution.py:1367
  (96 other events, 598.2 us)
Sparse Core Ops, SparseCore 0:
  48.7 51.1 all-gather.2
  197.6 49.5 reduce-scatter.1

commit v3 on v2

--- a/solution.py
+++ b/solution.py
@@ -200,7 +200,7 @@
 
 
 def fence(carry, after=()):
-    return launch(lambda *refs: None, [], [], 0.01, after, carry, name="fence", vmem_mib=1)
+    return launch(lambda *refs: None, [], [], 0.01, after, carry, name="fence", vmem_mib=60)
 
 
 def prepare_kernel(
@@ -833,13 +833,13 @@
 def outer_kernel(groups, core_ref, *rest):
     pairs, rest = rest[: 4 * groups], rest[4 * groups :]
     *smalls, out, left, right, small = rest
-    count = pairs[0].shape[0]
+    count = pairs[2].shape[1]
     quads, shards = out.shape[:2]
     block = left.shape[1] // quads
     for group in range(groups):
         left_ref, left_other, right_ref, right_other = pairs[4 * group : 4 * group + 4]
-        left[:count] = left_ref[...]
-        left[count:] = left_other[...]
+        left[:count] = left_ref[left_ref.shape[0] - count :]
+        left[count:] = left_other[left_ref.shape[0] - count :]
         for s in range(shards):
             right[:count] = right_ref[s]
             right[count:] = right_other[s]
@@ -877,7 +877,6 @@
             pltpu.VMEM((TABLE, width), BF16),
         ],
         name="mix_outer",
-        vmem_mib=16,
     )
 
 
@@ -1024,44 +1023,92 @@
 
 
 def home_kernel(groups, shards, place_ref, *rest):
-    parts, (out, lines) = rest[: groups * shards], rest[groups * shards :]
-    start = 0
-    for group in range(groups):
-        refs = parts[group * shards : (group + 1) * shards]
-        size = refs[0].shape[0]
-        if group == groups - 1:
-            size -= lines.shape[1]
-        total = refs[0][:size].astype(F32)
-        for ref in refs[1:]:
-            total = total + ref[:size].astype(F32)
-        out[start : start + size] = total.astype(BF16)
-        start += size
+    parts, rest = rest[: groups * shards], rest[groups * shards :]
+    if len(rest) == 1:
+        (out,) = rest
+        start = 0
+        for group in range(groups):
+            refs = parts[group * shards : (group + 1) * shards]
+            size = refs[0].shape[0]
+            total = refs[0][...].astype(F32)
+            for ref in refs[1:]:
+                total = total + ref[...].astype(F32)
+            out[start : start + size] = total.astype(BF16)
+            start += size
+        return
+    grads_ref, out, lines = rest
+    rows = parts[0].shape[0]
+    size = rows - lines.shape[1]
+    total = parts[0][:size].astype(F32)
+    for ref in parts[1:]:
+        total = total + ref[:size].astype(F32)
+    total = total.astype(BF16)
     for s in range(shards):
-        lines[s] = refs[s][size:].astype(F32)
+        lines[s] = parts[s][size:].astype(F32)
     model = lines.shape[1] // 4 * gain_chunk(0, lines.shape[2])
-    total = None
+    gains = None
     for owner in range(shards):
         which = lax.rem(owner - place_ref[0] + shards, shards)
         value = unpack_gains(lines[which], model)
-        total = value if total is None else [a + b for a, b in zip(total, value, strict=True)]
-    out[start:] = pack_gains(total, lines.shape[2])
-
-
-def home_sum(place, groups, extra):
+        gains = value if gains is None else [a + b for a, b in zip(gains, value, strict=True)]
+    gains = pack_gains(gains, lines.shape[2])
+    for quad in range(out.shape[0]):
+        out[quad, :size] = total
+        out[quad, size:rows] = gains
+        out[quad, rows:] = grads_ref[quad]
+
+
+def home_sum(place, groups, extra, grads=None, after=()):
     shards = len(groups[0])
     rows = sum(group[0].shape[0] for group in groups)
     width = groups[0][0].shape[1]
+    inputs = [place, *[part for group in groups for part in group]]
+    shape = (rows, width)
+    if grads is not None:
+        inputs.append(grads)
+        shape = (grads.shape[0], rows + grads.shape[1], width)
     return launch(
         functools.partial(home_kernel, len(groups), shards),
-        [place, *[part for group in groups for part in group]],
-        [smem()] + [vmem()] * (len(groups) * shards),
+        inputs,
+        [smem()] + [vmem()] * (len(inputs) - 1),
         0.1,
-        out_shape=[jax.ShapeDtypeStruct((rows, width), BF16)],
+        after,
+        out_shape=[jax.ShapeDtypeStruct(shape, BF16)],
         out_specs=[vmem()],
-        scratch_shapes=[pltpu.VMEM((shards, extra, width), F32)],
+        scratch_shapes=[pltpu.VMEM((shards, extra, width), F32)] if extra else [],
         name="home_sum",
         vmem_mib=16,
     )[0]
+
+
+def assemble_one_kernel(core_ref, own_ref, other_ref, gate_out, out_out, whole):
+    quads, rows, _ = own_ref.shape
+    block = rows // 2
+    for quad in range(quads):
+        for ref, who in ((own_ref, core_ref[0]), (other_ref, 1 - core_ref[0])):
+            start = pl.multiple_of((quad * 2 + who) * block, block)
+            gate_out[pl.ds(start, block), :] = ref[quad, :block].astype(F32)
+            whole[pl.ds(start, block), :] = ref[quad, block:].astype(F32)
+    out_out[...] = whole[...].T
+
+
+def assemble_one(core, own, other):
+    quads, rows, width = own.shape
+    model = quads * rows
+    return launch(
+        assemble_one_kernel,
+        [core, own, other],
+        [smem(), vmem(), vmem()],
+        0.1,
+        out_shape=[
+            jax.ShapeDtypeStruct((model, width), F32),
+            jax.ShapeDtypeStruct((width, model), F32),
+        ],
+        out_specs=[vmem()] * 2,
+        scratch_shapes=[pltpu.VMEM((model, width), F32)],
+        name="assemble_one",
+        vmem_mib=16,
+    )
 
 
 def assemble_kernel(
@@ -1070,8 +1117,6 @@
     own_ref,
     other_ref,
     decay_ref,
-    gate_out,
-    out_out,
     input_out,
     recall_out,
     admit_out,
@@ -1083,22 +1128,29 @@
     mean_out,
     gain_one_out,
     gain_two_out,
-    whole,
-    small,
+    *rest,
 ):
-    quads, rows, _ = own_ref.shape
-    model = gate_out.shape[0]
+    *grads_out, small = rest
+    quads, rows, width = other_ref.shape
+    piece, hidden = grads_out[0].shape
+    parts = hidden // (quads * width)
+    for quad in range(quads):
+        for part in range(3):
+            for i in range(parts):
+                start = rows + (part * parts + i) * piece
+                first = (quad * parts + i) * width
+                grads_out[part][:, first : first + width] = own_ref[
+                    quad, start : start + piece
+                ].astype(F32)
+    model = input_out.shape[0]
     block = model // (2 * quads)
     extra = TABLE // (2 * quads)
     for quad in range(quads):
         for ref, who in ((own_ref, core_ref[0]), (other_ref, 1 - core_ref[0])):
             start = pl.multiple_of((quad * 2 + who) * block, block)
-            gate_out[pl.ds(start, block), :] = ref[quad, :block].astype(F32)
-            whole[pl.ds(start, block), :] = ref[quad, block : 2 * block].astype(F32)
-            input_out[pl.ds(start, block), :] = ref[quad, 2 * block : 3 * block].astype(F32)
+            input_out[pl.ds(start, block), :] = ref[quad, :block].astype(F32)
             start = pl.multiple_of((quad * 2 + who) * extra, extra)
-            small[pl.ds(start, extra), :] = ref[quad, 3 * block : 3 * block + extra].astype(F32)
-    out_out[...] = whole[...].T
+            small[pl.ds(start, extra), :] = ref[quad, block : block + extra].astype(F32)
     heads, head, _ = recall_out.shape
     lines = small[2 * head : 2 * head + 16]
     for h in range(heads):
@@ -1115,18 +1167,17 @@
     for ref in (own_ref, other_ref):
         part = None
         for quad in range(quads):
-            value = unpack_gains(ref[quad, 3 * block + extra :], model)
+            value = unpack_gains(ref[quad, block + extra : rows], model)
             part = value if part is None else [a + b for a, b in zip(part, value, strict=True)]
         gains = part if gains is None else [a + b for a, b in zip(gains, part, strict=True)]
     gain_one_out[...] = gains[0].reshape(model)
     gain_two_out[...] = gains[1].reshape(model)
 
 
-def assemble(core, own, other, decay, model, heads, head, rows_total):
+def assemble(core, own, other, decay, model, heads, head, rows_total, piece):
     width = own.shape[2]
+    hidden = own.shape[0] * (own.shape[1] - other.shape[1]) * width // (3 * piece)
     shapes = [
-        (model, width),
-        (width, model),
         (model, width),
         (heads, head, head),
         (heads, head, head),
@@ -1138,6 +1189,9 @@
         (width,),
         (model,),
         (model,),
+        (piece, hidden),
+        (piece, hidden),
+        (piece, hidden),
     ]
     return launch(
         functools.partial(assemble_kernel, rows_total),
@@ -1146,7 +1200,7 @@
         0.1,
         out_shape=[jax.ShapeDtypeStruct(shape, F32) for shape in shapes],
         out_specs=[vmem()] * len(shapes),
-        scratch_shapes=[pltpu.VMEM((model, width), F32), pltpu.VMEM((TABLE, width), F32)],
+        scratch_shapes=[pltpu.VMEM((TABLE, width), F32)],
         name="assemble",
         vmem_mib=16,
     )
@@ -1308,25 +1362,28 @@
         quad_one, core_one, mlp_weights, cots, seconds, gate_grads, up_grads, hiddens, shards
     )
     results = lax.all_to_all(results, "quad", 0, 0, tiled=True)
+    block_out = (middle + jnp.sum(results.astype(F32), axis=0)).astype(BF16)
     middle_grad, branch_grad, gain_two, *made, own_grads, other_grads = middle_back(
         backs, middle, cotangent, mlp_gain, core_one, group, [], [own_grads, other_grads]
     )
 
-    def reduce(chip):
-        return jnp.sum(lax.all_to_all(chip, "quad", 0, 0, tiled=True).astype(F32), axis=0)
+    def spread(chip):
+        return lax.all_to_all(chip, "quad", 0, 0, tiled=True)
+
+    def add_up(arrived):
+        return jnp.sum(arrived.astype(F32), axis=0)
 
     grad_own, grad_other = halves(branch_grad, made)
-    block_out = (middle + jnp.sum(results.astype(F32), axis=0)).astype(BF16)
-    gate_back, adj, edge_back, own_grads = adjoint(
-        branch_grad, weights, gated, scan, kept, carry, mask, vec, [own_grads]
+    gate_back, adj, edge_back = adjoint(
+        branch_grad, weights, gated, scan, kept, carry, mask, vec, []
     )
     edges_back = [along(edge_back, -(i + 1)) for i in range(depth)]
     (chip_one,) = outer(
         core_one,
         quads,
         [
-            normed_own[HALO:],
-            normed_other[HALO:],
+            normed_own,
+            normed_other,
             gate_back,
             swap(gate_back),
             grad_own,
@@ -1334,15 +1391,15 @@
             branch_in,
             branch_in_other,
         ],
-        after=[*edges_back, results],
-    )
-    grads = add_pair(own_grads, swap(other_grads))
+    )
+    (chip_one,) = fence([chip_one], [*edges_back, results])
+    grads = add_pair(own_grads, swap(other_grads), edges_back)
     grads = lax.psum_scatter(grads, "chan", scatter_dimension=0)
 
     def home(totals):
         return [totals[0]] + [along(totals[s].astype(BF16), -s) for s in range(1, shards)]
 
-    sum_one = reduce(chip_one)
+    arrived_one = spread(chip_one)
     input_back, small, normed_grad = mix_back(
         weights, inputs, gate_back, kept, scan, adj, carry, mask, gates, vec, edge, edges_back, ahead,
         [chip_one],
@@ -1358,23 +1415,25 @@
         quads,
         [normed_own, normed_other, input_back, swap(input_back)],
         [small, swap(small)],
-        [sum_one, lines],
-    )
-    home_one = home(sum_one)
+    )
+    (chip_two,) = fence([chip_two], [arrived_one])
     extra = lines.shape[0]
-    totals = reduce(chip_two)
-    totals, grads = fence([totals, grads], home_one[1:])
-    grads = lax.all_to_all(grads, "quad", 0, 0, tiled=True)
-    grads = grads.transpose(1, 2, 0, 3).reshape(3, piece, hidden_width).astype(F32)
+    totals = add_up(spread(chip_two))
+    one = home_sum(place.reshape(1), [home(add_up(arrived_one))], 0)
+    (one,) = fence([one], [totals, lines])
+    own_one = share(one)
     totals = jnp.concatenate(
         [totals, jnp.broadcast_to(lines.astype(F32)[None], (shards, extra, width))], axis=1
     )
-    everything = home_sum(place.reshape(1), [home_one, home(totals)], extra)
-    (everything,) = fence([everything], [grads])
-    own = share(everything)
+    parts = own_width // width
+    grads = grads.reshape(quads, 3, piece, parts, width).transpose(0, 1, 3, 2, 4)
+    grads = grads.reshape(quads, 3 * parts * piece, width)
+    two = home_sum(place.reshape(1), [home(totals)], extra, grads, [own_one, block_out])
+    own_two = lax.all_to_all(two, "quad", 0, 0, tiled=True)
+    size = totals.shape[1]
+    grad_gate, grad_out = assemble_one(core_one, own_one, swap(own_one))
+    (own_two,) = fence([own_two], [grad_gate])
     (
-        grad_gate,
-        grad_out,
         grad_input,
         grad_recall,
         grad_admit,
@@ -1386,10 +1445,18 @@
         gate_mean,
         gain_one,
         gain_two,
+        *grads,
     ) = assemble(
-        core_one, own, swap(own), decay_param, model, heads, head, count * group * shards
-    )
-
+        core_one,
+        own_two,
+        swap(own_two[:, :size]),
+        decay_param,
+        model,
+        heads,
+        head,
+        count * group * shards,
+        piece,
+    )
     return (
         block_out,
         grad_tokens,

time: 362 us -> 343 us (0.948)
  blocking collectives: 20.1 us -> 0 us
  starting transfers between devices: 70.8 us -> 78.1 us
  local copies, waits for them, and re-layouts: 32.6 us -> 28.3 us
    all_to_all x1 -> x0, blocking collectives: 20.1 us -> none  [share(): return lax.all_to_all(every, 'quad', 0, 0, tiled=True)]
    all_to_all x3 -> x4, waiting for transfers between devices: 33.4 us -> 15.6 us  [the longest x1 8.99 us: on_device(): own_two = lax.all_to_all(two, 'quad', 0, 0, tiled=True)]
    unnamed x136 -> x141, local copies, waits for them, and re-layouts: 27.7 us -> 20.3 us
    ppermute x12 -> x13, waiting for transfers between devices: 2.73 us -> 9.13 us  [swap(): return lax.ppermute(values, 'core', [(0, 1), (1, 0)])]
    all_to_all x1, waiting for transfers between devices: 0.01 us -> 4.91 us  [on_device(): results = lax.all_to_all(results, 'quad', 0, 0, tiled=True)]
    ppermute x17, waiting for transfers between devices: 25.1 us -> 29.7 us  [along(): lax.ppermute(values, 'chan', [(i, (i + shift) % shards) for i in range(sh...]
    ppermute x17, starting transfers between devices: 16.1 us -> 19.7 us  [along(): lax.ppermute(values, 'chan', [(i, (i + shift) % shards) for i in range(sh...]
    all_to_all x3 -> x4, starting transfers between devices: 13.5 us -> 16.6 us  [the longest x2 9.36 us: spread(): return lax.all_to_all(chip, 'quad', 0, 0, tiled=True)]
  transfers between devices with their start and end apart: 54 -> 56, of which waited for: 21 -> 25; matrix products, arithmetic and copies ran while one was open for 5% -> 5% of each run, Pallas kernels for 27% -> 30%
where the time goes in v3:
time: 343 us; the launch traced here: 337 us
  Pallas kernels  104 us (30%)
  waiting for transfers between devices  101 us (29%)
  starting transfers between devices  78.1 us (23%)
  local copies, waits for them, and re-layouts  28.3 us (8%)
  between operations  15.4 us (4%)
  other arithmetic  10.5 us (3%)
    pallas_call x35, Pallas kernels, launch(): pl.pallas_call(body, out_shape=list(out_shape) + [jax.ShapeDtypeStruct(c....  104 us
    ppermute x18, waiting for transfers between devices, hop(): return lax.ppermute(values, 'quad', [(i, i ^ rel) for i in range(quads)])  41.6 us
    ppermute x17, waiting for transfers between devices, along(): lax.ppermute(values, 'chan', [(i, (i + shift) % shards) for i in range(sh...  29.7 us
    unnamed x141, local copies, waits for them, and re-layouts  20.3 us
    ppermute x17, starting transfers between devices, along(): lax.ppermute(values, 'chan', [(i, (i + shift) % shards) for i in range(sh...  19.7 us
    ppermute x18, starting transfers between devices, hop(): return lax.ppermute(values, 'quad', [(i, i ^ rel) for i in range(quads)])  18 us
    ppermute x13, starting transfers between devices, swap(): return lax.ppermute(values, 'core', [(0, 1), (1, 0)])  15 us
    all_to_all x2, starting transfers between devices, spread(): return lax.all_to_all(chip, 'quad', 0, 0, tiled=True)  9.36 us
  transfers between devices with their start and end apart: 56, of which 25 were waited for; matrix products, arithmetic and copies ran while one was open for 5% of the time, Pallas kernels for 30%

profile of v3, /device:TPU:17, one launch (start us, length us, event | category | flops | bytes accessed | tf_op | source)
XLA Modules:
  0.0 337.2 jit_solution(15934133729822126896)
XLA Ops:
  33.6 6.3 %mix_local.4 = (bf16[4,3,1024,384]{3,2,1,0:T(8,128)(2,1)}, bf16[4,272,384]{2,1,0:T(8,128)(2,1)}, bf16[4,256,384]{2,1,0:T(8,128)(2,1)}, f32[4,3,256,384]{3,2,1,0:...) custom-call(s32[8]{0:T(128)} %pad_add_fusion.1.refs_0_, ...), custom_call_target="tpu_custom_call" | custom-call | flops 1880999936 | bytes 5985000 | tf_op jit(solution)/shard_map/mix_local/pallas_call | solution.py:152
  39.9 5.3 %collective-permute-done.7.refs_3_ = bf16[1,416,384]{2,1,0:T(8,128)(2,1)S(1)} collective-permute-done((bf16[1,416,384]{2,1,0:T(8,128)(2,1)}, bf16[1,416,384]{2,1,0:T(8,128)(2,1)S(1)}, u32[]{:S(2)}, u32[]{:S(2)}) %collective-permute-start.7) | collective-permute-done | bytes 319520 | tf_op jit(solution)/shard_map/ppermute | solution.py:1243
  52.1 5.8 %mix_local.5 = (bf16[4,3,1024,384]{3,2,1,0:T(8,128)(2,1)}, bf16[4,272,384]{2,1,0:T(8,128)(2,1)}, bf16[4,256,384]{2,1,0:T(8,128)(2,1)}, f32[4,3,256,384]{3,2,1,0:...) custom-call(s32[8]{0:T(128)} %pad_add_fusion.1.refs_0_, ...), custom_call_target="tpu_custom_call", output_to_operand_aliasing={{0}: (5, {}), {1}: (6, {}), {2}: (7, {}), {3}: (8, {}), {4}... | custom-call | flops 1880999936 | bytes 5985000 | tf_op jit(solution)/shard_map/mix_local/pallas_call | solution.py:152
  57.9 5.9 %collective-permute-done.10.refs_2_ = bf16[1,416,384]{2,1,0:T(8,128)(2,1)S(1)} collective-permute-done((bf16[1,416,384]{2,1,0:T(8,128)(2,1)S(1)}, bf16[1,416,384]{2,1,0:T(8,128)(2,1)S(1)}, u32[]{:S(2)}, u32[]{:S(2)}) %collective-permute-start.10) | collective-permute-done | bytes 319520 | tf_op jit(solution)/shard_map/ppermute | solution.py:1243
  71.5 5.7 %mix_local.6 = (bf16[4,3,1024,384]{3,2,1,0:T(8,128)(2,1)}, bf16[4,272,384]{2,1,0:T(8,128)(2,1)}, bf16[4,256,384]{2,1,0:T(8,128)(2,1)}, f32[4,3,256,384]{3,2,1,0:...) custom-call(s32[8]{0:T(128)} %pad_add_fusion.1.refs_0_, ...), custom_call_target="tpu_custom_call", output_to_operand_aliasing={{0}: (5, {}), {1}: (6, {}), {2}: (7, {}), {3}: (8, {}), {4}... | custom-call | flops 1880999936 | bytes 5985000 | tf_op jit(solution)/shard_map/mix_local/pallas_call | solution.py:152
  77.3 6.4 %collective-permute-done.16.refs_3_ = bf16[1,416,384]{2,1,0:T(8,128)(2,1)S(1)} collective-permute-done((bf16[1,416,384]{2,1,0:T(8,128)(2,1)S(1)}, bf16[1,416,384]{2,1,0:T(8,128)(2,1)S(1)}, u32[]{:S(2)}, u32[]{:S(2)}) %collective-permute-start.16) | collective-permute-done | bytes 319520 | tf_op jit(solution)/shard_map/ppermute | solution.py:1243
  89.2 5.8 %mix_local.7 = (bf16[4,3,1024,384]{3,2,1,0:T(8,128)(2,1)}, bf16[4,272,384]{2,1,0:T(8,128)(2,1)}, bf16[4,256,384]{2,1,0:T(8,128)(2,1)}, f32[4,3,256,384]{3,2,1,0:...) custom-call(s32[8]{0:T(128)} %pad_add_fusion.1.refs_0_, ...), custom_call_target="tpu_custom_call", output_to_operand_aliasing={{0}: (5, {}), {1}: (6, {}), {2}: (7, {}), {3}: (8, {}), {4}... | custom-call | flops 1880999936 | bytes 5985000 | tf_op jit(solution)/shard_map/mix_local/pallas_call | solution.py:152
  95.0 5.0 %collective-permute-done.19.refs_0_.refs_1_.refs_6_ = bf16[256,1024]{1,0:T(8,128)(2,1)S(1)} collective-permute-done((bf16[256,1024]{1,0:T(8,128)(2,1)S(1)}, bf16[256,1024]{1,0:T(8,128)(2,1)S(1)}, u32[]{:S(2)}, u32[]{:S(2)}) %collective-permute-start.19) | collective-permute-done | bytes 524320 | tf_op jit(solution)/shard_map/ppermute | solution.py:1243
  110.5 7.1 %mix_branch.1 = (f32[4,8,384]{2,1,0:T(8,128)}, bf16[4,256,384]{2,1,0:T(8,128)(2,1)}, f32[256,1024]{1,0:T(8,128)}, bf16[256,1024]{1,0:T(8,128)(2,1)}, bf16[256,1024]{1,0:T(8,128)(2,1)}) custom-call(f32[4,2,256,384]{3,2,1,0:T(8,128)} %get-tuple-element.153.refs_0_.refs_3_.refs_5_, bf16[4,256,384]{2,1,0:T(8,128)(2,1)} %get-tuple-element.154.refs_1_.refs_2_, ...), custom_call_target="tpu_custom_call" | custom-call | flops 33000000 | bytes 105000 | tf_op jit(solution)/shard_map/mix_branch/pallas_call | solution.py:152
  138.6 4.6 %collective-permute-done.27.refs_0_.refs_10_ = bf16[256,1024]{1,0:T(8,128)(2,1)S(1)} collective-permute-done((bf16[256,1024]{1,0:T(8,128)(2,1)S(1)}, bf16[256,1024]{1,0:T(8,128)(2,1)S(1)}, u32[]{:S(2)}, u32[]{:S(2)}) %collective-permute-start.27) | collective-permute-done | bytes 524320 | tf_op jit(solution)/shard_map/ppermute | solution.py:1243
  147.7 8.8 %mlp_grads.1 = (bf16[4,4,3,32,768]{4,3,2,1,0:T(8,128)(2,1)S(1)}, bf16[4,4,3,32,768]{4,3,2,1,0:T(8,128)(2,1)}, bf16[4,256,1024]{2,1,0:T(8,128)(2,1)S(1)}) custom-call(s32[1]{0:T(128)} %bitcast.12.refs_0_, s32[1]{0:T(128)} %bitcast.4.refs_0_.refs_1_.refs_7_, bf16[3,1024,768]{2,1,0:T(8,128)(2,1)S(1)} %mlp_arrange.1.refs_2_, bf16[256,1024]{1,0:T(8,128)(2,1)S(1)} %copy-done.13, ...), custom_call_target="tpu_custom_call" | custom-call | flops 4950000128 | bytes 15750000 | tf_op jit(solution)/shard_map/mlp_grads/pallas_call | solution.py:152
  156.5 9.2 %collective-permute-done.30.refs_3_ = bf16[256,1024]{1,0:T(8,128)(2,1)S(1)} collective-permute-done((bf16[256,1024]{1,0:T(8,128)(2,1)S(1)}, bf16[256,1024]{1,0:T(8,128)(2,1)S(1)}, u32[]{:S(2)}, u32[]{:S(2)}) %collective-permute-start.30) | collective-permute-done | bytes 524320 | tf_op jit(solution)/shard_map/ppermute | solution.py:1243
  173.6 4.5 %all-to-all-start.1 = ((bf16[4,256,1024]{2,1,0:T(8,128)(2,1)}), bf16[4,256,1024]{2,1,0:T(8,128)(2,1)}, u32[]{:S(2)}, u32[]{:S(2)}) async-start(bf16[4,256,1024]{2,1,0:T(8,128)(2,1)} %copy-done.11), calls=%async_computation.1 | async-start | bytes 4194304 | tf_op jit(solution)/shard_map/all_to_all | solution.py:1364
  178.0 8.8 %mix_adjoint.1 = (bf16[4,256,384]{2,1,0:T(8,128)(2,1)}, f32[4,2,256,384]{3,2,1,0:T(8,128)}, f32[4,8,384]{2,1,0:T(8,128)}) custom-call(bf16[256,1024]{1,0:T(8,128)(2,1)} %copy-done.27, bf16[4,3,1024,384]{3,2,1,0:T(8,128)(2,1)} %get-tuple-element.155.refs_2_.refs_1_.refs_0_, bf16[4,256,384]{2,1,0:T(8,128)(2,1)} %get-tuple-element.154.refs_1_.refs_2_, ...), custom_call_target="tpu_custom_call" | custom-call | flops 33000000 | bytes 105000 | tf_op jit(solution)/shard_map/mix_adjoint/pallas_call | solution.py:152
  191.9 6.2 %mix_outer.2.refs_4_ = bf16[4,4,256,384]{3,2,1,0:T(8,128)(2,1)} custom-call(s32[1]{0:T(128)} %bitcast.4.refs_0_.refs_1_.refs_7_, bf16[272,512]{1,0:T(8,128)(2,1)} %copy-done.21, bf16[272,512]{1,0:T(8,128)(2,1)} %copy-done.59, bf16[4,256,384]{2,1,0:T(8,128)(2,1)} %get-tuple-element.188.refs_3_, bf16[4,256,384]{2,1,0:T(8,128)(2,1)} %collective-permute-done.34.refs_4_, ...), custom_call_target="tpu_custom_call" | custom-call | flops 33000000 | bytes 105000 | tf_op jit(solution)/shard_map/mix_outer/pallas_call | solution.py:152
  198.2 4.9 %all-to-all-done.1.refs_3_ = bf16[4,256,1024]{2,1,0:T(8,128)(2,1)} async-done(((bf16[4,256,1024]{2,1,0:T(8,128)(2,1)}), bf16[4,256,1024]{2,1,0:T(8,128)(2,1)}, u32[]{:S(2)}, u32[]{:S(2)}) %all-to-all-start.1) | async-done | bytes 2097184 | tf_op jit(solution)/shard_map/all_to_all | solution.py:1364
  203.2 4.8 %all-to-all-start.2 = ((bf16[4,4,256,384]{3,2,1,0:T(8,128)(2,1)}), bf16[4,4,256,384]{3,2,1,0:T(8,128)(2,1)}, u32[]{:S(2)}, u32[]{:S(2)}) async-start(bf16[4,4,256,384]{3,2,1,0:T(8,128)(2,1)} %fence.12.refs_17_), calls=%async_computation.2 | async-start | bytes 6291456 | tf_op jit(solution)/shard_map/all_to_all | solution.py:1371
  211.7 14.1 %mix_back.1 = (bf16[4,272,384]{2,1,0:T(8,128)(2,1)}, bf16[4,256,384]{2,1,0:T(8,128)(2,1)}, f32[272,1024]{1,0:T(8,128)}) custom-call(bf16[4,3,1024,384]{3,2,1,0:T(8,128)(2,1)} %get-tuple-element.155.refs_2_.refs_1_.refs_0_, bf16[4,3,1024,384]{3,2,1,0:T(8,128)(2,1)} %get-tuple-element.155.refs_2_.refs_1_.refs_0_, ...), custom_call_target="tpu_custom_call" | custom-call | flops 33000000 | bytes 105000 | tf_op jit(solution)/shard_map/mix_back/pallas_call | solution.py:152
  231.7 5.3 %mix_outer.3.refs_1_ = bf16[4,4,160,384]{3,2,1,0:T(8,128)(2,1)} custom-call(s32[1]{0:T(128)} %bitcast.4.refs_0_.refs_1_.refs_7_, bf16[272,512]{1,0:T(8,128)(2,1)} %copy-done.21, bf16[272,512]{1,0:T(8,128)(2,1)} %copy-done.59, bf16[4,272,384]{2,1,0:T(8,128)(2,1)} %get-tuple-element.199.refs_3_, bf16[4,272,384]{2,1,0:T(8,128)(2,1)} %copy-done.62, ...), custom_call_target="tpu_custom_call" | custom-call | flops 33000000 | bytes 105000 | tf_op jit(solution)/shard_map/mix_outer/pallas_call | solution.py:152
  237.0 6.6 %all-to-all-done.2.refs_0_ = bf16[4,4,256,384]{3,2,1,0:T(8,128)(2,1)} async-done(((bf16[4,4,256,384]{3,2,1,0:T(8,128)(2,1)}), bf16[4,4,256,384]{3,2,1,0:T(8,128)(2,1)}, u32[]{:S(2)}, u32[]{:S(2)}) %all-to-all-start.2) | async-done | bytes 3145760 | tf_op jit(solution)/shard_map/all_to_all | solution.py:1371
  243.6 4.6 %all-to-all-start.3 = ((bf16[4,4,160,384]{3,2,1,0:T(8,128)(2,1)}), bf16[4,4,160,384]{3,2,1,0:T(8,128)(2,1)}, u32[]{:S(2)}, u32[]{:S(2)}) async-start(bf16[4,4,160,384]{3,2,1,0:T(8,128)(2,1)} %fence.13), calls=%async_computation.3 | async-start | bytes 3932160 | tf_op jit(solution)/shard_map/all_to_all | solution.py:1371
  264.6 11.6 %collective-permute-done.40.refs_3_ = bf16[256,384]{1,0:T(8,128)(2,1)S(1)} collective-permute-done((bf16[256,384]{1,0:T(8,128)(2,1)S(1)}, bf16[256,384]{1,0:T(8,128)(2,1)S(1)}, u32[]{:S(2)}, u32[]{:S(2)}) %collective-permute-start.40) | collective-permute-done | bytes 196640 | tf_op jit(solution)/shard_map/ppermute | solution.py:1249
  295.7 7.0 %collective-permute-done.45.refs_4_ = bf16[176,384]{1,0:T(8,128)(2,1)S(1)} collective-permute-done((bf16[176,384]{1,0:T(8,128)(2,1)S(1)}, bf16[176,384]{1,0:T(8,128)(2,1)S(1)}, u32[]{:S(2)}, u32[]{:S(2)}) %collective-permute-start.45) | collective-permute-done | bytes 135200 | tf_op jit(solution)/shard_map/ppermute | solution.py:1249
  312.5 9.0 %all-to-all-done.5.refs_1_ = bf16[4,368,384]{2,1,0:T(8,128)(2,1)S(1)} async-done(((bf16[4,368,384]{2,1,0:T(8,128)(2,1)}), bf16[4,368,384]{2,1,0:T(8,128)(2,1)S(1)}, u32[]{:S(2)}, u32[]{:S(2)}) %all-to-all-start.5) | async-done | bytes 1130528 | tf_op jit(solution)/shard_map/all_to_all | solution.py:1432
  (298 shorter events, 158.5 us)
Async XLA Ops:
  7.2 18.9 %collective-permute-start.2 = (bf16[256,1024]{1,0:T(8,128)(2,1)}, bf16[256,1024]{1,0:T(8,128)(2,1)S(1)}, u32[]{:S(2)}, u32[]{:S(2)}) collective-permute-start(bf16[256,1024]{1,0:T(8,128)(2,1)} %refs_5_.4), channel_id=1, source_target_pairs={{0,8},{8,0},{16,24},{24,16},{1,9},{9,1},{17,25},{25,17},{2,10},{10... | collective-permute-start | bytes 1572872 | tf_op jit(solution)/shard_map/ppermute | solution.py:1243
  8.5 17.7 %collective-permute-start.3 = (bf16[256,1024]{1,0:T(8,128)(2,1)}, bf16[256,1024]{1,0:T(8,128)(2,1)S(1)}, u32[]{:S(2)}, u32[]{:S(2)}) collective-permute-start(bf16[256,1024]{1,0:T(8,128)(2,1)} %refs_5_.4), channel_id=1, source_target_pairs={{0,16},{8,24},{16,0},{24,8},{1,17},{9,25},{17,1},{25,9},{2,18},{10... | collective-permute-start | bytes 1572872 | tf_op jit(solution)/shard_map/ppermute | solution.py:1243
  16.9 22.9 %all-to-all-start = ((bf16[4,3,32,768]{3,2,1,0:T(8,128)(2,1)}), bf16[4,3,32,768]{3,2,1,0:T(8,128)(2,1)}, u32[]{:S(2)}, u32[]{:S(2)}) async-start(bf16[4,3,32,768]{3,2,1,0:T(8,128)(2,1)} %fence.9), calls=%async_computation | async-start | bytes 1179648 | tf_op jit(solution)/shard_map/all_to_all | solution.py:1310
  21.2 83.5 %all-gather.3.cloned.1.call-start = ((), (), s32[]{:S(2)}) async-start(), calls=%async_computation.8 | async-start | bytes 2949120 | tf_op jit(solution)/shard_map/all_gather | solution.py:1325
  30.8 14.4 %collective-permute-start.7 = (bf16[1,416,384]{2,1,0:T(8,128)(2,1)}, bf16[1,416,384]{2,1,0:T(8,128)(2,1)S(1)}, u32[]{:S(2)}, u32[]{:S(2)}) collective-permute-start(bf16[1,416,384]{2,1,0:T(8,128)(2,1)} %fence.8.refs_0_), channel_id=1, source_target_pairs={{0,24},{8,16},{16,8},{24,0},{1,25},{9,17},{17,9},{25,1},{2,26},{10... | collective-permute-start | bytes 958472 | tf_op jit(solution)/shard_map/ppermute | solution.py:1243
  30.8 14.4 %collective-permute-start.8 = (bf16[1,416,384]{2,1,0:T(8,128)(2,1)}, bf16[1,416,384]{2,1,0:T(8,128)(2,1)S(1)}, u32[]{:S(2)}, u32[]{:S(2)}) collective-permute-start(bf16[1,416,384]{2,1,0:T(8,128)(2,1)} %fence.8.refs_0_), channel_id=1, source_target_pairs={{0,1},{1,2},{2,3},{3,0},{4,5},{5,6},{6,7},{7,4},{8,9},{9,10},{10,1... | collective-permute-start | bytes 958472 | tf_op jit(solution)/shard_map/ppermute | solution.py:1249
  47.6 16.2 %collective-permute-start.10 = (bf16[1,416,384]{2,1,0:T(8,128)(2,1)S(1)}, bf16[1,416,384]{2,1,0:T(8,128)(2,1)S(1)}, u32[]{:S(2)}, u32[]{:S(2)}) collective-permute-start(bf16[1,416,384]{2,1,0:T(8,128)(2,1)S(1)} %get-tuple-element.125.refs_0_), channel_id=1, source_target_pairs={{0,16},{8,24},{16,0},{24,8},{1,17},{9,25},{17,1},{25,9},{2,18},{10... | collective-permute-start | bytes 958472 | tf_op jit(solution)/shard_map/ppermute | solution.py:1243
  48.9 14.9 %collective-permute-start.11 = (bf16[1,416,384]{2,1,0:T(8,128)(2,1)S(1)}, bf16[1,416,384]{2,1,0:T(8,128)(2,1)S(1)}, u32[]{:S(2)}, u32[]{:S(2)}) collective-permute-start(bf16[1,416,384]{2,1,0:T(8,128)(2,1)S(1)} %get-tuple-element.125.refs_0_), channel_id=1, source_target_pairs={{0,24},{8,16},{16,8},{24,0},{1,25},{9,17},{17,9},{25,1},{2,26},{10... | collective-permute-start | bytes 958472 | tf_op jit(solution)/shard_map/ppermute | solution.py:1243
  68.2 15.5 %collective-permute-start.16 = (bf16[1,416,384]{2,1,0:T(8,128)(2,1)S(1)}, bf16[1,416,384]{2,1,0:T(8,128)(2,1)S(1)}, u32[]{:S(2)}, u32[]{:S(2)}) collective-permute-start(bf16[1,416,384]{2,1,0:T(8,128)(2,1)S(1)} %get-tuple-element.135.refs_0_), channel_id=1, source_target_pairs={{0,24},{8,16},{16,8},{24,0},{1,25},{9,17},{17,9},{25,1},{2,26},{10... | collective-permute-start | bytes 958472 | tf_op jit(solution)/shard_map/ppermute | solution.py:1243
  85.6 14.4 %collective-permute-start.19 = (bf16[256,1024]{1,0:T(8,128)(2,1)S(1)}, bf16[256,1024]{1,0:T(8,128)(2,1)S(1)}, u32[]{:S(2)}, u32[]{:S(2)}) collective-permute-start(bf16[256,1024]{1,0:T(8,128)(2,1)S(1)} %get-tuple-element.156), channel_id=1, source_target_pairs={{0,24},{8,16},{16,8},{24,0},{1,25},{9,17},{17,9},{25,1},{2,26},{10... | collective-permute-start | bytes 1572872 | tf_op jit(solution)/shard_map/ppermute | solution.py:1243
  119.2 16.3 %collective-permute-start.25 = (bf16[256,1024]{1,0:T(8,128)(2,1)}, bf16[256,1024]{1,0:T(8,128)(2,1)S(1)}, u32[]{:S(2)}, u32[]{:S(2)}) collective-permute-start(bf16[256,1024]{1,0:T(8,128)(2,1)} %get-tuple-element.160.refs_3_.refs_0_.refs_7_), channel_id=1, source_target_pairs={{0,16},{8,24},{16,0},{24,8},{1,17},{9,25},{17,1},{25,9},{2,18},{10... | collective-permute-start | bytes 1572872 | tf_op jit(solution)/shard_map/ppermute | solution.py:1243
  125.4 17.7 %collective-permute-start.27 = (bf16[256,1024]{1,0:T(8,128)(2,1)S(1)}, bf16[256,1024]{1,0:T(8,128)(2,1)S(1)}, u32[]{:S(2)}, u32[]{:S(2)}) collective-permute-start(bf16[256,1024]{1,0:T(8,128)(2,1)S(1)} %get-tuple-element.163), channel_id=1, source_target_pairs={{0,24},{8,16},{16,8},{24,0},{1,25},{9,17},{17,9},{25,1},{2,26},{10... | collective-permute-start | bytes 1572872 | tf_op jit(solution)/shard_map/ppermute | solution.py:1243
  134.0 22.5 %collective-permute-start.28 = (bf16[256,1024]{1,0:T(8,128)(2,1)S(1)}, bf16[256,1024]{1,0:T(8,128)(2,1)S(1)}, u32[]{:S(2)}, u32[]{:S(2)}) collective-permute-start(bf16[256,1024]{1,0:T(8,128)(2,1)S(1)} %get-tuple-element.167.refs_3_), channel_id=1, source_target_pairs={{0,8},{8,0},{16,24},{24,16},{1,9},{9,1},{17,25},{25,17},{2,10},{10... | collective-permute-start | bytes 1572872 | tf_op jit(solution)/shard_map/ppermute | solution.py:1243
  138.5 18.0 %collective-permute-start.29 = (bf16[256,1024]{1,0:T(8,128)(2,1)S(1)}, bf16[256,1024]{1,0:T(8,128)(2,1)S(1)}, u32[]{:S(2)}, u32[]{:S(2)}) collective-permute-start(bf16[256,1024]{1,0:T(8,128)(2,1)S(1)} %get-tuple-element.169.refs_3_), channel_id=1, source_target_pairs={{0,16},{8,24},{16,0},{24,8},{1,17},{9,25},{17,1},{25,9},{2,18},{10... | collective-permute-start | bytes 1572872 | tf_op jit(solution)/shard_map/ppermute | solution.py:1243
  146.2 19.6 %collective-permute-start.30 = (bf16[256,1024]{1,0:T(8,128)(2,1)S(1)}, bf16[256,1024]{1,0:T(8,128)(2,1)S(1)}, u32[]{:S(2)}, u32[]{:S(2)}) collective-permute-start(bf16[256,1024]{1,0:T(8,128)(2,1)S(1)} %get-tuple-element.181), channel_id=1, source_target_pairs={{0,24},{8,16},{16,8},{24,0},{1,25},{9,17},{17,9},{25,1},{2,26},{10... | collective-permute-start | bytes 1572872 | tf_op jit(solution)/shard_map/ppermute | solution.py:1243
  170.4 37.6 %collective-permute-start.46 = (bf16[4,4,3,32,768]{4,3,2,1,0:T(8,128)(2,1)}, bf16[4,4,3,32,768]{4,3,2,1,0:T(8,128)(2,1)}, u32[]{:S(2)}, u32[]{:S(2)}) collective-permute-start(bf16[4,4,3,32,768]{4,3,2,1,0:T(8,128)(2,1)} %get-tuple-element.204), channel_id=1, source_target_pairs={{0,4},{4,0},{1,5},{5,1},{2,6},{6,2},{3,7},{7,3},{8,12},{12,8},{9,1... | collective-permute-start | bytes 7077896 | tf_op jit(solution)/shard_map/ppermute | solution.py:1246
  173.6 29.6 %all-to-all-start.1 = ((bf16[4,256,1024]{2,1,0:T(8,128)(2,1)}), bf16[4,256,1024]{2,1,0:T(8,128)(2,1)}, u32[]{:S(2)}, u32[]{:S(2)}) async-start(bf16[4,256,1024]{2,1,0:T(8,128)(2,1)} %copy-done.11), calls=%async_computation.1 | async-start | bytes 4194304 | tf_op jit(solution)/shard_map/all_to_all | solution.py:1364
  203.2 40.4 %all-to-all-start.2 = ((bf16[4,4,256,384]{3,2,1,0:T(8,128)(2,1)}), bf16[4,4,256,384]{3,2,1,0:T(8,128)(2,1)}, u32[]{:S(2)}, u32[]{:S(2)}) async-start(bf16[4,4,256,384]{3,2,1,0:T(8,128)(2,1)} %fence.12.refs_17_), calls=%async_computation.2 | async-start | bytes 6291456 | tf_op jit(solution)/shard_map/all_to_all | solution.py:1371
  208.0 83.0 %reduce-scatter.2.cloned.1.call-start = ((), (), s32[]{:S(2)}) async-start(), calls=%async_computation.7 | async-start | bytes 2949120 | tf_op jit(solution)/shard_map/reduce_scatter | solution.py:1397
  243.6 36.1 %all-to-all-start.3 = ((bf16[4,4,160,384]{3,2,1,0:T(8,128)(2,1)}), bf16[4,4,160,384]{3,2,1,0:T(8,128)(2,1)}, u32[]{:S(2)}, u32[]{:S(2)}) async-start(bf16[4,4,160,384]{3,2,1,0:T(8,128)(2,1)} %fence.13), calls=%async_computation.3 | async-start | bytes 3932160 | tf_op jit(solution)/shard_map/all_to_all | solution.py:1371
  260.0 16.2 %collective-permute-start.40 = (bf16[256,384]{1,0:T(8,128)(2,1)S(1)}, bf16[256,384]{1,0:T(8,128)(2,1)S(1)}, u32[]{:S(2)}, u32[]{:S(2)}) collective-permute-start(bf16[256,384]{1,0:T(8,128)(2,1)S(1)} %get-tuple-element.223), channel_id=1, source_target_pairs={{0,2},{1,3},{2,0},{3,1},{4,6},{5,7},{6,4},{7,5},{8,10},{9,11},{10,... | collective-permute-start | bytes 589832 | tf_op jit(solution)/shard_map/ppermute | solution.py:1249
  262.5 16.4 %collective-permute-start.41 = (bf16[256,384]{1,0:T(8,128)(2,1)S(1)}, bf16[256,384]{1,0:T(8,128)(2,1)S(1)}, u32[]{:S(2)}, u32[]{:S(2)}) collective-permute-start(bf16[256,384]{1,0:T(8,128)(2,1)S(1)} %get-tuple-element.222), channel_id=1, source_target_pairs={{0,1},{1,2},{2,3},{3,0},{4,5},{5,6},{6,7},{7,4},{8,9},{9,10},{10,1... | collective-permute-start | bytes 589832 | tf_op jit(solution)/shard_map/ppermute | solution.py:1249
  284.5 18.2 %all-to-all-start.4 = ((bf16[4,256,384]{2,1,0:T(8,128)(2,1)}), bf16[4,256,384]{2,1,0:T(8,128)(2,1)S(1)}, u32[]{:S(2)}, u32[]{:S(2)}) async-start(bf16[4,256,384]{2,1,0:T(8,128)(2,1)} %broadcast_in_dim.4), calls=%async_computation.4 | async-start | bytes 1572864 | tf_op jit(solution)/shard_map/all_to_all | solution.py:1253
  303.8 17.7 %all-to-all-start.5 = ((bf16[4,368,384]{2,1,0:T(8,128)(2,1)}), bf16[4,368,384]{2,1,0:T(8,128)(2,1)S(1)}, u32[]{:S(2)}, u32[]{:S(2)}) async-start(bf16[4,368,384]{2,1,0:T(8,128)(2,1)} %home_sum.3), calls=%async_computation.6 | async-start | bytes 2260992 | tf_op jit(solution)/shard_map/all_to_all | solution.py:1432
  (102 other events, 549.1 us)
Sparse Core Ops, SparseCore 0:
  47.7 51.8 all-gather.2
  211.9 50.1 reduce-scatter.1

commit v4 on v3

--- a/solution.py
+++ b/solution.py
@@ -94,20 +94,23 @@
     return a, b
 
 
+def same_block(width, head):
+    row = lax.broadcasted_iota(jnp.int32, (width, 1), 0) // head
+    col = lax.broadcasted_iota(jnp.int32, (1, width), 1) // head
+    return row == col
+
+
 def block_diagonal(flat, head, dtype):
     width = flat.shape[1]
     tall = jnp.concatenate([flat] * (width // head), axis=0)
     shape = (width, width)
-    row = lax.broadcasted_iota(jnp.int32, shape, 0) // head
-    col = lax.broadcasted_iota(jnp.int32, shape, 1) // head
-    return jnp.where(row == col, tall, 0.0).astype(dtype)
+    del shape
+    return jnp.where(same_block(width, head), tall, 0.0).astype(dtype)
 
 
 def fold_diagonal(square, head):
     width = square.shape[0]
-    row = lax.broadcasted_iota(jnp.int32, square.shape, 0) // head
-    col = lax.broadcasted_iota(jnp.int32, square.shape, 1) // head
-    kept = jnp.where(row == col, square, 0.0)
+    kept = jnp.where(same_block(width, head), square, 0.0)
     total = kept[:head]
     for start in range(head, width, head):
         total = total + kept[start : start + head]
@@ -749,13 +752,14 @@
     return both
 
 
-def tokens_back(inside, grad, halo, tokens, gain, middle_grad, gain_two, width):
+def tokens_back(inside, grad, halo, tokens, gain, middle_grad, gain_two, width, after):
     count, model = tokens.shape
     return launch(
         tokens_kernel,
         [inside, grad, halo, tokens, gain.reshape(1, model), middle_grad, gain_two],
         [smem()] + [vmem()] * 6,
         0.1,
+        after,
         out_shape=[
             jax.ShapeDtypeStruct((count, model), F32),
             jax.ShapeDtypeStruct((gain_lines(model, width), width), BF16),
@@ -914,10 +918,11 @@
     speed = STRENGTH * vec[7:8]
     rate = recall * speed
     decay = jnp.exp(-rate)
-    size = jnp.sqrt(one_minus_exp(2.0 * rate))
-    sized = adj * size
+    square = one_minus_exp(2.0 * rate)
+    inverse = lax.rsqrt(square)
+    sized = adj * (square * inverse)
     pulled = adj * admit
-    log_grad = decay * (adj * before * mask_ref[:, 1:2] - pulled * conv * decay / size)
+    log_grad = decay * (adj * before * mask_ref[:, 1:2] - pulled * conv * decay * inverse)
     recall_grad = -speed * log_grad * recall * (1.0 - recall)
     admit_grad = sized * conv * admit * (1.0 - admit)
     conv_grad = sized * admit
@@ -1033,7 +1038,8 @@
             total = refs[0][...].astype(F32)
             for ref in refs[1:]:
                 total = total + ref[...].astype(F32)
-            out[start : start + size] = total.astype(BF16)
+            for quad in range(out.shape[0]):
+                out[quad, start : start + size] = total.astype(BF16)
             start += size
         return
     grads_ref, out, lines = rest
@@ -1058,12 +1064,12 @@
         out[quad, rows:] = grads_ref[quad]
 
 
-def home_sum(place, groups, extra, grads=None, after=()):
+def home_sum(place, groups, extra, grads=None, after=(), quads=1):
     shards = len(groups[0])
     rows = sum(group[0].shape[0] for group in groups)
     width = groups[0][0].shape[1]
     inputs = [place, *[part for group in groups for part in group]]
-    shape = (rows, width)
+    shape = (quads, rows, width)
     if grads is not None:
         inputs.append(grads)
         shape = (grads.shape[0], rows + grads.shape[1], width)
@@ -1330,16 +1336,15 @@
         if s < shards - 1:
             arrived = along(arrived, 1)
     weights, inputs, gated, kept, scan, edge, gates, vec = stacks
-    (edge,) = fence([edge], cots[near:])
+    edge, gathered = fence([edge, gathered], cots[near:])
+    other_gathered = swap(gathered)
     depth = LENGTH // count - 1
     behind = [along(edge, i + 1) for i in range(depth)]
-    (gathered,) = fence([gathered], behind)
     carry, branch_in, middle, second, again = branch(
         scan, gated, weights, tokens, mlp_gain.reshape(1, model), behind, []
     )
-    mlp_weights = arrange(core_one, gathered, swap(gathered), [second])
+    mlp_weights = arrange(core_one, gathered, other_gathered, [second])
     ahead = [along(edge, -(i + 1)) for i in range(depth - 1)]
-    branch_in_other = swap(branch_in)
 
     gate_grads, up_grads, hiddens, backs, seconds = [], [], [], [], []
     for rel in range(quads):
@@ -1349,7 +1354,7 @@
             seconds.append(hop(second if rel < near else again, rel))
         gate_grad, up_grad, hidden, back, *carry_on = mlp_block(
             seconds[rel], cots[rel], mlp_weights,
-            backs[-1:] if rel else [*ahead, branch_in_other], [] if rel else [again],
+            backs[-1:] if rel else [*ahead], [] if rel else [again],
         )
         if rel == 0:
             (again,) = carry_on
@@ -1374,8 +1379,8 @@
         return jnp.sum(arrived.astype(F32), axis=0)
 
     grad_own, grad_other = halves(branch_grad, made)
-    gate_back, adj, edge_back = adjoint(
-        branch_grad, weights, gated, scan, kept, carry, mask, vec, []
+    gate_back, adj, edge_back, branch_in = adjoint(
+        branch_grad, weights, gated, scan, kept, carry, mask, vec, [branch_in]
     )
     edges_back = [along(edge_back, -(i + 1)) for i in range(depth)]
     (chip_one,) = outer(
@@ -1389,11 +1394,11 @@
             grad_own,
             swap(grad_other),
             branch_in,
-            branch_in_other,
+            swap(branch_in),
         ],
     )
-    (chip_one,) = fence([chip_one], [*edges_back, results])
-    grads = add_pair(own_grads, swap(other_grads), edges_back)
+    grads = add_pair(own_grads, swap(other_grads), [*edges_back, chip_one])
+    (chip_one,) = fence([chip_one], [*edges_back, results, grads])
     grads = lax.psum_scatter(grads, "chan", scatter_dimension=0)
 
     def home(totals):
@@ -1405,10 +1410,11 @@
         [chip_one],
     )
 
+    sum_one = add_up(arrived_one)
     halo_grad = along(normed_grad[:HALO].astype(BF16), -1)
     inside = ((place + 1) * count % LENGTH != 0).astype(jnp.int32).reshape(1)
     grad_tokens, lines = tokens_back(
-        inside, normed_grad, halo_grad, tokens, norm_gain, middle_grad, gain_two, width
+        inside, normed_grad, halo_grad, tokens, norm_gain, middle_grad, gain_two, width, [sum_one]
     )
     (chip_two,) = outer(
         core_one,
@@ -1419,20 +1425,20 @@
     (chip_two,) = fence([chip_two], [arrived_one])
     extra = lines.shape[0]
     totals = add_up(spread(chip_two))
-    one = home_sum(place.reshape(1), [home(add_up(arrived_one))], 0)
+    one = home_sum(place.reshape(1), [home(sum_one)], 0, quads=quads)
     (one,) = fence([one], [totals, lines])
-    own_one = share(one)
+    own_one = spread(one)
     totals = jnp.concatenate(
         [totals, jnp.broadcast_to(lines.astype(F32)[None], (shards, extra, width))], axis=1
     )
     parts = own_width // width
     grads = grads.reshape(quads, 3, piece, parts, width).transpose(0, 1, 3, 2, 4)
     grads = grads.reshape(quads, 3 * parts * piece, width)
-    two = home_sum(place.reshape(1), [home(totals)], extra, grads, [own_one, block_out])
+    two = home_sum(place.reshape(1), [home(totals)], extra, grads, [own_one])
     own_two = lax.all_to_all(two, "quad", 0, 0, tiled=True)
     size = totals.shape[1]
     grad_gate, grad_out = assemble_one(core_one, own_one, swap(own_one))
-    (own_two,) = fence([own_two], [grad_gate])
+    (own_two,) = fence([own_two], [grad_gate, block_out])
     (
         grad_input,
         grad_recall,

time: 343 us -> 334 us (0.974)
  waiting for transfers between devices: 101 us -> 93.5 us
    all_to_all x1, waiting for transfers between devices: 4.91 us -> 0.01 us  [on_device(): results = lax.all_to_all(results, 'quad', 0, 0, tiled=True)]
    all_to_all x2 -> x3, waiting for transfers between devices: 6.61 us -> 10.6 us  [spread(): return lax.all_to_all(chip, 'quad', 0, 0, tiled=True)]
    all_to_all x2 -> x3, starting transfers between devices: 9.36 us -> 13.2 us  [spread(): return lax.all_to_all(chip, 'quad', 0, 0, tiled=True)]
    all_to_all x1 -> x0, starting transfers between devices: 3.55 us -> none  [share(): return lax.all_to_all(every, 'quad', 0, 0, tiled=True)]
    unnamed x141 -> x131, local copies, waits for them, and re-layouts: 20.3 us -> 21.1 us
    pallas_call x35 -> x34, Pallas kernels: 104 us -> 103 us  [launch(): pl.pallas_call(body, out_shape=list(out_shape) + [jax.ShapeDtypeStruct(c....]
  transfers between devices with their start and end apart: 56 -> 56, of which waited for: 25 -> 21; matrix products, arithmetic and copies ran while one was open for 5% -> 5% of each run, Pallas kernels for 30% -> 30%
where the time goes in v4:
time: 334 us; the launch traced here: 328 us
  Pallas kernels  103 us (31%)
  waiting for transfers between devices  93.5 us (28%)
  starting transfers between devices  77.8 us (23%)
  local copies, waits for them, and re-layouts  28.1 us (8%)
  between operations  15.3 us (5%)
  other arithmetic  10.3 us (3%)
    pallas_call x34, Pallas kernels, launch(): pl.pallas_call(body, out_shape=list(out_shape) + [jax.ShapeDtypeStruct(c....  103 us
    ppermute x18, waiting for transfers between devices, hop(): return lax.ppermute(values, 'quad', [(i, i ^ rel) for i in range(quads)])  40.8 us
    ppermute x17, waiting for transfers between devices, along(): lax.ppermute(values, 'chan', [(i, (i + shift) % shards) for i in range(sh...  27 us
    unnamed x131, local copies, waits for them, and re-layouts  21.1 us
    ppermute x17, starting transfers between devices, along(): lax.ppermute(values, 'chan', [(i, (i + shift) % shards) for i in range(sh...  19.8 us
    ppermute x18, starting transfers between devices, hop(): return lax.ppermute(values, 'quad', [(i, i ^ rel) for i in range(quads)])  18 us
    ppermute x13, starting transfers between devices, swap(): return lax.ppermute(values, 'core', [(0, 1), (1, 0)])  14.4 us
    all_to_all x3, starting transfers between devices, spread(): return lax.all_to_all(chip, 'quad', 0, 0, tiled=True)  13.2 us
  transfers between devices with their start and end apart: 56, of which 21 were waited for; matrix products, arithmetic and copies ran while one was open for 5% of the time, Pallas kernels for 30%

profile of v4, /device:TPU:17, one launch (start us, length us, event | category | flops | bytes accessed | tf_op | source)
XLA Modules:
  0.0 328.2 jit_solution(3614610516040971690)
XLA Ops:
  16.9 4.3 %all-to-all-start = ((bf16[4,3,32,768]{3,2,1,0:T(8,128)(2,1)}), bf16[4,3,32,768]{3,2,1,0:T(8,128)(2,1)}, u32[]{:S(2)}, u32[]{:S(2)}) async-start(bf16[4,3,32,768]{3,2,1,0:T(8,128)(2,1)} %fence.8), calls=%async_computation | async-start | bytes 1179648 | tf_op jit(solution)/shard_map/all_to_all | solution.py:1316
  33.5 6.3 %mix_local.4 = (bf16[4,3,1024,384]{3,2,1,0:T(8,128)(2,1)}, bf16[4,272,384]{2,1,0:T(8,128)(2,1)}, bf16[4,256,384]{2,1,0:T(8,128)(2,1)}, f32[4,3,256,384]{3,2,1,0:...) custom-call(s32[8]{0:T(128)} %pad_add_fusion.1.refs_0_, ...), custom_call_target="tpu_custom_call" | custom-call | flops 1880999936 | bytes 5985000 | tf_op jit(solution)/shard_map/mix_local/pallas_call | solution.py:155
  39.9 5.2 %collective-permute-done.7.refs_3_ = bf16[1,416,384]{2,1,0:T(8,128)(2,1)S(1)} collective-permute-done((bf16[1,416,384]{2,1,0:T(8,128)(2,1)}, bf16[1,416,384]{2,1,0:T(8,128)(2,1)S(1)}, u32[]{:S(2)}, u32[]{:S(2)}) %collective-permute-start.7) | collective-permute-done | bytes 319520 | tf_op jit(solution)/shard_map/ppermute | solution.py:1249
  52.0 5.8 %mix_local.5 = (bf16[4,3,1024,384]{3,2,1,0:T(8,128)(2,1)}, bf16[4,272,384]{2,1,0:T(8,128)(2,1)}, bf16[4,256,384]{2,1,0:T(8,128)(2,1)}, f32[4,3,256,384]{3,2,1,0:...) custom-call(s32[8]{0:T(128)} %pad_add_fusion.1.refs_0_, ...), custom_call_target="tpu_custom_call", output_to_operand_aliasing={{0}: (5, {}), {1}: (6, {}), {2}: (7, {}), {3}: (8, {}), {4}... | custom-call | flops 1880999936 | bytes 5985000 | tf_op jit(solution)/shard_map/mix_local/pallas_call | solution.py:155
  57.8 5.9 %collective-permute-done.10.refs_2_ = bf16[1,416,384]{2,1,0:T(8,128)(2,1)S(1)} collective-permute-done((bf16[1,416,384]{2,1,0:T(8,128)(2,1)S(1)}, bf16[1,416,384]{2,1,0:T(8,128)(2,1)S(1)}, u32[]{:S(2)}, u32[]{:S(2)}) %collective-permute-start.10) | collective-permute-done | bytes 319520 | tf_op jit(solution)/shard_map/ppermute | solution.py:1249
  71.5 5.8 %mix_local.6 = (bf16[4,3,1024,384]{3,2,1,0:T(8,128)(2,1)}, bf16[4,272,384]{2,1,0:T(8,128)(2,1)}, bf16[4,256,384]{2,1,0:T(8,128)(2,1)}, f32[4,3,256,384]{3,2,1,0:...) custom-call(s32[8]{0:T(128)} %pad_add_fusion.1.refs_0_, ...), custom_call_target="tpu_custom_call", output_to_operand_aliasing={{0}: (5, {}), {1}: (6, {}), {2}: (7, {}), {3}: (8, {}), {4}... | custom-call | flops 1880999936 | bytes 5985000 | tf_op jit(solution)/shard_map/mix_local/pallas_call | solution.py:155
  77.3 6.4 %collective-permute-done.16.refs_3_ = bf16[1,416,384]{2,1,0:T(8,128)(2,1)S(1)} collective-permute-done((bf16[1,416,384]{2,1,0:T(8,128)(2,1)S(1)}, bf16[1,416,384]{2,1,0:T(8,128)(2,1)S(1)}, u32[]{:S(2)}, u32[]{:S(2)}) %collective-permute-start.16) | collective-permute-done | bytes 319520 | tf_op jit(solution)/shard_map/ppermute | solution.py:1249
  89.2 5.8 %mix_local.7 = (bf16[4,3,1024,384]{3,2,1,0:T(8,128)(2,1)}, bf16[4,272,384]{2,1,0:T(8,128)(2,1)}, bf16[4,256,384]{2,1,0:T(8,128)(2,1)}, f32[4,3,256,384]{3,2,1,0:...) custom-call(s32[8]{0:T(128)} %pad_add_fusion.1.refs_0_, ...), custom_call_target="tpu_custom_call", output_to_operand_aliasing={{0}: (5, {}), {1}: (6, {}), {2}: (7, {}), {3}: (8, {}), {4}... | custom-call | flops 1880999936 | bytes 5985000 | tf_op jit(solution)/shard_map/mix_local/pallas_call | solution.py:155
  95.0 4.9 %collective-permute-done.19.refs_0_.refs_1_.refs_6_ = bf16[256,1024]{1,0:T(8,128)(2,1)S(1)} collective-permute-done((bf16[256,1024]{1,0:T(8,128)(2,1)S(1)}, bf16[256,1024]{1,0:T(8,128)(2,1)S(1)}, u32[]{:S(2)}, u32[]{:S(2)}) %collective-permute-start.19) | collective-permute-done | bytes 524320 | tf_op jit(solution)/shard_map/ppermute | solution.py:1249
  109.6 7.1 %mix_branch.1 = (f32[4,8,384]{2,1,0:T(8,128)}, bf16[4,256,384]{2,1,0:T(8,128)(2,1)}, f32[256,1024]{1,0:T(8,128)}, bf16[256,1024]{1,0:T(8,128)(2,1)}, bf16[256,1024]{1,0:T(8,128)(2,1)}) custom-call(f32[4,2,256,384]{3,2,1,0:T(8,128)} %get-tuple-element.156.refs_0_.refs_3_.refs_5_, bf16[4,256,384]{2,1,0:T(8,128)(2,1)} %get-tuple-element.157.refs_1_.refs_2_, ...), custom_call_target="tpu_custom_call" | custom-call | flops 33000000 | bytes 105000 | tf_op jit(solution)/shard_map/mix_branch/pallas_call | solution.py:155
  136.9 4.6 %collective-permute-done.26.refs_0_.refs_10_ = bf16[256,1024]{1,0:T(8,128)(2,1)S(1)} collective-permute-done((bf16[256,1024]{1,0:T(8,128)(2,1)S(1)}, bf16[256,1024]{1,0:T(8,128)(2,1)S(1)}, u32[]{:S(2)}, u32[]{:S(2)}) %collective-permute-start.26) | collective-permute-done | bytes 524320 | tf_op jit(solution)/shard_map/ppermute | solution.py:1249
  146.0 8.7 %mlp_grads.1 = (bf16[4,4,3,32,768]{4,3,2,1,0:T(8,128)(2,1)S(1)}, bf16[4,4,3,32,768]{4,3,2,1,0:T(8,128)(2,1)}, bf16[4,256,1024]{2,1,0:T(8,128)(2,1)S(1)}) custom-call(s32[1]{0:T(128)} %bitcast.13.refs_0_, s32[1]{0:T(128)} %bitcast.4.refs_0_.refs_1_.refs_7_, bf16[3,1024,768]{2,1,0:T(8,128)(2,1)S(1)} %mlp_arrange.1.refs_2_, bf16[256,1024]{1,0:T(8,128)(2,1)S(1)} %copy-done.14, ...), custom_call_target="tpu_custom_call" | custom-call | flops 4950000128 | bytes 15750000 | tf_op jit(solution)/shard_map/mlp_grads/pallas_call | solution.py:155
  154.7 9.2 %collective-permute-done.29.refs_3_ = bf16[256,1024]{1,0:T(8,128)(2,1)S(1)} collective-permute-done((bf16[256,1024]{1,0:T(8,128)(2,1)S(1)}, bf16[256,1024]{1,0:T(8,128)(2,1)S(1)}, u32[]{:S(2)}, u32[]{:S(2)}) %collective-permute-start.29) | collective-permute-done | bytes 524320 | tf_op jit(solution)/shard_map/ppermute | solution.py:1249
  171.9 4.5 %all-to-all-start.1 = ((bf16[4,256,1024]{2,1,0:T(8,128)(2,1)}), bf16[4,256,1024]{2,1,0:T(8,128)(2,1)}, u32[]{:S(2)}, u32[]{:S(2)}) async-start(bf16[4,256,1024]{2,1,0:T(8,128)(2,1)} %copy-done.12), calls=%async_computation.1 | async-start | bytes 4194304 | tf_op jit(solution)/shard_map/all_to_all | solution.py:1369
  176.5 8.8 %mix_adjoint.1 = (bf16[4,256,384]{2,1,0:T(8,128)(2,1)}, f32[4,2,256,384]{3,2,1,0:T(8,128)}, f32[4,8,384]{2,1,0:T(8,128)}, bf16[4,256,384]{2,1,0:T(8,128)(2,1)}) custom-call(bf16[256,1024]{1,0:T(8,128)(2,1)} %copy-done.26, bf16[4,3,1024,384]{3,2,1,0:T(8,128)(2,1)} %get-tuple-element.158.refs_2_.refs_1_.refs_0_, ...), custom_call_target="tpu_custom_call", output_to_operand_aliasing={{3}: (8, {})} | custom-call | flops 33000000 | bytes 105000 | tf_op jit(solution)/shard_map/mix_adjoint/pallas_call | solution.py:155
  192.4 6.2 %mix_outer.2.refs_5_ = bf16[4,4,256,384]{3,2,1,0:T(8,128)(2,1)} custom-call(s32[1]{0:T(128)} %bitcast.4.refs_0_.refs_1_.refs_7_, bf16[272,512]{1,0:T(8,128)(2,1)} %copy-done.21, bf16[272,512]{1,0:T(8,128)(2,1)} %copy-done.54, bf16[4,256,384]{2,1,0:T(8,128)(2,1)} %get-tuple-element.193.refs_3_, bf16[4,256,384]{2,1,0:T(8,128)(2,1)} %collective-permute-done.34.refs_4_, ...), custom_call_target="tpu_custom_call" | custom-call | flops 33000000 | bytes 105000 | tf_op jit(solution)/shard_map/mix_outer/pallas_call | solution.py:155
  204.3 4.9 %all-to-all-start.2 = ((bf16[4,4,256,384]{3,2,1,0:T(8,128)(2,1)}), bf16[4,4,256,384]{3,2,1,0:T(8,128)(2,1)}, u32[]{:S(2)}, u32[]{:S(2)}) async-start(bf16[4,4,256,384]{3,2,1,0:T(8,128)(2,1)} %fence.10.refs_17_), calls=%async_computation.2 | async-start | bytes 6291456 | tf_op jit(solution)/shard_map/all_to_all | solution.py:1376
  209.2 13.5 %mix_back.1 = (bf16[4,272,384]{2,1,0:T(8,128)(2,1)}, bf16[4,256,384]{2,1,0:T(8,128)(2,1)}, f32[272,1024]{1,0:T(8,128)}) custom-call(bf16[4,3,1024,384]{3,2,1,0:T(8,128)(2,1)} %get-tuple-element.158.refs_2_.refs_1_.refs_0_, bf16[4,3,1024,384]{3,2,1,0:T(8,128)(2,1)} %get-tuple-element.158.refs_2_.refs_1_.refs_0_, ...), custom_call_target="tpu_custom_call" | custom-call | flops 33000000 | bytes 105000 | tf_op jit(solution)/shard_map/mix_back/pallas_call | solution.py:155
  228.9 5.4 %mix_outer.3.refs_1_ = bf16[4,4,160,384]{3,2,1,0:T(8,128)(2,1)} custom-call(s32[1]{0:T(128)} %bitcast.4.refs_0_.refs_1_.refs_7_, bf16[272,512]{1,0:T(8,128)(2,1)} %copy-done.21, bf16[272,512]{1,0:T(8,128)(2,1)} %copy-done.54, bf16[4,272,384]{2,1,0:T(8,128)(2,1)} %get-tuple-element.207.refs_3_, bf16[4,272,384]{2,1,0:T(8,128)(2,1)} %copy-done.57, ...), custom_call_target="tpu_custom_call" | custom-call | flops 33000000 | bytes 105000 | tf_op jit(solution)/shard_map/mix_outer/pallas_call | solution.py:155
  234.2 10.6 %all-to-all-done.2.refs_0_ = bf16[4,4,256,384]{3,2,1,0:T(8,128)(2,1)} async-done(((bf16[4,4,256,384]{3,2,1,0:T(8,128)(2,1)}), bf16[4,4,256,384]{3,2,1,0:T(8,128)(2,1)}, u32[]{:S(2)}, u32[]{:S(2)}) %all-to-all-start.2) | async-done | bytes 3145760 | tf_op jit(solution)/shard_map/all_to_all | solution.py:1376
  244.9 4.6 %all-to-all-start.3 = ((bf16[4,4,160,384]{3,2,1,0:T(8,128)(2,1)}), bf16[4,4,160,384]{3,2,1,0:T(8,128)(2,1)}, u32[]{:S(2)}, u32[]{:S(2)}) async-start(bf16[4,4,160,384]{3,2,1,0:T(8,128)(2,1)} %fence.11), calls=%async_computation.3 | async-start | bytes 3932160 | tf_op jit(solution)/shard_map/all_to_all | solution.py:1376
  257.6 11.4 %collective-permute-done.41.refs_3_ = bf16[256,384]{1,0:T(8,128)(2,1)S(1)} collective-permute-done((bf16[256,384]{1,0:T(8,128)(2,1)S(1)}, bf16[256,384]{1,0:T(8,128)(2,1)S(1)}, u32[]{:S(2)}, u32[]{:S(2)}) %collective-permute-start.41) | collective-permute-done | bytes 196640 | tf_op jit(solution)/shard_map/ppermute | solution.py:1255
  286.3 7.7 %collective-permute-done.46.refs_4_ = bf16[176,384]{1,0:T(8,128)(2,1)S(1)} collective-permute-done((bf16[176,384]{1,0:T(8,128)(2,1)S(1)}, bf16[176,384]{1,0:T(8,128)(2,1)S(1)}, u32[]{:S(2)}, u32[]{:S(2)}) %collective-permute-start.46) | collective-permute-done | bytes 135200 | tf_op jit(solution)/shard_map/ppermute | solution.py:1255
  304.8 7.8 %all-to-all-done.5.refs_2_ = bf16[4,368,384]{2,1,0:T(8,128)(2,1)S(1)} async-done(((bf16[4,368,384]{2,1,0:T(8,128)(2,1)}), bf16[4,368,384]{2,1,0:T(8,128)(2,1)S(1)}, u32[]{:S(2)}, u32[]{:S(2)}) %all-to-all-start.5) | async-done | bytes 1130528 | tf_op jit(solution)/shard_map/all_to_all | solution.py:1438
  (286 shorter events, 147.4 us)
Async XLA Ops:
  7.2 18.9 %collective-permute-start.2 = (bf16[256,1024]{1,0:T(8,128)(2,1)}, bf16[256,1024]{1,0:T(8,128)(2,1)S(1)}, u32[]{:S(2)}, u32[]{:S(2)}) collective-permute-start(bf16[256,1024]{1,0:T(8,128)(2,1)} %refs_5_.4), channel_id=1, source_target_pairs={{0,8},{8,0},{16,24},{24,16},{1,9},{9,1},{17,25},{25,17},{2,10},{10... | collective-permute-start | bytes 1572872 | tf_op jit(solution)/shard_map/ppermute | solution.py:1249
  8.5 17.6 %collective-permute-start.3 = (bf16[256,1024]{1,0:T(8,128)(2,1)}, bf16[256,1024]{1,0:T(8,128)(2,1)S(1)}, u32[]{:S(2)}, u32[]{:S(2)}) collective-permute-start(bf16[256,1024]{1,0:T(8,128)(2,1)} %refs_5_.4), channel_id=1, source_target_pairs={{0,16},{8,24},{16,0},{24,8},{1,17},{9,25},{17,1},{25,9},{2,18},{10... | collective-permute-start | bytes 1572872 | tf_op jit(solution)/shard_map/ppermute | solution.py:1249
  16.9 22.9 %all-to-all-start = ((bf16[4,3,32,768]{3,2,1,0:T(8,128)(2,1)}), bf16[4,3,32,768]{3,2,1,0:T(8,128)(2,1)}, u32[]{:S(2)}, u32[]{:S(2)}) async-start(bf16[4,3,32,768]{3,2,1,0:T(8,128)(2,1)} %fence.8), calls=%async_computation | async-start | bytes 1179648 | tf_op jit(solution)/shard_map/all_to_all | solution.py:1316
  21.2 78.7 %all-gather.3.cloned.1.call-start = ((), (), s32[]{:S(2)}) async-start(), calls=%async_computation.8 | async-start | bytes 2949120 | tf_op jit(solution)/shard_map/all_gather | solution.py:1331
  30.7 14.4 %collective-permute-start.8 = (bf16[1,416,384]{2,1,0:T(8,128)(2,1)}, bf16[1,416,384]{2,1,0:T(8,128)(2,1)S(1)}, u32[]{:S(2)}, u32[]{:S(2)}) collective-permute-start(bf16[1,416,384]{2,1,0:T(8,128)(2,1)} %fence.7.refs_0_), channel_id=1, source_target_pairs={{0,1},{1,2},{2,3},{3,0},{4,5},{5,6},{6,7},{7,4},{8,9},{9,10},{10,1... | collective-permute-start | bytes 958472 | tf_op jit(solution)/shard_map/ppermute | solution.py:1255
  47.6 16.2 %collective-permute-start.10 = (bf16[1,416,384]{2,1,0:T(8,128)(2,1)S(1)}, bf16[1,416,384]{2,1,0:T(8,128)(2,1)S(1)}, u32[]{:S(2)}, u32[]{:S(2)}) collective-permute-start(bf16[1,416,384]{2,1,0:T(8,128)(2,1)S(1)} %get-tuple-element.128.refs_0_), channel_id=1, source_target_pairs={{0,16},{8,24},{16,0},{24,8},{1,17},{9,25},{17,1},{25,9},{2,18},{10... | collective-permute-start | bytes 958472 | tf_op jit(solution)/shard_map/ppermute | solution.py:1249
  48.8 14.9 %collective-permute-start.11 = (bf16[1,416,384]{2,1,0:T(8,128)(2,1)S(1)}, bf16[1,416,384]{2,1,0:T(8,128)(2,1)S(1)}, u32[]{:S(2)}, u32[]{:S(2)}) collective-permute-start(bf16[1,416,384]{2,1,0:T(8,128)(2,1)S(1)} %get-tuple-element.128.refs_0_), channel_id=1, source_target_pairs={{0,24},{8,16},{16,8},{24,0},{1,25},{9,17},{17,9},{25,1},{2,26},{10... | collective-permute-start | bytes 958472 | tf_op jit(solution)/shard_map/ppermute | solution.py:1249
  68.1 15.5 %collective-permute-start.16 = (bf16[1,416,384]{2,1,0:T(8,128)(2,1)S(1)}, bf16[1,416,384]{2,1,0:T(8,128)(2,1)S(1)}, u32[]{:S(2)}, u32[]{:S(2)}) collective-permute-start(bf16[1,416,384]{2,1,0:T(8,128)(2,1)S(1)} %get-tuple-element.138.refs_0_), channel_id=1, source_target_pairs={{0,24},{8,16},{16,8},{24,0},{1,25},{9,17},{17,9},{25,1},{2,26},{10... | collective-permute-start | bytes 958472 | tf_op jit(solution)/shard_map/ppermute | solution.py:1249
  85.5 14.4 %collective-permute-start.19 = (bf16[256,1024]{1,0:T(8,128)(2,1)S(1)}, bf16[256,1024]{1,0:T(8,128)(2,1)S(1)}, u32[]{:S(2)}, u32[]{:S(2)}) collective-permute-start(bf16[256,1024]{1,0:T(8,128)(2,1)S(1)} %get-tuple-element.159), channel_id=1, source_target_pairs={{0,24},{8,16},{16,8},{24,0},{1,25},{9,17},{17,9},{25,1},{2,26},{10... | collective-permute-start | bytes 1572872 | tf_op jit(solution)/shard_map/ppermute | solution.py:1249
  100.7 17.5 %collective-permute-start.23 = (bf16[4,4,3,32,768]{4,3,2,1,0:T(8,128)(2,1)}, bf16[4,4,3,32,768]{4,3,2,1,0:T(8,128)(2,1)}, u32[]{:S(2)}, u32[]{:S(2)}) collective-permute-start(bf16[4,4,3,32,768]{4,3,2,1,0:T(8,128)(2,1)} %get-tuple-element.164.refs_1_), channel_id=1, source_target_pairs={{0,4},{4,0},{1,5},{5,1},{2,6},{6,2},{3,7},{7,3},{8,12},{12,8},{9,1... | collective-permute-start | bytes 7077896 | tf_op jit(solution)/shard_map/ppermute | solution.py:1252
  118.2 15.6 %collective-permute-start.25 = (bf16[256,1024]{1,0:T(8,128)(2,1)}, bf16[256,1024]{1,0:T(8,128)(2,1)S(1)}, u32[]{:S(2)}, u32[]{:S(2)}) collective-permute-start(bf16[256,1024]{1,0:T(8,128)(2,1)} %get-tuple-element.165.refs_3_.refs_0_.refs_7_), channel_id=1, source_target_pairs={{0,16},{8,24},{16,0},{24,8},{1,17},{9,25},{17,1},{25,9},{2,18},{10... | collective-permute-start | bytes 1572872 | tf_op jit(solution)/shard_map/ppermute | solution.py:1249
  124.5 17.0 %collective-permute-start.26 = (bf16[256,1024]{1,0:T(8,128)(2,1)S(1)}, bf16[256,1024]{1,0:T(8,128)(2,1)S(1)}, u32[]{:S(2)}, u32[]{:S(2)}) collective-permute-start(bf16[256,1024]{1,0:T(8,128)(2,1)S(1)} %get-tuple-element.167), channel_id=1, source_target_pairs={{0,24},{8,16},{16,8},{24,0},{1,25},{9,17},{17,9},{25,1},{2,26},{10... | collective-permute-start | bytes 1572872 | tf_op jit(solution)/shard_map/ppermute | solution.py:1249
  132.3 22.4 %collective-permute-start.27 = (bf16[256,1024]{1,0:T(8,128)(2,1)S(1)}, bf16[256,1024]{1,0:T(8,128)(2,1)S(1)}, u32[]{:S(2)}, u32[]{:S(2)}) collective-permute-start(bf16[256,1024]{1,0:T(8,128)(2,1)S(1)} %get-tuple-element.171.refs_3_), channel_id=1, source_target_pairs={{0,8},{8,0},{16,24},{24,16},{1,9},{9,1},{17,25},{25,17},{2,10},{10... | collective-permute-start | bytes 1572872 | tf_op jit(solution)/shard_map/ppermute | solution.py:1249
  136.8 17.9 %collective-permute-start.28 = (bf16[256,1024]{1,0:T(8,128)(2,1)S(1)}, bf16[256,1024]{1,0:T(8,128)(2,1)S(1)}, u32[]{:S(2)}, u32[]{:S(2)}) collective-permute-start(bf16[256,1024]{1,0:T(8,128)(2,1)S(1)} %get-tuple-element.173.refs_3_), channel_id=1, source_target_pairs={{0,16},{8,24},{16,0},{24,8},{1,17},{9,25},{17,1},{25,9},{2,18},{10... | collective-permute-start | bytes 1572872 | tf_op jit(solution)/shard_map/ppermute | solution.py:1249
  144.4 19.5 %collective-permute-start.29 = (bf16[256,1024]{1,0:T(8,128)(2,1)S(1)}, bf16[256,1024]{1,0:T(8,128)(2,1)S(1)}, u32[]{:S(2)}, u32[]{:S(2)}) collective-permute-start(bf16[256,1024]{1,0:T(8,128)(2,1)S(1)} %get-tuple-element.185), channel_id=1, source_target_pairs={{0,24},{8,16},{16,8},{24,0},{1,25},{9,17},{17,9},{25,1},{2,26},{10... | collective-permute-start | bytes 1572872 | tf_op jit(solution)/shard_map/ppermute | solution.py:1249
  168.7 30.0 %collective-permute-start.33 = (bf16[4,4,3,32,768]{4,3,2,1,0:T(8,128)(2,1)}, bf16[4,4,3,32,768]{4,3,2,1,0:T(8,128)(2,1)}, u32[]{:S(2)}, u32[]{:S(2)}) collective-permute-start(bf16[4,4,3,32,768]{4,3,2,1,0:T(8,128)(2,1)} %get-tuple-element.198), channel_id=1, source_target_pairs={{0,4},{4,0},{1,5},{5,1},{2,6},{6,2},{3,7},{7,3},{8,12},{12,8},{9,1... | collective-permute-start | bytes 7077896 | tf_op jit(solution)/shard_map/ppermute | solution.py:1252
  171.9 32.3 %all-to-all-start.1 = ((bf16[4,256,1024]{2,1,0:T(8,128)(2,1)}), bf16[4,256,1024]{2,1,0:T(8,128)(2,1)}, u32[]{:S(2)}, u32[]{:S(2)}) async-start(bf16[4,256,1024]{2,1,0:T(8,128)(2,1)} %copy-done.12), calls=%async_computation.1 | async-start | bytes 4194304 | tf_op jit(solution)/shard_map/all_to_all | solution.py:1369
  176.4 105.3 %reduce-scatter.2.cloned.1.call-start = ((), (), s32[]{:S(2)}) async-start(), calls=%async_computation.7 | async-start | bytes 2949120 | tf_op jit(solution)/shard_map/reduce_scatter | solution.py:1402
  204.3 40.6 %all-to-all-start.2 = ((bf16[4,4,256,384]{3,2,1,0:T(8,128)(2,1)}), bf16[4,4,256,384]{3,2,1,0:T(8,128)(2,1)}, u32[]{:S(2)}, u32[]{:S(2)}) async-start(bf16[4,4,256,384]{3,2,1,0:T(8,128)(2,1)} %fence.10.refs_17_), calls=%async_computation.2 | async-start | bytes 6291456 | tf_op jit(solution)/shard_map/all_to_all | solution.py:1376
  244.9 28.5 %all-to-all-start.3 = ((bf16[4,4,160,384]{3,2,1,0:T(8,128)(2,1)}), bf16[4,4,160,384]{3,2,1,0:T(8,128)(2,1)}, u32[]{:S(2)}, u32[]{:S(2)}) async-start(bf16[4,4,160,384]{3,2,1,0:T(8,128)(2,1)} %fence.11), calls=%async_computation.3 | async-start | bytes 3932160 | tf_op jit(solution)/shard_map/all_to_all | solution.py:1376
  252.9 16.1 %collective-permute-start.41 = (bf16[256,384]{1,0:T(8,128)(2,1)S(1)}, bf16[256,384]{1,0:T(8,128)(2,1)S(1)}, u32[]{:S(2)}, u32[]{:S(2)}) collective-permute-start(bf16[256,384]{1,0:T(8,128)(2,1)S(1)} %get-tuple-element.229), channel_id=1, source_target_pairs={{0,2},{1,3},{2,0},{3,1},{4,6},{5,7},{6,4},{7,5},{8,10},{9,11},{10,... | collective-permute-start | bytes 589832 | tf_op jit(solution)/shard_map/ppermute | solution.py:1255
  256.0 16.4 %collective-permute-start.42 = (bf16[256,384]{1,0:T(8,128)(2,1)S(1)}, bf16[256,384]{1,0:T(8,128)(2,1)S(1)}, u32[]{:S(2)}, u32[]{:S(2)}) collective-permute-start(bf16[256,384]{1,0:T(8,128)(2,1)S(1)} %get-tuple-element.228), channel_id=1, source_target_pairs={{0,1},{1,2},{2,3},{3,0},{4,5},{5,6},{6,7},{7,4},{8,9},{9,10},{10,1... | collective-permute-start | bytes 589832 | tf_op jit(solution)/shard_map/ppermute | solution.py:1255
  276.3 17.7 %all-to-all-start.4 = ((bf16[4,256,384]{2,1,0:T(8,128)(2,1)}), bf16[4,256,384]{2,1,0:T(8,128)(2,1)S(1)}, u32[]{:S(2)}, u32[]{:S(2)}) async-start(bf16[4,256,384]{2,1,0:T(8,128)(2,1)} %fence.12), calls=%async_computation.4 | async-start | bytes 1572864 | tf_op jit(solution)/shard_map/all_to_all | solution.py:1376
  295.1 17.5 %all-to-all-start.5 = ((bf16[4,368,384]{2,1,0:T(8,128)(2,1)}), bf16[4,368,384]{2,1,0:T(8,128)(2,1)S(1)}, u32[]{:S(2)}, u32[]{:S(2)}) async-start(bf16[4,368,384]{2,1,0:T(8,128)(2,1)} %home_sum.3), calls=%async_computation.6 | async-start | bytes 2260992 | tf_op jit(solution)/shard_map/all_to_all | solution.py:1438
  (97 other events, 539.5 us)
Sparse Core Ops, SparseCore 0:
  47.7 51.8 all-gather.2
  204.4 47.9 reduce-scatter.1

commit v5 on v4

--- a/solution.py
+++ b/solution.py
@@ -834,51 +834,68 @@
     )
 
 
-def outer_kernel(groups, core_ref, *rest):
+def outer_kernel(groups, quads, core_ref, quad_ref, *rest):
     pairs, rest = rest[: 4 * groups], rest[4 * groups :]
-    *smalls, out, left, right, small = rest
+    *rest, left, right, small, whole = rest
+    if len(rest) in (3, 2 + quads):
+        smalls, outs = rest[:2], rest[2:]
+    else:
+        smalls, outs = [], rest
     count = pairs[2].shape[1]
-    quads, shards = out.shape[:2]
+    shards = outs[0].shape[-3]
     block = left.shape[1] // quads
+
+    def put(s, rows, member, values):
+        if len(outs) == 1:
+            outs[0][member, s, rows] = values
+        else:
+            outs[member][s, rows] = values
+
     for group in range(groups):
         left_ref, left_other, right_ref, right_other = pairs[4 * group : 4 * group + 4]
         left[:count] = left_ref[left_ref.shape[0] - count :]
         left[count:] = left_other[left_ref.shape[0] - count :]
+        rows = slice(group * block, (group + 1) * block)
         for s in range(shards):
             right[:count] = right_ref[s]
             right[count:] = right_other[s]
-            total = mm(left[...], right[...], 0, 0).astype(BF16)
-            for quad in range(quads):
-                out[quad, s, group * block : (group + 1) * block] = total[
-                    quad * block : (quad + 1) * block
-                ]
+            whole[...] = mm(left[...], right[...], 0, 0).astype(BF16)
+            for member in range(quads):
+                quad = member if len(outs) == 1 else quad_ref[0] ^ member
+                start = quad * block
+                if len(outs) > 1:
+                    start = pl.multiple_of(start, block)
+                put(s, rows, member, whole[pl.ds(start, block), :])
     if smalls:
-        extra = out.shape[2] - groups * block
+        extra = outs[0].shape[-2] - groups * block
+        rows = slice(groups * block, groups * block + extra)
         for s in range(shards):
             small[...] = (smalls[0][s].astype(F32) + smalls[1][s].astype(F32)).astype(BF16)
-            for quad in range(quads):
+            for member in range(quads):
+                quad = member if len(outs) == 1 else quad_ref[0] ^ member
                 start = pl.multiple_of((quad * 2 + core_ref[0]) * extra, extra)
-                out[quad, s, groups * block :] = small[pl.ds(start, extra), :]
-
-
-def outer(core, quads, pairs, smalls=(), after=(), carry=()):
+                put(s, rows, member, small[pl.ds(start, extra), :])
+
+
+def outer(core, quad, quads, pairs, smalls=(), after=(), relative=False):
     shards, count, width = pairs[2].shape
     model = pairs[0].shape[1]
     groups = len(pairs) // 4
     rows = groups * model // quads + (TABLE // (2 * quads) if smalls else 0)
+    shapes = [(shards, rows, width)] * quads if relative else [(quads, shards, rows, width)]
     return launch(
-        functools.partial(outer_kernel, groups),
-        [core, *pairs, *smalls],
-        [smem()] + [vmem()] * (len(pairs) + len(smalls)),
+        functools.partial(outer_kernel, groups, quads),
+        [core, quad, *pairs, *smalls],
+        [smem()] * 2 + [vmem()] * (len(pairs) + len(smalls)),
         0.1,
         after,
-        carry,
-        out_shape=[jax.ShapeDtypeStruct((quads, shards, rows, width), BF16)],
-        out_specs=[vmem()],
+        out_shape=[jax.ShapeDtypeStruct(shape, BF16) for shape in shapes],
+        out_specs=[vmem()] * len(shapes),
         scratch_shapes=[
             pltpu.VMEM((2 * count, model), BF16),
             pltpu.VMEM((2 * count, width), BF16),
             pltpu.VMEM((TABLE, width), BF16),
+            pltpu.VMEM((model, width), BF16),
         ],
         name="mix_outer",
     )
@@ -1367,7 +1384,6 @@
         quad_one, core_one, mlp_weights, cots, seconds, gate_grads, up_grads, hiddens, shards
     )
     results = lax.all_to_all(results, "quad", 0, 0, tiled=True)
-    block_out = (middle + jnp.sum(results.astype(F32), axis=0)).astype(BF16)
     middle_grad, branch_grad, gain_two, *made, own_grads, other_grads = middle_back(
         backs, middle, cotangent, mlp_gain, core_one, group, [], [own_grads, other_grads]
     )
@@ -1385,6 +1401,7 @@
     edges_back = [along(edge_back, -(i + 1)) for i in range(depth)]
     (chip_one,) = outer(
         core_one,
+        quad_one,
         quads,
         [
             normed_own,
@@ -1410,23 +1427,29 @@
         [chip_one],
     )
 
+    chip_two = outer(
+        core_one,
+        quad_one,
+        quads,
+        [normed_own, normed_other, input_back, swap(input_back)],
+        [small, swap(small)],
+        relative=True,
+    )
+    parts_two = [chip_two[0]] + [hop(chip_two[rel], rel) for rel in range(1, quads)]
     sum_one = add_up(arrived_one)
+    (results,) = fence([results], [sum_one])
+    block_out = (middle + jnp.sum(results.astype(F32), axis=0)).astype(BF16)
     halo_grad = along(normed_grad[:HALO].astype(BF16), -1)
     inside = ((place + 1) * count % LENGTH != 0).astype(jnp.int32).reshape(1)
     grad_tokens, lines = tokens_back(
         inside, normed_grad, halo_grad, tokens, norm_gain, middle_grad, gain_two, width, [sum_one]
     )
-    (chip_two,) = outer(
-        core_one,
-        quads,
-        [normed_own, normed_other, input_back, swap(input_back)],
-        [small, swap(small)],
-    )
-    (chip_two,) = fence([chip_two], [arrived_one])
     extra = lines.shape[0]
-    totals = add_up(spread(chip_two))
-    one = home_sum(place.reshape(1), [home(sum_one)], 0, quads=quads)
-    (one,) = fence([one], [totals, lines])
+    home_one = home(sum_one)
+    parts_two[1:] = fence(parts_two[1:], [lines, block_out])
+    totals = sum(part.astype(F32) for part in parts_two)
+    one = home_sum(place.reshape(1), [home_one], 0, quads=quads)
+    (one,) = fence([one], [totals, lines, block_out])
     own_one = spread(one)
     totals = jnp.concatenate(
         [totals, jnp.broadcast_to(lines.astype(F32)[None], (shards, extra, width))], axis=1
@@ -1438,7 +1461,6 @@
     own_two = lax.all_to_all(two, "quad", 0, 0, tiled=True)
     size = totals.shape[1]
     grad_gate, grad_out = assemble_one(core_one, own_one, swap(own_one))
-    (own_two,) = fence([own_two], [grad_gate, block_out])
     (
         grad_input,
         grad_recall,

time: 334 us -> 327 us (0.979)
  waiting for transfers between devices: 93.5 us -> 87.8 us
    ppermute x17, waiting for transfers between devices: 27 us -> 14.3 us  [along(): lax.ppermute(values, 'chan', [(i, (i + shift) % shards) for i in range(sh...]
    ppermute x18 -> x21, waiting for transfers between devices: 40.8 us -> 48.4 us  [hop(): return lax.ppermute(values, 'quad', [(i, i ^ rel) for i in range(quads)])]
    all_to_all x1, waiting for transfers between devices: 7.79 us -> 13.1 us  [on_device(): own_two = lax.all_to_all(two, 'quad', 0, 0, tiled=True)]
    all_to_all x3 -> x2, starting transfers between devices: 13.2 us -> 8.55 us  [spread(): return lax.all_to_all(chip, 'quad', 0, 0, tiled=True)]
    ppermute x18 -> x21, starting transfers between devices: 18 us -> 20.9 us  [hop(): return lax.ppermute(values, 'quad', [(i, i ^ rel) for i in range(quads)])]
    all_to_all x3 -> x2, waiting for transfers between devices: 10.6 us -> 7.73 us  [spread(): return lax.all_to_all(chip, 'quad', 0, 0, tiled=True)]
    unnamed x131 -> x133, local copies, waits for them, and re-layouts: 21.1 us -> 22.8 us
  transfers between devices with their start and end apart: 56 -> 58, of which waited for: 21 -> 20; matrix products, arithmetic and copies ran while one was open for 5% -> 5% of each run, Pallas kernels for 30% -> 31%
where the time goes in v5:
time: 327 us; the launch traced here: 322 us
  Pallas kernels  104 us (32%)
  waiting for transfers between devices  87.8 us (27%)
  starting transfers between devices  74.8 us (23%)
  local copies, waits for them, and re-layouts  30.3 us (9%)
  between operations  15.3 us (5%)
  other arithmetic  9.84 us (3%)
    pallas_call x34, Pallas kernels, launch(): pl.pallas_call(body, out_shape=list(out_shape) + [jax.ShapeDtypeStruct(c....  104 us
    ppermute x21, waiting for transfers between devices, hop(): return lax.ppermute(values, 'quad', [(i, i ^ rel) for i in range(quads)])  48.4 us
    unnamed x133, local copies, waits for them, and re-layouts  22.8 us
    ppermute x21, starting transfers between devices, hop(): return lax.ppermute(values, 'quad', [(i, i ^ rel) for i in range(quads)])  20.9 us
    ppermute x17, starting transfers between devices, along(): lax.ppermute(values, 'chan', [(i, (i + shift) % shards) for i in range(sh...  18.4 us
    ppermute x13, starting transfers between devices, swap(): return lax.ppermute(values, 'core', [(0, 1), (1, 0)])  14.4 us
    ppermute x17, waiting for transfers between devices, along(): lax.ppermute(values, 'chan', [(i, (i + shift) % shards) for i in range(sh...  14.3 us
    all_to_all x1, waiting for transfers between devices, on_device(): own_two = lax.all_to_all(two, 'quad', 0, 0, tiled=True)  13.1 us
  transfers between devices with their start and end apart: 58, of which 20 were waited for; matrix products, arithmetic and copies ran while one was open for 5% of the time, Pallas kernels for 31%

profile of v5, /device:TPU:17, one launch (start us, length us, event | category | flops | bytes accessed | tf_op | source)
XLA Modules:
  0.0 321.8 jit_solution(5196002634391358791)
XLA Ops:
  16.9 4.3 %all-to-all-start = ((bf16[4,3,32,768]{3,2,1,0:T(8,128)(2,1)}), bf16[4,3,32,768]{3,2,1,0:T(8,128)(2,1)}, u32[]{:S(2)}, u32[]{:S(2)}) async-start(bf16[4,3,32,768]{3,2,1,0:T(8,128)(2,1)} %fence.8), calls=%async_computation | async-start | bytes 1179648 | tf_op jit(solution)/shard_map/all_to_all | solution.py:1333
  33.5 6.3 %mix_local.4 = (bf16[4,3,1024,384]{3,2,1,0:T(8,128)(2,1)}, bf16[4,272,384]{2,1,0:T(8,128)(2,1)}, bf16[4,256,384]{2,1,0:T(8,128)(2,1)}, f32[4,3,256,384]{3,2,1,0:...) custom-call(s32[8]{0:T(128)} %pad_add_fusion.1.refs_0_, ...), custom_call_target="tpu_custom_call" | custom-call | flops 1880999936 | bytes 5985000 | tf_op jit(solution)/shard_map/mix_local/pallas_call | solution.py:155
  39.9 5.2 %collective-permute-done.7.refs_3_ = bf16[1,416,384]{2,1,0:T(8,128)(2,1)S(1)} collective-permute-done((bf16[1,416,384]{2,1,0:T(8,128)(2,1)}, bf16[1,416,384]{2,1,0:T(8,128)(2,1)S(1)}, u32[]{:S(2)}, u32[]{:S(2)}) %collective-permute-start.7) | collective-permute-done | bytes 319520 | tf_op jit(solution)/shard_map/ppermute | solution.py:1266
  52.0 5.8 %mix_local.5 = (bf16[4,3,1024,384]{3,2,1,0:T(8,128)(2,1)}, bf16[4,272,384]{2,1,0:T(8,128)(2,1)}, bf16[4,256,384]{2,1,0:T(8,128)(2,1)}, f32[4,3,256,384]{3,2,1,0:...) custom-call(s32[8]{0:T(128)} %pad_add_fusion.1.refs_0_, ...), custom_call_target="tpu_custom_call", output_to_operand_aliasing={{0}: (5, {}), {1}: (6, {}), {2}: (7, {}), {3}: (8, {}), {4}... | custom-call | flops 1880999936 | bytes 5985000 | tf_op jit(solution)/shard_map/mix_local/pallas_call | solution.py:155
  57.8 5.9 %collective-permute-done.10.refs_2_ = bf16[1,416,384]{2,1,0:T(8,128)(2,1)S(1)} collective-permute-done((bf16[1,416,384]{2,1,0:T(8,128)(2,1)S(1)}, bf16[1,416,384]{2,1,0:T(8,128)(2,1)S(1)}, u32[]{:S(2)}, u32[]{:S(2)}) %collective-permute-start.10) | collective-permute-done | bytes 319520 | tf_op jit(solution)/shard_map/ppermute | solution.py:1266
  71.5 5.8 %mix_local.6 = (bf16[4,3,1024,384]{3,2,1,0:T(8,128)(2,1)}, bf16[4,272,384]{2,1,0:T(8,128)(2,1)}, bf16[4,256,384]{2,1,0:T(8,128)(2,1)}, f32[4,3,256,384]{3,2,1,0:...) custom-call(s32[8]{0:T(128)} %pad_add_fusion.1.refs_0_, ...), custom_call_target="tpu_custom_call", output_to_operand_aliasing={{0}: (5, {}), {1}: (6, {}), {2}: (7, {}), {3}: (8, {}), {4}... | custom-call | flops 1880999936 | bytes 5985000 | tf_op jit(solution)/shard_map/mix_local/pallas_call | solution.py:155
  77.3 6.4 %collective-permute-done.16.refs_3_ = bf16[1,416,384]{2,1,0:T(8,128)(2,1)S(1)} collective-permute-done((bf16[1,416,384]{2,1,0:T(8,128)(2,1)S(1)}, bf16[1,416,384]{2,1,0:T(8,128)(2,1)S(1)}, u32[]{:S(2)}, u32[]{:S(2)}) %collective-permute-start.16) | collective-permute-done | bytes 319520 | tf_op jit(solution)/shard_map/ppermute | solution.py:1266
  89.2 5.8 %mix_local.7 = (bf16[4,3,1024,384]{3,2,1,0:T(8,128)(2,1)}, bf16[4,272,384]{2,1,0:T(8,128)(2,1)}, bf16[4,256,384]{2,1,0:T(8,128)(2,1)}, f32[4,3,256,384]{3,2,1,0:...) custom-call(s32[8]{0:T(128)} %pad_add_fusion.1.refs_0_, ...), custom_call_target="tpu_custom_call", output_to_operand_aliasing={{0}: (5, {}), {1}: (6, {}), {2}: (7, {}), {3}: (8, {}), {4}... | custom-call | flops 1880999936 | bytes 5985000 | tf_op jit(solution)/shard_map/mix_local/pallas_call | solution.py:155
  95.0 4.9 %collective-permute-done.19.refs_0_.refs_1_.refs_6_ = bf16[256,1024]{1,0:T(8,128)(2,1)S(1)} collective-permute-done((bf16[256,1024]{1,0:T(8,128)(2,1)S(1)}, bf16[256,1024]{1,0:T(8,128)(2,1)S(1)}, u32[]{:S(2)}, u32[]{:S(2)}) %collective-permute-start.19) | collective-permute-done | bytes 524320 | tf_op jit(solution)/shard_map/ppermute | solution.py:1266
  109.6 7.1 %mix_branch.1 = (f32[4,8,384]{2,1,0:T(8,128)}, bf16[4,256,384]{2,1,0:T(8,128)(2,1)}, f32[256,1024]{1,0:T(8,128)}, bf16[256,1024]{1,0:T(8,128)(2,1)}, bf16[256,1024]{1,0:T(8,128)(2,1)}) custom-call(f32[4,2,256,384]{3,2,1,0:T(8,128)} %get-tuple-element.163.refs_0_.refs_3_.refs_5_, bf16[4,256,384]{2,1,0:T(8,128)(2,1)} %get-tuple-element.164.refs_1_.refs_2_, ...), custom_call_target="tpu_custom_call" | custom-call | flops 33000000 | bytes 105000 | tf_op jit(solution)/shard_map/mix_branch/pallas_call | solution.py:155
  136.9 4.6 %collective-permute-done.28.refs_0_.refs_10_ = bf16[256,1024]{1,0:T(8,128)(2,1)S(1)} collective-permute-done((bf16[256,1024]{1,0:T(8,128)(2,1)S(1)}, bf16[256,1024]{1,0:T(8,128)(2,1)S(1)}, u32[]{:S(2)}, u32[]{:S(2)}) %collective-permute-start.28) | collective-permute-done | bytes 524320 | tf_op jit(solution)/shard_map/ppermute | solution.py:1266
  146.0 8.7 %mlp_grads.1 = (bf16[4,4,3,32,768]{4,3,2,1,0:T(8,128)(2,1)S(1)}, bf16[4,4,3,32,768]{4,3,2,1,0:T(8,128)(2,1)}, bf16[4,256,1024]{2,1,0:T(8,128)(2,1)S(1)}) custom-call(s32[1]{0:T(128)} %bitcast.13.refs_0_.refs_1_, s32[1]{0:T(128)} %bitcast.4.refs_0_.refs_1_.refs_7_, bf16[3,1024,768]{2,1,0:T(8,128)(2,1)S(1)} %mlp_arrange.1.refs_2_, ...), custom_call_target="tpu_custom_call" | custom-call | flops 4950000128 | bytes 15750000 | tf_op jit(solution)/shard_map/mlp_grads/pallas_call | solution.py:155
  154.7 9.3 %collective-permute-done.29.refs_3_ = bf16[256,1024]{1,0:T(8,128)(2,1)S(1)} collective-permute-done((bf16[256,1024]{1,0:T(8,128)(2,1)S(1)}, bf16[256,1024]{1,0:T(8,128)(2,1)S(1)}, u32[]{:S(2)}, u32[]{:S(2)}) %collective-permute-start.29) | collective-permute-done | bytes 524320 | tf_op jit(solution)/shard_map/ppermute | solution.py:1266
  171.9 4.5 %all-to-all-start.1 = ((bf16[4,256,1024]{2,1,0:T(8,128)(2,1)}), bf16[4,256,1024]{2,1,0:T(8,128)(2,1)}, u32[]{:S(2)}, u32[]{:S(2)}) async-start(bf16[4,256,1024]{2,1,0:T(8,128)(2,1)} %copy-done.12), calls=%async_computation.1 | async-start | bytes 4194304 | tf_op jit(solution)/shard_map/all_to_all | solution.py:1386
  176.4 8.8 %mix_adjoint.1 = (bf16[4,256,384]{2,1,0:T(8,128)(2,1)}, f32[4,2,256,384]{3,2,1,0:T(8,128)}, f32[4,8,384]{2,1,0:T(8,128)}, bf16[4,256,384]{2,1,0:T(8,128)(2,1)}) custom-call(bf16[256,1024]{1,0:T(8,128)(2,1)} %copy-done.26, bf16[4,3,1024,384]{3,2,1,0:T(8,128)(2,1)} %get-tuple-element.165.refs_2_.refs_1_.refs_0_, ...), custom_call_target="tpu_custom_call", output_to_operand_aliasing={{3}: (8, {})} | custom-call | flops 33000000 | bytes 105000 | tf_op jit(solution)/shard_map/mix_adjoint/pallas_call | solution.py:155
  192.3 6.6 %mix_outer.2.refs_5_ = bf16[4,4,256,384]{3,2,1,0:T(8,128)(2,1)} custom-call(s32[1]{0:T(128)} %bitcast.4.refs_0_.refs_1_.refs_7_, s32[1]{0:T(128)} %bitcast.13.refs_0_.refs_1_, bf16[272,512]{1,0:T(8,128)(2,1)} %copy-done.21, bf16[272,512]{1,0:T(8,128)(2,1)} %copy-done.53, bf16[4,256,384]{2,1,0:T(8,128)(2,1)} %get-tuple-element.203.refs_4_.refs_3_, ...), custom_call_target="tpu_custom_call" | custom-call | flops 33000000 | bytes 105000 | tf_op jit(solution)/shard_map/mix_outer/pallas_call | solution.py:155
  204.6 4.9 %all-to-all-start.2 = ((bf16[4,4,256,384]{3,2,1,0:T(8,128)(2,1)}), bf16[4,4,256,384]{3,2,1,0:T(8,128)(2,1)}, u32[]{:S(2)}, u32[]{:S(2)}) async-start(bf16[4,4,256,384]{3,2,1,0:T(8,128)(2,1)} %fence.10.refs_17_), calls=%async_computation.2 | async-start | bytes 6291456 | tf_op jit(solution)/shard_map/all_to_all | solution.py:1392
  209.5 13.6 %mix_back.1 = (bf16[4,272,384]{2,1,0:T(8,128)(2,1)}, bf16[4,256,384]{2,1,0:T(8,128)(2,1)}, f32[272,1024]{1,0:T(8,128)}) custom-call(bf16[4,3,1024,384]{3,2,1,0:T(8,128)(2,1)} %get-tuple-element.165.refs_2_.refs_1_.refs_0_, bf16[4,3,1024,384]{3,2,1,0:T(8,128)(2,1)} %get-tuple-element.165.refs_2_.refs_1_.refs_0_, ...), custom_call_target="tpu_custom_call" | custom-call | flops 33000000 | bytes 105000 | tf_op jit(solution)/shard_map/mix_back/pallas_call | solution.py:155
  229.1 5.4 %mix_outer.3 = (bf16[4,160,384]{2,1,0:T(8,128)(2,1)}, bf16[4,160,384]{2,1,0:T(8,128)(2,1)}, bf16[4,160,384]{2,1,0:T(8,128)(2,1)}, bf16[4,160,384]{2,1,0:T(8,128)(2,1)}) custom-call(s32[1]{0:T(128)} %bitcast.4.refs_0_.refs_1_.refs_7_, s32[1]{0:T(128)} %bitcast.13.refs_0_.refs_1_, bf16[272,512]{1,0:T(8,128)(2,1)} %copy-done.21, bf16[272,512]{1,0:T(8,128)(2,1)} %copy-done.53, ...), custom_call_target="tpu_custom_call" | custom-call | flops 33000000 | bytes 105000 | tf_op jit(solution)/shard_map/mix_outer/pallas_call | solution.py:155
  237.4 7.7 %all-to-all-done.2 = bf16[4,4,256,384]{3,2,1,0:T(8,128)(2,1)} async-done(((bf16[4,4,256,384]{3,2,1,0:T(8,128)(2,1)}), bf16[4,4,256,384]{3,2,1,0:T(8,128)(2,1)}, u32[]{:S(2)}, u32[]{:S(2)}) %all-to-all-start.2) | async-done | bytes 3145760 | tf_op jit(solution)/shard_map/all_to_all | solution.py:1392
  259.4 7.7 %collective-permute-done.42.refs_4_ = bf16[4,160,384]{2,1,0:T(8,128)(2,1)} collective-permute-done((bf16[4,160,384]{2,1,0:T(8,128)(2,1)}, bf16[4,160,384]{2,1,0:T(8,128)(2,1)}, u32[]{:S(2)}, u32[]{:S(2)}) %collective-permute-start.42) | collective-permute-done | bytes 491552 | tf_op jit(solution)/shard_map/ppermute | solution.py:1266
  279.3 6.7 %collective-permute-done.44.refs_3_ = bf16[176,384]{1,0:T(8,128)(2,1)S(1)} collective-permute-done((bf16[176,384]{1,0:T(8,128)(2,1)S(1)}, bf16[176,384]{1,0:T(8,128)(2,1)S(1)}, u32[]{:S(2)}, u32[]{:S(2)}) %collective-permute-start.44) | collective-permute-done | bytes 135200 | tf_op jit(solution)/shard_map/ppermute | solution.py:1272
  286.0 3.9 %collective-permute-done.45.refs_4_ = bf16[176,384]{1,0:T(8,128)(2,1)S(1)} collective-permute-done((bf16[176,384]{1,0:T(8,128)(2,1)S(1)}, bf16[176,384]{1,0:T(8,128)(2,1)S(1)}, u32[]{:S(2)}, u32[]{:S(2)}) %collective-permute-start.45) | collective-permute-done | bytes 135200 | tf_op jit(solution)/shard_map/ppermute | solution.py:1272
  295.6 13.1 %all-to-all-done.4.refs_1_ = bf16[4,368,384]{2,1,0:T(8,128)(2,1)S(1)} async-done(((bf16[4,368,384]{2,1,0:T(8,128)(2,1)}), bf16[4,368,384]{2,1,0:T(8,128)(2,1)S(1)}, u32[]{:S(2)}, u32[]{:S(2)}) %all-to-all-start.4) | async-done | bytes 1130528 | tf_op jit(solution)/shard_map/all_to_all | solution.py:1461
  (292 shorter events, 143.4 us)
Async XLA Ops:
  7.2 18.9 %collective-permute-start.2 = (bf16[256,1024]{1,0:T(8,128)(2,1)}, bf16[256,1024]{1,0:T(8,128)(2,1)S(1)}, u32[]{:S(2)}, u32[]{:S(2)}) collective-permute-start(bf16[256,1024]{1,0:T(8,128)(2,1)} %refs_5_.4), channel_id=1, source_target_pairs={{0,8},{8,0},{16,24},{24,16},{1,9},{9,1},{17,25},{25,17},{2,10},{10... | collective-permute-start | bytes 1572872 | tf_op jit(solution)/shard_map/ppermute | solution.py:1266
  8.5 17.6 %collective-permute-start.3 = (bf16[256,1024]{1,0:T(8,128)(2,1)}, bf16[256,1024]{1,0:T(8,128)(2,1)S(1)}, u32[]{:S(2)}, u32[]{:S(2)}) collective-permute-start(bf16[256,1024]{1,0:T(8,128)(2,1)} %refs_5_.4), channel_id=1, source_target_pairs={{0,16},{8,24},{16,0},{24,8},{1,17},{9,25},{17,1},{25,9},{2,18},{10... | collective-permute-start | bytes 1572872 | tf_op jit(solution)/shard_map/ppermute | solution.py:1266
  16.9 23.0 %all-to-all-start = ((bf16[4,3,32,768]{3,2,1,0:T(8,128)(2,1)}), bf16[4,3,32,768]{3,2,1,0:T(8,128)(2,1)}, u32[]{:S(2)}, u32[]{:S(2)}) async-start(bf16[4,3,32,768]{3,2,1,0:T(8,128)(2,1)} %fence.8), calls=%async_computation | async-start | bytes 1179648 | tf_op jit(solution)/shard_map/all_to_all | solution.py:1333
  21.2 78.7 %all-gather.3.cloned.1.call-start = ((), (), s32[]{:S(2)}) async-start(), calls=%async_computation.7 | async-start | bytes 2949120 | tf_op jit(solution)/shard_map/all_gather | solution.py:1348
  47.6 16.2 %collective-permute-start.10 = (bf16[1,416,384]{2,1,0:T(8,128)(2,1)S(1)}, bf16[1,416,384]{2,1,0:T(8,128)(2,1)S(1)}, u32[]{:S(2)}, u32[]{:S(2)}) collective-permute-start(bf16[1,416,384]{2,1,0:T(8,128)(2,1)S(1)} %get-tuple-element.135.refs_0_), channel_id=1, source_target_pairs={{0,16},{8,24},{16,0},{24,8},{1,17},{9,25},{17,1},{25,9},{2,18},{10... | collective-permute-start | bytes 958472 | tf_op jit(solution)/shard_map/ppermute | solution.py:1266
  100.7 17.5 %collective-permute-start.23 = (bf16[4,4,3,32,768]{4,3,2,1,0:T(8,128)(2,1)}, bf16[4,4,3,32,768]{4,3,2,1,0:T(8,128)(2,1)}, u32[]{:S(2)}, u32[]{:S(2)}) collective-permute-start(bf16[4,4,3,32,768]{4,3,2,1,0:T(8,128)(2,1)} %get-tuple-element.172.refs_1_), channel_id=1, source_target_pairs={{0,4},{4,0},{1,5},{5,1},{2,6},{6,2},{3,7},{7,3},{8,12},{12,8},{9,1... | collective-permute-start | bytes 7077896 | tf_op jit(solution)/shard_map/ppermute | solution.py:1269
  118.2 15.6 %collective-permute-start.26 = (bf16[256,1024]{1,0:T(8,128)(2,1)}, bf16[256,1024]{1,0:T(8,128)(2,1)S(1)}, u32[]{:S(2)}, u32[]{:S(2)}) collective-permute-start(bf16[256,1024]{1,0:T(8,128)(2,1)} %get-tuple-element.171.refs_3_.refs_0_.refs_7_), channel_id=1, source_target_pairs={{0,16},{8,24},{16,0},{24,8},{1,17},{9,25},{17,1},{25,9},{2,18},{10... | collective-permute-start | bytes 1572872 | tf_op jit(solution)/shard_map/ppermute | solution.py:1266
  124.5 17.0 %collective-permute-start.28 = (bf16[256,1024]{1,0:T(8,128)(2,1)S(1)}, bf16[256,1024]{1,0:T(8,128)(2,1)S(1)}, u32[]{:S(2)}, u32[]{:S(2)}) collective-permute-start(bf16[256,1024]{1,0:T(8,128)(2,1)S(1)} %get-tuple-element.177), channel_id=1, source_target_pairs={{0,24},{8,16},{16,8},{24,0},{1,25},{9,17},{17,9},{25,1},{2,26},{10... | collective-permute-start | bytes 1572872 | tf_op jit(solution)/shard_map/ppermute | solution.py:1266
  132.3 22.4 %collective-permute-start.25 = (bf16[256,1024]{1,0:T(8,128)(2,1)S(1)}, bf16[256,1024]{1,0:T(8,128)(2,1)S(1)}, u32[]{:S(2)}, u32[]{:S(2)}) collective-permute-start(bf16[256,1024]{1,0:T(8,128)(2,1)S(1)} %get-tuple-element.175.refs_3_), channel_id=1, source_target_pairs={{0,8},{8,0},{16,24},{24,16},{1,9},{9,1},{17,25},{25,17},{2,10},{10... | collective-permute-start | bytes 1572872 | tf_op jit(solution)/shard_map/ppermute | solution.py:1266
  136.8 17.9 %collective-permute-start.27 = (bf16[256,1024]{1,0:T(8,128)(2,1)S(1)}, bf16[256,1024]{1,0:T(8,128)(2,1)S(1)}, u32[]{:S(2)}, u32[]{:S(2)}) collective-permute-start(bf16[256,1024]{1,0:T(8,128)(2,1)S(1)} %get-tuple-element.176.refs_3_), channel_id=1, source_target_pairs={{0,16},{8,24},{16,0},{24,8},{1,17},{9,25},{17,1},{25,9},{2,18},{10... | collective-permute-start | bytes 1572872 | tf_op jit(solution)/shard_map/ppermute | solution.py:1266
  144.4 19.5 %collective-permute-start.29 = (bf16[256,1024]{1,0:T(8,128)(2,1)S(1)}, bf16[256,1024]{1,0:T(8,128)(2,1)S(1)}, u32[]{:S(2)}, u32[]{:S(2)}) collective-permute-start(bf16[256,1024]{1,0:T(8,128)(2,1)S(1)} %get-tuple-element.178), channel_id=1, source_target_pairs={{0,24},{8,16},{16,8},{24,0},{1,25},{9,17},{17,9},{25,1},{2,26},{10... | collective-permute-start | bytes 1572872 | tf_op jit(solution)/shard_map/ppermute | solution.py:1266
  168.7 30.3 %collective-permute-start.33 = (bf16[4,4,3,32,768]{4,3,2,1,0:T(8,128)(2,1)}, bf16[4,4,3,32,768]{4,3,2,1,0:T(8,128)(2,1)}, u32[]{:S(2)}, u32[]{:S(2)}) collective-permute-start(bf16[4,4,3,32,768]{4,3,2,1,0:T(8,128)(2,1)} %get-tuple-element.201), channel_id=1, source_target_pairs={{0,4},{4,0},{1,5},{5,1},{2,6},{6,2},{3,7},{7,3},{8,12},{12,8},{9,1... | collective-permute-start | bytes 7077896 | tf_op jit(solution)/shard_map/ppermute | solution.py:1269
  171.9 32.7 %all-to-all-start.1 = ((bf16[4,256,1024]{2,1,0:T(8,128)(2,1)}), bf16[4,256,1024]{2,1,0:T(8,128)(2,1)}, u32[]{:S(2)}, u32[]{:S(2)}) async-start(bf16[4,256,1024]{2,1,0:T(8,128)(2,1)} %copy-done.12), calls=%async_computation.1 | async-start | bytes 4194304 | tf_op jit(solution)/shard_map/all_to_all | solution.py:1386
  176.4 100.9 %reduce-scatter.2.cloned.1.call-start = ((), (), s32[]{:S(2)}) async-start(), calls=%async_computation.6 | async-start | bytes 2949120 | tf_op jit(solution)/shard_map/reduce_scatter | solution.py:1419
  204.6 40.6 %all-to-all-start.2 = ((bf16[4,4,256,384]{3,2,1,0:T(8,128)(2,1)}), bf16[4,4,256,384]{3,2,1,0:T(8,128)(2,1)}, u32[]{:S(2)}, u32[]{:S(2)}) async-start(bf16[4,4,256,384]{3,2,1,0:T(8,128)(2,1)} %fence.10.refs_17_), calls=%async_computation.2 | async-start | bytes 6291456 | tf_op jit(solution)/shard_map/all_to_all | solution.py:1392
  225.5 23.5 %collective-permute-start.37 = (bf16[16,1024]{1,0:T(8,128)(2,1)}, bf16[16,1024]{1,0:T(8,128)(2,1)S(1)}, u32[]{:S(2)}, u32[]{:S(2)}) collective-permute-start(bf16[16,1024]{1,0:T(8,128)(2,1)} %slice.78), channel_id=1, source_target_pairs={{0,3},{1,0},{2,1},{3,2},{4,7},{5,4},{6,5},{7,6},{8,11},{9,8},{10,9... | collective-permute-start | bytes 98312 | tf_op jit(solution)/shard_map/ppermute | solution.py:1272
  234.5 24.8 %collective-permute-start.40 = (bf16[4,160,384]{2,1,0:T(8,128)(2,1)}, bf16[4,160,384]{2,1,0:T(8,128)(2,1)S(1)}, u32[]{:S(2)}, u32[]{:S(2)}) collective-permute-start(bf16[4,160,384]{2,1,0:T(8,128)(2,1)} %get-tuple-element.218), channel_id=1, source_target_pairs={{0,8},{8,0},{16,24},{24,16},{1,9},{9,1},{17,25},{25,17},{2,10},{10... | collective-permute-start | bytes 1474568 | tf_op jit(solution)/shard_map/ppermute | solution.py:1266
  236.3 23.1 %collective-permute-start.41 = (bf16[4,160,384]{2,1,0:T(8,128)(2,1)}, bf16[4,160,384]{2,1,0:T(8,128)(2,1)}, u32[]{:S(2)}, u32[]{:S(2)}) collective-permute-start(bf16[4,160,384]{2,1,0:T(8,128)(2,1)} %get-tuple-element.219), channel_id=1, source_target_pairs={{0,16},{8,24},{16,0},{24,8},{1,17},{9,25},{17,1},{25,9},{2,18},{10... | collective-permute-start | bytes 1474568 | tf_op jit(solution)/shard_map/ppermute | solution.py:1266
  237.4 29.6 %collective-permute-start.42 = (bf16[4,160,384]{2,1,0:T(8,128)(2,1)}, bf16[4,160,384]{2,1,0:T(8,128)(2,1)}, u32[]{:S(2)}, u32[]{:S(2)}) collective-permute-start(bf16[4,160,384]{2,1,0:T(8,128)(2,1)} %get-tuple-element.220), channel_id=1, source_target_pairs={{0,24},{8,16},{16,8},{24,0},{1,25},{9,17},{17,9},{25,1},{2,26},{10... | collective-permute-start | bytes 1474568 | tf_op jit(solution)/shard_map/ppermute | solution.py:1266
  248.8 21.7 %collective-permute-start.46 = (bf16[256,384]{1,0:T(8,128)(2,1)}, bf16[256,384]{1,0:T(8,128)(2,1)S(1)}, u32[]{:S(2)}, u32[]{:S(2)}) collective-permute-start(bf16[256,384]{1,0:T(8,128)(2,1)} %get-tuple-element.244), channel_id=1, source_target_pairs={{0,3},{1,0},{2,1},{3,2},{4,7},{5,4},{6,5},{7,6},{8,11},{9,8},{10,9... | collective-permute-start | bytes 589832 | tf_op jit(solution)/shard_map/ppermute | solution.py:1272
  249.0 21.6 %collective-permute-start.47 = (bf16[256,384]{1,0:T(8,128)(2,1)}, bf16[256,384]{1,0:T(8,128)(2,1)S(1)}, u32[]{:S(2)}, u32[]{:S(2)}) collective-permute-start(bf16[256,384]{1,0:T(8,128)(2,1)} %get-tuple-element.243), channel_id=1, source_target_pairs={{0,2},{1,3},{2,0},{3,1},{4,6},{5,7},{6,4},{7,5},{8,10},{9,11},{10,... | collective-permute-start | bytes 589832 | tf_op jit(solution)/shard_map/ppermute | solution.py:1272
  271.6 18.4 %all-to-all-start.3 = ((bf16[4,256,384]{2,1,0:T(8,128)(2,1)}), bf16[4,256,384]{2,1,0:T(8,128)(2,1)S(1)}, u32[]{:S(2)}, u32[]{:S(2)}) async-start(bf16[4,256,384]{2,1,0:T(8,128)(2,1)} %fence.13), calls=%async_computation.4 | async-start | bytes 1572864 | tf_op jit(solution)/shard_map/all_to_all | solution.py:1392
  291.1 17.6 %all-to-all-start.4 = ((bf16[4,368,384]{2,1,0:T(8,128)(2,1)}), bf16[4,368,384]{2,1,0:T(8,128)(2,1)S(1)}, u32[]{:S(2)}, u32[]{:S(2)}) async-start(bf16[4,368,384]{2,1,0:T(8,128)(2,1)} %home_sum.3), calls=%async_computation.5 | async-start | bytes 2260992 | tf_op jit(solution)/shard_map/all_to_all | solution.py:1461
  294.8 15.6 %collective-permute-start.50 = (bf16[4,256,384]{2,1,0:T(8,128)(2,1)S(1)}, bf16[4,256,384]{2,1,0:T(8,128)(2,1)S(1)}, u32[]{:S(2)}, u32[]{:S(2)}) collective-permute-start(bf16[4,256,384]{2,1,0:T(8,128)(2,1)S(1)} %all-to-all-done.3.refs_6_.refs_1_), channel_id=1, source_target_pairs={{0,4},{4,0},{1,5},{5,1},{2,6},{6,2},{3,7},{7,3},{8,12},{12,8},{9,1... | collective-permute-start | bytes 2359304 | tf_op jit(solution)/shard_map/ppermute | solution.py:1269
  (100 other events, 608.5 us)
Sparse Core Ops, SparseCore 0:
  47.7 51.8 all-gather.2
  204.7 48.7 reduce-scatter.1

commit v6 on v5

--- a/solution.py
+++ b/solution.py
@@ -313,10 +313,10 @@
 
 def mix_local_kernel(own, head, counts, stacked, slots_ref, normed_ref, mask_ref, *rest):
     piece_refs, rest = rest[: len(counts)], rest[len(counts) :]
-    weights, inputs_out, gated_out, kept_out, scan_out, edge_out, gates_out, vec_out = rest[
-        stacked : stacked + 8
-    ]
-    (table,) = rest[stacked + 8 :]
+    weights, inputs_out, gated_out, kept_out, scan_out, edge_out, gates_out, vec_out, sums_out = (
+        rest[stacked : stacked + 9]
+    )
+    (table,) = rest[stacked + 9 :]
     model = normed_ref.shape[1]
     if own:
         weights[0] = piece_refs[0][...]
@@ -368,7 +368,7 @@
     scan_out[0, 1] = state
     edge_out[0, 0:1] = product[count - 1 :]
     edge_out[0, 1:2] = state[count - 1 :]
-    edge_out[0, 2:3] = jnp.sum(decay, axis=0, keepdims=True)
+    sums_out[0] = jnp.sum(decay, axis=0, keepdims=True)
 
 
 def mix_local(shard, shards, head, slots, normed, mask, pieces, stacks, after=(), carry=()):
@@ -383,9 +383,10 @@
         ((shards, count, width), BF16),
         ((shards, 3, count, width), F32),
         ((shards, 2, count, width), F32),
-        ((shards, 8, width), F32),
+        ((shards, 2, width), F32),
         ((shards, 2 * head, width), BF16),
         ((shards, 8, width), F32),
+        ((shards, 1, width), F32),
     ]
 
     def at(shape):
@@ -413,7 +414,7 @@
         aliases=aliases,
         name="mix_local",
     )
-    return outs[:8], outs[8:]
+    return outs[:9], outs[9:]
 
 
 def carried(edges):
@@ -456,7 +457,7 @@
     model = tokens.shape[1]
 
     def edge_spec(shift):
-        return pl.BlockSpec((1, 8, width), lambda s: ((s + shards - shift % shards) % shards, 0, 0))
+        return pl.BlockSpec((1, 2, width), lambda s: ((s + shards - shift % shards) % shards, 0, 0))
 
     return launch(
         functools.partial(branch_kernel, len(edges)),
@@ -795,7 +796,7 @@
     product, value = scan_up(shifted, into * act)
     adjoint_out[0, 0] = product
     adjoint_out[0, 1] = value
-    edge_out[0] = jnp.broadcast_to(decay[0:1] * value[0:1], edge_out.shape[1:])
+    edge_out[0] = decay[0:1] * value[0:1]
 
 
 def adjoint(grad, weights, gated, scan, kept, carry, mask, vec, through):
@@ -827,9 +828,9 @@
         out_shape=[
             jax.ShapeDtypeStruct((shards, count, width), BF16),
             jax.ShapeDtypeStruct((shards, 2, count, width), F32),
-            jax.ShapeDtypeStruct((shards, 8, width), F32),
+            jax.ShapeDtypeStruct((shards, 1, width), F32),
         ],
-        out_specs=[at(count, width), at(2, count, width), at(8, width)],
+        out_specs=[at(count, width), at(2, count, width), at(1, width)],
         name="mix_adjoint",
     )
 
@@ -937,7 +938,7 @@
     decay = jnp.exp(-rate)
     square = one_minus_exp(2.0 * rate)
     inverse = lax.rsqrt(square)
-    sized = adj * (square * inverse)
+    sized = adj * jnp.sqrt(square)
     pulled = adj * admit
     log_grad = decay * (adj * before * mask_ref[:, 1:2] - pulled * conv * decay * inverse)
     recall_grad = -speed * log_grad * recall * (1.0 - recall)
@@ -969,7 +970,7 @@
         jnp.sum(recall_grad, axis=0, keepdims=True),
         jnp.sum(admit_grad, axis=0, keepdims=True),
         jnp.sum(recall * log_grad, axis=0, keepdims=True),
-        edge_ref[0, 2:3],
+        edge_ref[0],
     ]
     rows.append(jnp.zeros((TABLE - 2 * head - len(rows), width), F32))
     small_out[0, 2 * head :] = jnp.concatenate(rows, axis=0).astype(BF16)
@@ -1005,8 +1006,8 @@
     def at(*shape):
         return pl.BlockSpec((1,) + shape, lambda s: (s,) + (0,) * len(shape))
 
-    def ahead_spec(shift):
-        return pl.BlockSpec((1, 8, width), lambda s: ((s + shift) % shards, 0, 0))
+    def ahead_spec(shift, rows=2):
+        return pl.BlockSpec((1, rows, width), lambda s: ((s + shift) % shards, 0, 0))
 
     return launch(
         functools.partial(mix_back_kernel, head, depth),
@@ -1026,9 +1027,9 @@
             flat(*mask.shape),
             at(2 * head, width),
             at(8, width),
-            at(8, width),
+            at(1, width),
         ]
-        + [ahead_spec(i + 1) for i in range(depth)]
+        + [ahead_spec(i + 1, 1) for i in range(depth)]
         + [ahead_spec(i + 1) for i in range(depth - 1)],
         0.1,
         after,
@@ -1136,6 +1137,7 @@
 
 def assemble_kernel(
     rows_total,
+    rows,
     core_ref,
     own_ref,
     other_ref,
@@ -1154,7 +1156,7 @@
     *rest,
 ):
     *grads_out, small = rest
-    quads, rows, width = other_ref.shape
+    quads, _, width = other_ref.shape
     piece, hidden = grads_out[0].shape
     parts = hidden // (quads * width)
     for quad in range(quads):
@@ -1197,9 +1199,9 @@
     gain_two_out[...] = gains[1].reshape(model)
 
 
-def assemble(core, own, other, decay, model, heads, head, rows_total, piece):
+def assemble(core, own, other, size, decay, model, heads, head, rows_total, piece):
     width = own.shape[2]
-    hidden = own.shape[0] * (own.shape[1] - other.shape[1]) * width // (3 * piece)
+    hidden = own.shape[0] * (own.shape[1] - size) * width // (3 * piece)
     shapes = [
         (model, width),
         (heads, head, head),
@@ -1217,7 +1219,7 @@
         (piece, hidden),
     ]
     return launch(
-        functools.partial(assemble_kernel, rows_total),
+        functools.partial(assemble_kernel, rows_total, size),
         [core, own, other, decay],
         [smem(), vmem(), vmem(), vmem()],
         0.1,
@@ -1352,7 +1354,7 @@
         held = [arrived] + [hop(arrived, rel) for rel in range(1, quads)]
         if s < shards - 1:
             arrived = along(arrived, 1)
-    weights, inputs, gated, kept, scan, edge, gates, vec = stacks
+    weights, inputs, gated, kept, scan, edge, gates, vec, sums = stacks
     edge, gathered = fence([edge, gathered], cots[near:])
     other_gathered = swap(gathered)
     depth = LENGTH // count - 1
@@ -1423,7 +1425,7 @@
 
     arrived_one = spread(chip_one)
     input_back, small, normed_grad = mix_back(
-        weights, inputs, gate_back, kept, scan, adj, carry, mask, gates, vec, edge, edges_back, ahead,
+        weights, inputs, gate_back, kept, scan, adj, carry, mask, gates, vec, sums, edges_back, ahead,
         [chip_one],
     )
 
@@ -1477,7 +1479,8 @@
     ) = assemble(
         core_one,
         own_two,
-        swap(own_two[:, :size]),
+        swap(own_two),
+        size,
         decay_param,
         model,
         heads,

time: 327 us -> 328 us (level)
  the two profiles are of different devices: /device:TPU:17 before, /device:TPU:0 now
where the time goes in v6:
time: 328 us; the launch traced here: 322 us
  Pallas kernels  103 us (31%)
  waiting for transfers between devices  76.3 us (23%)
  starting transfers between devices  71.2 us (22%)
  local copies, waits for them, and re-layouts  28.4 us (9%)
  blocking collectives  18.1 us (6%)
  between operations  15.3 us (5%)
  other arithmetic  9.86 us (3%)
    pallas_call x34, Pallas kernels, launch(): pl.pallas_call(body, out_shape=list(out_shape) + [jax.ShapeDtypeStruct(c....  103 us
    ppermute x21, waiting for transfers between devices, hop(): return lax.ppermute(values, 'quad', [(i, i ^ rel) for i in range(quads)])  46.2 us
    ppermute x21, starting transfers between devices, hop(): return lax.ppermute(values, 'quad', [(i, i ^ rel) for i in range(quads)])  27.3 us
    ppermute x17, starting transfers between devices, along(): lax.ppermute(values, 'chan', [(i, (i + shift) % shards) for i in range(sh...  24.2 us
    unnamed x129, local copies, waits for them, and re-layouts  21.5 us
    all_to_all x1, blocking collectives, on_device(): own_two = lax.all_to_all(two, 'quad', 0, 0, tiled=True)  18.1 us
    ppermute x17, waiting for transfers between devices, along(): lax.ppermute(values, 'chan', [(i, (i + shift) % shards) for i in range(sh...  13.9 us
    all_to_all x2, waiting for transfers between devices, spread(): return lax.all_to_all(chip, 'quad', 0, 0, tiled=True)  9.36 us
  transfers between devices with their start and end apart: 57, of which 21 were waited for; matrix products, arithmetic and copies ran while one was open for 5% of the time, Pallas kernels for 31%

profile of v6, /device:TPU:0, one launch (start us, length us, event | category | flops | bytes accessed | tf_op | source)
XLA Modules:
  0.0 322.3 jit_solution(8608400111408279877)
XLA Ops:
  20.8 4.3 %all-to-all-start = ((bf16[4,3,32,768]{3,2,1,0:T(8,128)(2,1)}), bf16[4,3,32,768]{3,2,1,0:T(8,128)(2,1)}, u32[]{:S(2)}, u32[]{:S(2)}) async-start(bf16[4,3,32,768]{3,2,1,0:T(8,128)(2,1)} %fence.8), calls=%async_computation | async-start | bytes 1179648 | tf_op jit(solution)/shard_map/all_to_all | solution.py:1335
  37.0 6.3 %mix_local.4 = (bf16[4,3,1024,384]{3,2,1,0:T(8,128)(2,1)}, bf16[4,272,384]{2,1,0:T(8,128)(2,1)}, bf16[4,256,384]{2,1,0:T(8,128)(2,1)}, f32[4,3,256,384]{3,2,1,0:...) custom-call(s32[8]{0:T(128)} %pad_add_fusion.1.refs_0_, ...), custom_call_target="tpu_custom_call" | custom-call | flops 1880999936 | bytes 5985000 | tf_op jit(solution)/shard_map/mix_local/pallas_call | solution.py:155
  43.3 5.4 %collective-permute-done.6.refs_2_ = bf16[1,416,384]{2,1,0:T(8,128)(2,1)S(1)} collective-permute-done((bf16[1,416,384]{2,1,0:T(8,128)(2,1)}, bf16[1,416,384]{2,1,0:T(8,128)(2,1)S(1)}, u32[]{:S(2)}, u32[]{:S(2)}) %collective-permute-start.6) | collective-permute-done | bytes 319520 | tf_op jit(solution)/shard_map/ppermute | solution.py:1268
  55.2 6.0 %mix_local.5 = (bf16[4,3,1024,384]{3,2,1,0:T(8,128)(2,1)}, bf16[4,272,384]{2,1,0:T(8,128)(2,1)}, bf16[4,256,384]{2,1,0:T(8,128)(2,1)}, f32[4,3,256,384]{3,2,1,0:...) custom-call(s32[8]{0:T(128)} %pad_add_fusion.1.refs_0_, ...), custom_call_target="tpu_custom_call", output_to_operand_aliasing={{0}: (5, {}), {1}: (6, {}), {2}: (7, {}), {3}: (8, {}), {4}... | custom-call | flops 1880999936 | bytes 5985000 | tf_op jit(solution)/shard_map/mix_local/pallas_call | solution.py:155
  61.2 5.2 %collective-permute-done.10.refs_2_ = bf16[1,416,384]{2,1,0:T(8,128)(2,1)S(1)} collective-permute-done((bf16[1,416,384]{2,1,0:T(8,128)(2,1)S(1)}, bf16[1,416,384]{2,1,0:T(8,128)(2,1)S(1)}, u32[]{:S(2)}, u32[]{:S(2)}) %collective-permute-start.10) | collective-permute-done | bytes 319520 | tf_op jit(solution)/shard_map/ppermute | solution.py:1268
  73.3 5.8 %mix_local.6 = (bf16[4,3,1024,384]{3,2,1,0:T(8,128)(2,1)}, bf16[4,272,384]{2,1,0:T(8,128)(2,1)}, bf16[4,256,384]{2,1,0:T(8,128)(2,1)}, f32[4,3,256,384]{3,2,1,0:...) custom-call(s32[8]{0:T(128)} %pad_add_fusion.1.refs_0_, ...), custom_call_target="tpu_custom_call", output_to_operand_aliasing={{0}: (5, {}), {1}: (6, {}), {2}: (7, {}), {3}: (8, {}), {4}... | custom-call | flops 1880999936 | bytes 5985000 | tf_op jit(solution)/shard_map/mix_local/pallas_call | solution.py:155
  79.9 6.4 %collective-permute-done.16.refs_3_ = bf16[1,416,384]{2,1,0:T(8,128)(2,1)S(1)} collective-permute-done((bf16[1,416,384]{2,1,0:T(8,128)(2,1)S(1)}, bf16[1,416,384]{2,1,0:T(8,128)(2,1)S(1)}, u32[]{:S(2)}, u32[]{:S(2)}) %collective-permute-start.16) | collective-permute-done | bytes 319520 | tf_op jit(solution)/shard_map/ppermute | solution.py:1268
  91.2 5.9 %mix_local.7 = (bf16[4,3,1024,384]{3,2,1,0:T(8,128)(2,1)}, bf16[4,272,384]{2,1,0:T(8,128)(2,1)}, bf16[4,256,384]{2,1,0:T(8,128)(2,1)}, f32[4,3,256,384]{3,2,1,0:...) custom-call(s32[8]{0:T(128)} %pad_add_fusion.1.refs_0_, ...), custom_call_target="tpu_custom_call", output_to_operand_aliasing={{0}: (5, {}), {1}: (6, {}), {2}: (7, {}), {3}: (8, {}), {4}... | custom-call | flops 1880999936 | bytes 5985000 | tf_op jit(solution)/shard_map/mix_local/pallas_call | solution.py:155
  97.2 5.3 %collective-permute-done.19.refs_0_.refs_1_.refs_6_ = bf16[256,1024]{1,0:T(8,128)(2,1)S(1)} collective-permute-done((bf16[256,1024]{1,0:T(8,128)(2,1)S(1)}, bf16[256,1024]{1,0:T(8,128)(2,1)S(1)}, u32[]{:S(2)}, u32[]{:S(2)}) %collective-permute-start.19) | collective-permute-done | bytes 524320 | tf_op jit(solution)/shard_map/ppermute | solution.py:1268
  112.2 7.0 %mix_branch.1 = (f32[4,8,384]{2,1,0:T(8,128)}, bf16[4,256,384]{2,1,0:T(8,128)(2,1)}, f32[256,1024]{1,0:T(8,128)}, bf16[256,1024]{1,0:T(8,128)(2,1)}, bf16[256,1024]{1,0:T(8,128)(2,1)}) custom-call(f32[4,2,256,384]{3,2,1,0:T(8,128)} %get-tuple-element.170.refs_0_.refs_3_.refs_5_, bf16[4,256,384]{2,1,0:T(8,128)(2,1)} %get-tuple-element.171.refs_1_.refs_2_, ...), custom_call_target="tpu_custom_call" | custom-call | flops 33000000 | bytes 105000 | tf_op jit(solution)/shard_map/mix_branch/pallas_call | solution.py:155
  129.0 5.3 %collective-permute-done.24.refs_0_.refs_8_ = bf16[256,1024]{1,0:T(8,128)(2,1)S(1)} collective-permute-done((bf16[256,1024]{1,0:T(8,128)(2,1)}, bf16[256,1024]{1,0:T(8,128)(2,1)S(1)}, u32[]{:S(2)}, u32[]{:S(2)}) %collective-permute-start.24) | collective-permute-done | bytes 524320 | tf_op jit(solution)/shard_map/ppermute | solution.py:1268
  139.1 4.8 %collective-permute-done.26.refs_0_.refs_9_ = bf16[256,1024]{1,0:T(8,128)(2,1)S(1)} collective-permute-done((bf16[256,1024]{1,0:T(8,128)(2,1)}, bf16[256,1024]{1,0:T(8,128)(2,1)S(1)}, u32[]{:S(2)}, u32[]{:S(2)}) %collective-permute-start.26) | collective-permute-done | bytes 524320 | tf_op jit(solution)/shard_map/ppermute | solution.py:1268
  151.3 8.8 %mlp_grads.1 = (bf16[4,4,3,32,768]{4,3,2,1,0:T(8,128)(2,1)S(1)}, bf16[4,4,3,32,768]{4,3,2,1,0:T(8,128)(2,1)}, bf16[4,256,1024]{2,1,0:T(8,128)(2,1)S(1)}) custom-call(s32[1]{0:T(128)} %bitcast.13.refs_0_.refs_1_, s32[1]{0:T(128)} %bitcast.4.refs_0_.refs_1_.refs_7_, bf16[3,1024,768]{2,1,0:T(8,128)(2,1)S(1)} %mlp_arrange.1.refs_2_, ...), custom_call_target="tpu_custom_call" | custom-call | flops 4950000128 | bytes 15750000 | tf_op jit(solution)/shard_map/mlp_grads/pallas_call | solution.py:155
  160.1 7.3 %collective-permute-done.27.refs_2_ = bf16[256,1024]{1,0:T(8,128)(2,1)S(1)} collective-permute-done((bf16[256,1024]{1,0:T(8,128)(2,1)S(1)}, bf16[256,1024]{1,0:T(8,128)(2,1)S(1)}, u32[]{:S(2)}, u32[]{:S(2)}) %collective-permute-start.27) | collective-permute-done | bytes 524320 | tf_op jit(solution)/shard_map/ppermute | solution.py:1268
  171.5 4.5 %all-to-all-start.1 = ((bf16[4,256,1024]{2,1,0:T(8,128)(2,1)}), bf16[4,256,1024]{2,1,0:T(8,128)(2,1)}, u32[]{:S(2)}, u32[]{:S(2)}) async-start(bf16[4,256,1024]{2,1,0:T(8,128)(2,1)} %copy-done.9), calls=%async_computation.1 | async-start | bytes 4194304 | tf_op jit(solution)/shard_map/all_to_all | solution.py:1388
  176.0 8.8 %mix_adjoint.1 = (bf16[4,256,384]{2,1,0:T(8,128)(2,1)}, f32[4,2,256,384]{3,2,1,0:T(8,128)}, f32[4,1,384]{2,1,0:T(1,128)}, bf16[4,256,384]{2,1,0:T(8,128)(2,1)}) custom-call(bf16[256,1024]{1,0:T(8,128)(2,1)} %copy-done.26, bf16[4,3,1024,384]{3,2,1,0:T(8,128)(2,1)} %get-tuple-element.172.refs_2_.refs_1_.refs_0_, ...), custom_call_target="tpu_custom_call", output_to_operand_aliasing={{3}: (8, {})} | custom-call | flops 33000000 | bytes 105000 | tf_op jit(solution)/shard_map/mix_adjoint/pallas_call | solution.py:155
  191.2 6.6 %mix_outer.2.refs_5_ = bf16[4,4,256,384]{3,2,1,0:T(8,128)(2,1)} custom-call(s32[1]{0:T(128)} %bitcast.4.refs_0_.refs_1_.refs_7_, s32[1]{0:T(128)} %bitcast.13.refs_0_.refs_1_, bf16[272,512]{1,0:T(8,128)(2,1)} %copy-done.18, bf16[272,512]{1,0:T(8,128)(2,1)} %copy-done.50, bf16[4,256,384]{2,1,0:T(8,128)(2,1)} %get-tuple-element.210.refs_4_.refs_3_, ...), custom_call_target="tpu_custom_call" | custom-call | flops 33000000 | bytes 105000 | tf_op jit(solution)/shard_map/mix_outer/pallas_call | solution.py:155
  203.4 4.9 %all-to-all-start.2 = ((bf16[4,4,256,384]{3,2,1,0:T(8,128)(2,1)}), bf16[4,4,256,384]{3,2,1,0:T(8,128)(2,1)}, u32[]{:S(2)}, u32[]{:S(2)}) async-start(bf16[4,4,256,384]{3,2,1,0:T(8,128)(2,1)} %fence.10.refs_17_), calls=%async_computation.2 | async-start | bytes 6291456 | tf_op jit(solution)/shard_map/all_to_all | solution.py:1394
  208.3 13.7 %mix_back.1 = (bf16[4,272,384]{2,1,0:T(8,128)(2,1)}, bf16[4,256,384]{2,1,0:T(8,128)(2,1)}, f32[272,1024]{1,0:T(8,128)}) custom-call(bf16[4,3,1024,384]{3,2,1,0:T(8,128)(2,1)} %get-tuple-element.172.refs_2_.refs_1_.refs_0_, bf16[4,3,1024,384]{3,2,1,0:T(8,128)(2,1)} %get-tuple-element.172.refs_2_.refs_1_.refs_0_, ...), custom_call_target="tpu_custom_call" | custom-call | flops 33000000 | bytes 105000 | tf_op jit(solution)/shard_map/mix_back/pallas_call | solution.py:155
  227.6 5.4 %mix_outer.3 = (bf16[4,160,384]{2,1,0:T(8,128)(2,1)}, bf16[4,160,384]{2,1,0:T(8,128)(2,1)}, bf16[4,160,384]{2,1,0:T(8,128)(2,1)}, bf16[4,160,384]{2,1,0:T(8,128)(2,1)}) custom-call(s32[1]{0:T(128)} %bitcast.4.refs_0_.refs_1_.refs_7_, s32[1]{0:T(128)} %bitcast.13.refs_0_.refs_1_, bf16[272,512]{1,0:T(8,128)(2,1)} %copy-done.18, bf16[272,512]{1,0:T(8,128)(2,1)} %copy-done.50, ...), custom_call_target="tpu_custom_call" | custom-call | flops 33000000 | bytes 105000 | tf_op jit(solution)/shard_map/mix_outer/pallas_call | solution.py:155
  236.5 9.4 %all-to-all-done.2 = bf16[4,4,256,384]{3,2,1,0:T(8,128)(2,1)} async-done(((bf16[4,4,256,384]{3,2,1,0:T(8,128)(2,1)}), bf16[4,4,256,384]{3,2,1,0:T(8,128)(2,1)}, u32[]{:S(2)}, u32[]{:S(2)}) %all-to-all-start.2) | async-done | bytes 3145760 | tf_op jit(solution)/shard_map/all_to_all | solution.py:1394
  261.1 5.6 %collective-permute-done.42.refs_4_ = bf16[4,160,384]{2,1,0:T(8,128)(2,1)} collective-permute-done((bf16[4,160,384]{2,1,0:T(8,128)(2,1)}, bf16[4,160,384]{2,1,0:T(8,128)(2,1)}, u32[]{:S(2)}, u32[]{:S(2)}) %collective-permute-start.42) | collective-permute-done | bytes 491552 | tf_op jit(solution)/shard_map/ppermute | solution.py:1268
  281.4 7.3 %collective-permute-done.44.refs_3_ = bf16[176,384]{1,0:T(8,128)(2,1)S(1)} collective-permute-done((bf16[176,384]{1,0:T(8,128)(2,1)S(1)}, bf16[176,384]{1,0:T(8,128)(2,1)S(1)}, u32[]{:S(2)}, u32[]{:S(2)}) %collective-permute-start.44) | collective-permute-done | bytes 135200 | tf_op jit(solution)/shard_map/ppermute | solution.py:1274
  288.9 18.1 %all_to_all.25.refs_1_ = bf16[4,368,384]{2,1,0:T(8,128)(2,1)S(1)} all-to-all(bf16[4,368,384]{2,1,0:T(8,128)(2,1)S(1)} %home_sum.3), channel_id=1, replica_groups=mesh['quad'=4,'core'=2,'chan'=4] {'quad'}, dimensions={0} | all-to-all | bytes 2260992 | tf_op jit(solution)/shard_map/all_to_all | solution.py:1463
  (286 shorter events, 138.9 us)
Async XLA Ops:
  7.2 21.4 %collective-permute-start.2 = (bf16[256,1024]{1,0:T(8,128)(2,1)}, bf16[256,1024]{1,0:T(8,128)(2,1)S(1)}, u32[]{:S(2)}, u32[]{:S(2)}) collective-permute-start(bf16[256,1024]{1,0:T(8,128)(2,1)} %refs_5_.4), channel_id=1, source_target_pairs={{0,8},{8,0},{16,24},{24,16},{1,9},{9,1},{17,25},{25,17},{2,10},{10... | collective-permute-start | bytes 1572872 | tf_op jit(solution)/shard_map/ppermute | solution.py:1268
  10.2 18.4 %collective-permute-start.3 = (bf16[256,1024]{1,0:T(8,128)(2,1)}, bf16[256,1024]{1,0:T(8,128)(2,1)S(1)}, u32[]{:S(2)}, u32[]{:S(2)}) collective-permute-start(bf16[256,1024]{1,0:T(8,128)(2,1)} %refs_5_.4), channel_id=1, source_target_pairs={{0,16},{8,24},{16,0},{24,8},{1,17},{9,25},{17,1},{25,9},{2,18},{10... | collective-permute-start | bytes 1572872 | tf_op jit(solution)/shard_map/ppermute | solution.py:1268
  20.8 22.5 %all-to-all-start = ((bf16[4,3,32,768]{3,2,1,0:T(8,128)(2,1)}), bf16[4,3,32,768]{3,2,1,0:T(8,128)(2,1)}, u32[]{:S(2)}, u32[]{:S(2)}) async-start(bf16[4,3,32,768]{3,2,1,0:T(8,128)(2,1)} %fence.8), calls=%async_computation | async-start | bytes 1179648 | tf_op jit(solution)/shard_map/all_to_all | solution.py:1335
  25.1 77.6 %all-gather.3.cloned.1.call-start = ((), (), s32[]{:S(2)}) async-start(), calls=%async_computation.7 | async-start | bytes 2949120 | tf_op jit(solution)/shard_map/all_gather | solution.py:1350
  32.3 16.4 %collective-permute-start.6 = (bf16[1,416,384]{2,1,0:T(8,128)(2,1)}, bf16[1,416,384]{2,1,0:T(8,128)(2,1)S(1)}, u32[]{:S(2)}, u32[]{:S(2)}) collective-permute-start(bf16[1,416,384]{2,1,0:T(8,128)(2,1)} %fence.7.refs_0_), channel_id=1, source_target_pairs={{0,16},{8,24},{16,0},{24,8},{1,17},{9,25},{17,1},{25,9},{2,18},{10... | collective-permute-start | bytes 958472 | tf_op jit(solution)/shard_map/ppermute | solution.py:1268
  49.6 16.8 %collective-permute-start.10 = (bf16[1,416,384]{2,1,0:T(8,128)(2,1)S(1)}, bf16[1,416,384]{2,1,0:T(8,128)(2,1)S(1)}, u32[]{:S(2)}, u32[]{:S(2)}) collective-permute-start(bf16[1,416,384]{2,1,0:T(8,128)(2,1)S(1)} %get-tuple-element.139.refs_0_), channel_id=1, source_target_pairs={{0,16},{8,24},{16,0},{24,8},{1,17},{9,25},{17,1},{25,9},{2,18},{10... | collective-permute-start | bytes 958472 | tf_op jit(solution)/shard_map/ppermute | solution.py:1268
  70.7 15.6 %collective-permute-start.16 = (bf16[1,416,384]{2,1,0:T(8,128)(2,1)S(1)}, bf16[1,416,384]{2,1,0:T(8,128)(2,1)S(1)}, u32[]{:S(2)}, u32[]{:S(2)}) collective-permute-start(bf16[1,416,384]{2,1,0:T(8,128)(2,1)S(1)} %get-tuple-element.150.refs_0_), channel_id=1, source_target_pairs={{0,24},{8,16},{16,8},{24,0},{1,25},{9,17},{17,9},{25,1},{2,26},{10... | collective-permute-start | bytes 958472 | tf_op jit(solution)/shard_map/ppermute | solution.py:1268
  103.3 18.1 %collective-permute-start.23 = (bf16[4,4,3,32,768]{4,3,2,1,0:T(8,128)(2,1)}, bf16[4,4,3,32,768]{4,3,2,1,0:T(8,128)(2,1)}, u32[]{:S(2)}, u32[]{:S(2)}) collective-permute-start(bf16[4,4,3,32,768]{4,3,2,1,0:T(8,128)(2,1)} %get-tuple-element.179.refs_1_), channel_id=1, source_target_pairs={{0,4},{4,0},{1,5},{5,1},{2,6},{6,2},{3,7},{7,3},{8,12},{12,8},{9,1... | collective-permute-start | bytes 7077896 | tf_op jit(solution)/shard_map/ppermute | solution.py:1271
  121.0 22.9 %collective-permute-start.26 = (bf16[256,1024]{1,0:T(8,128)(2,1)}, bf16[256,1024]{1,0:T(8,128)(2,1)S(1)}, u32[]{:S(2)}, u32[]{:S(2)}) collective-permute-start(bf16[256,1024]{1,0:T(8,128)(2,1)} %get-tuple-element.178.refs_3_.refs_0_.refs_7_), channel_id=1, source_target_pairs={{0,16},{8,24},{16,0},{24,8},{1,17},{9,25},{17,1},{25,9},{2,18},{10... | collective-permute-start | bytes 1572872 | tf_op jit(solution)/shard_map/ppermute | solution.py:1268
  127.5 19.5 %collective-permute-start.28 = (bf16[256,1024]{1,0:T(8,128)(2,1)S(1)}, bf16[256,1024]{1,0:T(8,128)(2,1)S(1)}, u32[]{:S(2)}, u32[]{:S(2)}) collective-permute-start(bf16[256,1024]{1,0:T(8,128)(2,1)S(1)} %get-tuple-element.184), channel_id=1, source_target_pairs={{0,24},{8,16},{16,8},{24,0},{1,25},{9,17},{17,9},{25,1},{2,26},{10... | collective-permute-start | bytes 1572872 | tf_op jit(solution)/shard_map/ppermute | solution.py:1268
  137.3 30.1 %collective-permute-start.25 = (bf16[256,1024]{1,0:T(8,128)(2,1)S(1)}, bf16[256,1024]{1,0:T(8,128)(2,1)S(1)}, u32[]{:S(2)}, u32[]{:S(2)}) collective-permute-start(bf16[256,1024]{1,0:T(8,128)(2,1)S(1)} %get-tuple-element.182.refs_3_), channel_id=1, source_target_pairs={{0,8},{8,0},{16,24},{24,16},{1,9},{9,1},{17,25},{25,17},{2,10},{10... | collective-permute-start | bytes 1572872 | tf_op jit(solution)/shard_map/ppermute | solution.py:1268
  146.9 20.5 %collective-permute-start.27 = (bf16[256,1024]{1,0:T(8,128)(2,1)S(1)}, bf16[256,1024]{1,0:T(8,128)(2,1)S(1)}, u32[]{:S(2)}, u32[]{:S(2)}) collective-permute-start(bf16[256,1024]{1,0:T(8,128)(2,1)S(1)} %get-tuple-element.183.refs_3_), channel_id=1, source_target_pairs={{0,16},{8,24},{16,0},{24,8},{1,17},{9,25},{17,1},{25,9},{2,18},{10... | collective-permute-start | bytes 1572872 | tf_op jit(solution)/shard_map/ppermute | solution.py:1268
  150.0 17.4 %collective-permute-start.29 = (bf16[256,1024]{1,0:T(8,128)(2,1)S(1)}, bf16[256,1024]{1,0:T(8,128)(2,1)S(1)}, u32[]{:S(2)}, u32[]{:S(2)}) collective-permute-start(bf16[256,1024]{1,0:T(8,128)(2,1)S(1)} %get-tuple-element.185), channel_id=1, source_target_pairs={{0,24},{8,16},{16,8},{24,0},{1,25},{9,17},{17,9},{25,1},{2,26},{10... | collective-permute-start | bytes 1572872 | tf_op jit(solution)/shard_map/ppermute | solution.py:1268
  171.5 26.3 %collective-permute-start.33 = (bf16[4,4,3,32,768]{4,3,2,1,0:T(8,128)(2,1)}, bf16[4,4,3,32,768]{4,3,2,1,0:T(8,128)(2,1)}, u32[]{:S(2)}, u32[]{:S(2)}) collective-permute-start(bf16[4,4,3,32,768]{4,3,2,1,0:T(8,128)(2,1)} %get-tuple-element.208), channel_id=1, source_target_pairs={{0,4},{4,0},{1,5},{5,1},{2,6},{6,2},{3,7},{7,3},{8,12},{12,8},{9,1... | collective-permute-start | bytes 7077896 | tf_op jit(solution)/shard_map/ppermute | solution.py:1271
  171.5 31.9 %all-to-all-start.1 = ((bf16[4,256,1024]{2,1,0:T(8,128)(2,1)}), bf16[4,256,1024]{2,1,0:T(8,128)(2,1)}, u32[]{:S(2)}, u32[]{:S(2)}) async-start(bf16[4,256,1024]{2,1,0:T(8,128)(2,1)} %copy-done.9), calls=%async_computation.1 | async-start | bytes 4194304 | tf_op jit(solution)/shard_map/all_to_all | solution.py:1388
  176.0 102.0 %reduce-scatter.2.cloned.1.call-start = ((), (), s32[]{:S(2)}) async-start(), calls=%async_computation.6 | async-start | bytes 2949120 | tf_op jit(solution)/shard_map/reduce_scatter | solution.py:1421
  203.4 42.4 %all-to-all-start.2 = ((bf16[4,4,256,384]{3,2,1,0:T(8,128)(2,1)}), bf16[4,4,256,384]{3,2,1,0:T(8,128)(2,1)}, u32[]{:S(2)}, u32[]{:S(2)}) async-start(bf16[4,4,256,384]{3,2,1,0:T(8,128)(2,1)} %fence.10.refs_17_), calls=%async_computation.2 | async-start | bytes 6291456 | tf_op jit(solution)/shard_map/all_to_all | solution.py:1394
  223.5 28.3 %collective-permute-start.37 = (bf16[16,1024]{1,0:T(8,128)(2,1)S(1)}, bf16[16,1024]{1,0:T(8,128)(2,1)S(1)}, u32[]{:S(2)}, u32[]{:S(2)}) collective-permute-start(bf16[16,1024]{1,0:T(8,128)(2,1)S(1)} %slice.73), channel_id=1, source_target_pairs={{0,3},{1,0},{2,1},{3,2},{4,7},{5,4},{6,5},{7,6},{8,11},{9,8},{10,9... | collective-permute-start | bytes 98312 | tf_op jit(solution)/shard_map/ppermute | solution.py:1274
  233.0 27.2 %collective-permute-start.40 = (bf16[4,160,384]{2,1,0:T(8,128)(2,1)}, bf16[4,160,384]{2,1,0:T(8,128)(2,1)S(1)}, u32[]{:S(2)}, u32[]{:S(2)}) collective-permute-start(bf16[4,160,384]{2,1,0:T(8,128)(2,1)} %get-tuple-element.226), channel_id=1, source_target_pairs={{0,8},{8,0},{16,24},{24,16},{1,9},{9,1},{17,25},{25,17},{2,10},{10... | collective-permute-start | bytes 1474568 | tf_op jit(solution)/shard_map/ppermute | solution.py:1268
  235.0 26.1 %collective-permute-start.41 = (bf16[4,160,384]{2,1,0:T(8,128)(2,1)}, bf16[4,160,384]{2,1,0:T(8,128)(2,1)}, u32[]{:S(2)}, u32[]{:S(2)}) collective-permute-start(bf16[4,160,384]{2,1,0:T(8,128)(2,1)} %get-tuple-element.227), channel_id=1, source_target_pairs={{0,16},{8,24},{16,0},{24,8},{1,17},{9,25},{17,1},{25,9},{2,18},{10... | collective-permute-start | bytes 1474568 | tf_op jit(solution)/shard_map/ppermute | solution.py:1268
  236.4 30.3 %collective-permute-start.42 = (bf16[4,160,384]{2,1,0:T(8,128)(2,1)}, bf16[4,160,384]{2,1,0:T(8,128)(2,1)}, u32[]{:S(2)}, u32[]{:S(2)}) collective-permute-start(bf16[4,160,384]{2,1,0:T(8,128)(2,1)} %get-tuple-element.228), channel_id=1, source_target_pairs={{0,24},{8,16},{16,8},{24,0},{1,25},{9,17},{17,9},{25,1},{2,26},{10... | collective-permute-start | bytes 1474568 | tf_op jit(solution)/shard_map/ppermute | solution.py:1268
  249.5 20.7 %collective-permute-start.46 = (bf16[256,384]{1,0:T(8,128)(2,1)}, bf16[256,384]{1,0:T(8,128)(2,1)S(1)}, u32[]{:S(2)}, u32[]{:S(2)}) collective-permute-start(bf16[256,384]{1,0:T(8,128)(2,1)} %get-tuple-element.252), channel_id=1, source_target_pairs={{0,3},{1,0},{2,1},{3,2},{4,7},{5,4},{6,5},{7,6},{8,11},{9,8},{10,9... | collective-permute-start | bytes 589832 | tf_op jit(solution)/shard_map/ppermute | solution.py:1274
  251.7 18.5 %collective-permute-start.47 = (bf16[256,384]{1,0:T(8,128)(2,1)}, bf16[256,384]{1,0:T(8,128)(2,1)S(1)}, u32[]{:S(2)}, u32[]{:S(2)}) collective-permute-start(bf16[256,384]{1,0:T(8,128)(2,1)} %get-tuple-element.251), channel_id=1, source_target_pairs={{0,2},{1,3},{2,0},{3,1},{4,6},{5,7},{6,4},{7,5},{8,10},{9,11},{10,... | collective-permute-start | bytes 589832 | tf_op jit(solution)/shard_map/ppermute | solution.py:1274
  271.2 17.4 %all-to-all-start.3 = ((bf16[4,256,384]{2,1,0:T(8,128)(2,1)}), bf16[4,256,384]{2,1,0:T(8,128)(2,1)S(1)}, u32[]{:S(2)}, u32[]{:S(2)}) async-start(bf16[4,256,384]{2,1,0:T(8,128)(2,1)} %fence.13), calls=%async_computation.4 | async-start | bytes 1572864 | tf_op jit(solution)/shard_map/all_to_all | solution.py:1394
  (97 other events, 599.7 us)
Sparse Core Ops, SparseCore 0:
  49.7 52.9 all-gather.2
  203.5 48.9 reduce-scatter.1
